TPU v7x, 32 devices: a whole 2x2x4 slice. The times are simulated.
32 devices in a mesh: row: 8 (over y, x, core), col: 4 (over z).
Axes of the slice: x: 2, y: 2, z: 4, core: 2. Of those that a mesh axis runs over, the one named last changes fastest.
Arguments:
- amplitudes: bfloat16 [4096, 3072], P(('row', 'col')), may hold values from -6 to 6
- integrals: bfloat16 [8, 3072, 9600], P('col', None, 'row'), may hold values from -0.109375 to 0.109375
- irreps: int32 [4096], P(('row', 'col')), may hold values from 0 to 7, as said below
- row_mirror: int32 [4096], P(('row', 'col')), may hold values from 0 to 127, as said below
- col_mirror: int32 [9600], replicated, may hold values from 0 to 9599, as said below
Outputs:
- symmetrized: bfloat16 [4096, 9600], P(('row', 'col'))
Inputs may be any that keep to these rules, and one draw needn't show every extreme that they name: `irreps`: among the 128 pairs of one block, no irrep occurs more than 32 times; in every block one irrep, the same for all blocks, occurs exactly 32 times. A pair and its mirrored partner have the same irrep. `row_mirror`: within each block of 128 pairs the map is an involution without fixed points. `col_mirror`: an involution of the 9600 slab columns without fixed points.
All inputs are finite; a program needn't handle non-finite values.
Results may differ from a plain program's by a relative error of at most 0.0051.
Values may be sent and summed in bfloat16 or wider, within the bound.
No kernel may reach another device: no remote copies, remote signals or barrier semaphores. Data moves between devices by JAX's collectives and lax.ppermute only.
A program may use at most 192 MiB of HBM per device.

v0:
```python
import jax
import jax.numpy as jnp
from jax import lax
from jax.sharding import PartitionSpec as P

IRREPS = 8


def body(amplitudes, integrals, irreps, row_mirror, col_mirror):
    pair_count = amplitudes.shape[0]
    contract = amplitudes.shape[1]
    col_count = lax.axis_size("col")
    per_owner = integrals.shape[0]
    capacity = pair_count // 4
    onehot = (irreps[:, None] == jnp.arange(IRREPS, dtype=jnp.int32)[None, :]).astype(jnp.int32)
    before = jnp.cumsum(onehot, axis=0) - onehot
    slot_index = jnp.sum(before * onehot, axis=1)
    owner_col = irreps // per_owner
    within = irreps % per_owner
    position = within * (col_count * capacity) + owner_col * capacity + slot_index
    outgoing = (
        jnp.zeros((per_owner * col_count * capacity, contract), jnp.bfloat16)
        .at[position]
        .set(amplitudes)
    )
    outgoing = outgoing.reshape(per_owner, col_count, capacity, contract)
    arrived = lax.all_to_all(outgoing, "col", split_axis=1, concat_axis=1, tiled=True)
    arrived = arrived.reshape(per_owner, col_count * capacity, contract)
    shares = jnp.einsum(
        "irk,iks->irs",
        lax.all_gather(arrived, "row", axis=1, tiled=True),
        integrals,
        preferred_element_type=jnp.float32,
    ).astype(jnp.bfloat16)
    result = lax.all_to_all(shares, "row", split_axis=1, concat_axis=2, tiled=True)
    slab_width = result.shape[2]
    result = result.reshape(per_owner, col_count, capacity, slab_width)
    returned = lax.all_to_all(result, "col", split_axis=1, concat_axis=1, tiled=True)
    ladder = returned.reshape(per_owner * col_count * capacity, slab_width)[position]
    mirrored = ladder[row_mirror][:, col_mirror]
    return (ladder.astype(jnp.float32) + mirrored.astype(jnp.float32)).astype(jnp.bfloat16)


def solution(mesh):
    return jax.shard_map(
        body,
        mesh=mesh,
        in_specs=(
            P(("row", "col"), None),
            P("col", None, "row"),
            P(("row", "col")),
            P(("row", "col")),
            P(),
        ),
        out_specs=P(("row", "col"), None),
        check_vma=False,
    )
```

profile of v0, /device:TPU:0, one launch (start us, length us, event | category | flops | bytes accessed | tf_op | source)
XLA Modules:
  0.0 416.4 jit_solution(5335740450326958981)
XLA Ops:
  6.5 0.0 all-gather.2.cloned.1.call-start
  6.5 0.7 fusion.3
  7.3 0.2 reduce_window_sum.11
  7.5 0.8 select_reduce_fusion
  8.3 0.7 compare_select_fusion.2
  9.0 2.8 scatter_custom_fusion
  11.8 0.1 copy.11
  11.9 43.1 %all_to_all.25 = bf16[2,4,32,3072]{3,2,0,1:T(8,128)(2,1)S(1)} all-to-all(bf16[2,4,32,3072]{3,2,0,1:T(8,128)(2,1)S(1)} %copy.11), channel_id=1, replica_groups=mesh['row'=8,'col'=4] {'col'}, dimensions={1} | all-to-all | bytes 3145728 | tf_op jit(solution)/shard_map/all_to_all | solution.py:27
  55.0 1.3 copy.12
  56.3 0.0 all-gather.2.cloned.1.call-update
  56.3 71.4 %all-gather.2.cloned.1.call-done = bf16[2,1024,3072]{2,1,0:T(8,128)(2,1)} async-done(((bf16[2,128,3072]{2,1,0:T(8,128)(2,1)}), bf16[2,1024,3072]{2,1,0:T(8,128)(2,1)}) %all-gather.2.cloned.1.call-update) | async-done | bytes 12582928 | tf_op jit(solution)/shard_map/all_gather | solution.py:31
  127.7 22.0 %convolution_convert_fusion = bf16[2,1024,1200]{1,2,0:T(8,128)(2,1)} fusion(bf16[2,1024,3072]{2,1,0:T(8,128)(2,1)} %all-gather.2.cloned.1.call-done, bf16[2,3072,1200]{1,2,0:T(8,128)(2,1)} %param.6), kind=kOutput, calls=%fused_computation.4 | convolution fusion | flops 15101952000 | bytes 32243712 | tf_op jit(solution)/shard_map/irk,iks->irs/dot_general | solution.py:29
  149.7 13.7 %copy.13 = bf16[2,1024,1200]{2,0,1:T(2,128)(2,1)} copy(bf16[2,1024,1200]{1,2,0:T(8,128)(2,1)} %convolution_convert_fusion) | data formatting | bytes 9830400 | tf_op jit(solution)/shard_map/convert_element_type | solution.py:34
  163.5 64.0 %all_to_all.26 = bf16[2,1024,1200]{2,0,1:T(2,128)(2,1)S(1)} all-to-all(bf16[2,1024,1200]{2,0,1:T(2,128)(2,1)} %copy.13), channel_id=1, replica_groups=mesh['row'=8,'col'=4] {'row'}, dimensions={1} | all-to-all | bytes 9830400 | tf_op jit(solution)/shard_map/all_to_all | solution.py:35
  227.4 5.2 %copy.20 = bf16[2,8,128,1200]{3,1,2,0:T(8,128)(2,1)} copy(bf16[2,8,128,1200]{3,0,2,1:T(2,128)(2,1)S(1)} %bitcast.16) | data formatting | bytes 9830400 | tf_op jit(solution)/shard_map/all_to_all | solution.py:35
  232.6 9.3 %reshape.16 = bf16[2,4,32,9600]{3,2,1,0:T(8,128)(2,1)} reshape(bf16[2,128,8,1200]{3,2,1,0:T(8,128)(2,1)} %bitcast.17) | data formatting | bytes 9830400 | tf_op jit(solution)/shard_map/reshape | solution.py:37
  242.0 5.1 %copy.15 = bf16[2,4,32,9600]{3,2,0,1:T(8,128)(2,1)} copy(bf16[2,4,32,9600]{3,2,1,0:T(8,128)(2,1)} %reshape.16) | data formatting | bytes 9830400 | tf_op jit(solution)/shard_map/reshape | solution.py:37
  247.1 0.0 copy-start.1
  247.1 0.0 copy-start
  247.1 5.1 %all-to-all-start.2 = ((bf16[2,4,32,9600]{3,2,0,1:T(8,128)(2,1)}), bf16[2,4,32,9600]{3,2,0,1:T(8,128)(2,1)}, u32[]{:S(2)}, u32[]{:S(2)}) async-start(bf16[2,4,32,9600]{3,2,0,1:T(8,128)(2,1)} %copy.15), calls=%async_computation.2 | async-start | bytes 9830400 | tf_op jit(solution)/shard_map/all_to_all | solution.py:38
  252.2 0.0 copy-done.1
  252.2 0.0 copy-done
  252.3 108.2 %all-to-all-done.2 = bf16[2,4,32,9600]{3,2,0,1:T(8,128)(2,1)} async-done(((bf16[2,4,32,9600]{3,2,0,1:T(8,128)(2,1)}), bf16[2,4,32,9600]{3,2,0,1:T(8,128)(2,1)}, u32[]{:S(2)}, u32[]{:S(2)}) %all-to-all-start.2) | async-done | bytes 4915232 | tf_op jit(solution)/shard_map/all_to_all | solution.py:38
  360.5 5.0 %copy.16 = bf16[2,4,32,9600]{3,2,1,0:T(8,128)(2,1)} copy(bf16[2,4,32,9600]{3,2,0,1:T(8,128)(2,1)} %all-to-all-done.2) | data formatting | bytes 9830400 | tf_op jit(solution)/shard_map/all_to_all | solution.py:38
  365.4 7.5 %gather_fusion = bf16[128,9600]{1,0:T(8,128)(2,1)S(1)} fusion(bf16[256,9600]{1,0:T(8,128)(2,1)} %bitcast.15, s32[1024]{0:T(1024)S(1)} %pad_clamp_fusion.2), kind=kCustom, calls=%fused_computation | custom fusion | bytes 4915712 | tf_op jit(solution)/shard_map/gather | solution.py:39
  372.9 3.5 gather_fusion.1
  376.5 4.3 %copy.17 = bf16[128,9600]{0,1:T(8,128)(2,1)} copy(bf16[128,9600]{1,0:T(8,128)(2,1)} %gather_fusion.1) | data formatting | bytes 4915200 | tf_op jit(solution)/shard_map/gather | solution.py:40
  380.8 20.7 %gather_fusion.2 = bf16[9600,128]{1,0:T(8,128)(2,1)} fusion(bf16[128,9600]{0,1:T(8,128)(2,1)} %copy.17, s32[10240]{0:T(1024)S(1)} %pad_clamp_fusion), kind=kCustom, calls=%fused_computation.2 | custom fusion | bytes 4953600 | tf_op jit(solution)/shard_map/gather | solution.py:40
  401.5 4.4 %copy.18 = bf16[9600,128]{0,1:T(8,128)(2,1)} copy(bf16[9600,128]{1,0:T(8,128)(2,1)} %gather_fusion.2) | data formatting | bytes 4915200 | tf_op jit(solution)/shard_map/gather | solution.py:40
  405.8 3.7 fusion
  (5 shorter events, 0.0 us)
Async XLA Ops:
  6.5 121.2 %all-gather.2.cloned.1.call-start = ((), (), s32[]{:S(2)}) async-start(), calls=%async_computation.3 | async-start | bytes 14155776 | tf_op jit(solution)/shard_map/all_gather | solution.py:31
  247.1 5.1 %copy-start.1 = (s32[128]{0:T(128)S(1)}, s32[128]{0:T(128)}, u32[]{:S(2)}) copy-start(s32[128]{0:T(128)} %param.8) | copy-start | bytes 1540
  247.1 5.2 %copy-start = (s32[9600]{0:T(1024)S(1)}, s32[9600]{0:T(1024)}, u32[]{:S(2)}) copy-start(s32[9600]{0:T(1024)} %param.9) | copy-start | bytes 115204
  247.1 113.4 %all-to-all-start.2 = ((bf16[2,4,32,9600]{3,2,0,1:T(8,128)(2,1)}), bf16[2,4,32,9600]{3,2,0,1:T(8,128)(2,1)}, u32[]{:S(2)}, u32[]{:S(2)}) async-start(bf16[2,4,32,9600]{3,2,0,1:T(8,128)(2,1)} %copy.15), calls=%async_computation.2 | async-start | bytes 9830400 | tf_op jit(solution)/shard_map/all_to_all | solution.py:38
Sparse Core Ops, SparseCore 0:
  56.4 71.2 all-gather.1
where the time goes:
time: 418 us; the launch traced here: 416 us
  waiting for transfers between devices  180 us (43%)
  blocking collectives  107 us (26%)
  local copies, waits for them, and re-layouts  82.9 us (20%)
  matrix products  22 us (5%)
  between operations  13.5 us (3%)
  other arithmetic  6.13 us (1%)
  starting transfers between devices  5.11 us (1%)
    all_to_all x1, waiting for transfers between devices, body(): lax.all_to_all(result, 'col', split_axis=1, concat_axis=1, tiled=True)  108 us
    all_gather x1, waiting for transfers between devices, body(): lax.all_gather(arrived, 'row', axis=1, tiled=True)  71.4 us
    all_to_all x1, blocking collectives, body(): lax.all_to_all(shares, 'row', split_axis=1, concat_axis=2, tiled=True)  64 us
    all_to_all x1, blocking collectives, body(): lax.all_to_all(outgoing, 'col', split_axis=1, concat_axis=1, tiled=True)  43.1 us
    gather x4, local copies, waits for them, and re-layouts, body(): mirrored = ladder[row_mirror][:, col_mirror]  32.9 us
    dot_general x1, matrix products, body(): jnp.einsum('irk,iks->irs', lax.all_gather(arrived, 'row', axis=1, tiled=T...  22 us
    reshape x2, local copies, waits for them, and re-layouts, body(): result = result.reshape(per_owner, col_count, capacity, slab_width)  14.4 us
    convert_element_type x1, local copies, waits for them, and re-layouts, body(): shares = jnp.einsum('irk,iks->irs', lax.all_gather(arrived, 'row', axis=1...  13.7 us
  transfers between devices with their start and end apart: 2, of which 2 were waited for; matrix products, arithmetic and copies ran while one was open for 0% of the time, Pallas kernels for 0%

commit v1 on v0

v1 whole, which is shorter than its diff:
```python
import functools

import jax
import jax.numpy as jnp
from jax import lax
from jax.experimental import pallas as pl
from jax.experimental.pallas import tpu as pltpu
from jax.sharding import PartitionSpec as P

IRREPS = 8
F32, BF16, I32 = jnp.float32, jnp.bfloat16, jnp.int32
NN = (((1,), (0,)), ((), ()))
NT = (((1,), (1,)), ((), ()))
VMEM_LIMIT = 56 * 1024 * 1024


def iota(shape, dim):
    return lax.broadcasted_iota(I32, shape, dim)


def params():
    return pltpu.CompilerParams(vmem_limit_bytes=VMEM_LIMIT)


def pack_kernel(cols, owned, half, where_ref, irreps_ref, mirror_ref, amp_ref, slot_ref, *out_refs):
    pairs = irreps_ref.shape[1]
    square = (pairs, pairs)
    irreps = jnp.broadcast_to(irreps_ref[...], square)
    mirror = jnp.broadcast_to(mirror_ref[...], square)
    irreps_t = irreps.astype(F32).T.astype(I32)
    mirror_t = mirror.astype(F32).T.astype(I32)
    down, across = iota(square, 0), iota(square, 1)
    first = jnp.minimum(across, mirror)
    counted = (mirror_t > down) & (irreps_t == irreps) & (down < first)
    rank = jnp.sum(counted.astype(I32), axis=0, keepdims=True)
    partner = (across[:1] != first[:1]).astype(I32)
    slot = irreps_ref[...] * (2 * half) + partner * half + rank
    slot_ref[...] = slot
    rows = owned * 2 * half
    amp = amp_ref[...]
    for k in range(cols):
        base = (where_ref[1] ^ k) * rows
        onehot = (slot == base + iota((rows, pairs), 0)).astype(F32).astype(BF16)
        out_refs[k][...] = lax.dot_general(onehot, amp, NN, preferred_element_type=F32).astype(BF16)


def pack(where, irreps, mirror, amplitudes, cols, owned, half):
    pairs, contract = amplitudes.shape
    rows = owned * 2 * half
    whole = lambda shape: pl.BlockSpec(shape, lambda i, w: (0, 0))
    out = pl.pallas_call(
        functools.partial(pack_kernel, cols, owned, half),
        grid_spec=pltpu.PrefetchScalarGridSpec(
            num_scalar_prefetch=1,
            grid=(1,),
            in_specs=[whole((1, pairs)), whole((1, pairs)), whole((pairs, contract))],
            out_specs=[whole((1, pairs))] + [whole((rows, contract))] * cols,
        ),
        out_shape=[jax.ShapeDtypeStruct((1, pairs), I32)]
        + [jax.ShapeDtypeStruct((rows, contract), BF16)] * cols,
        compiler_params=params(),
        cost_estimate=pl.CostEstimate(
            flops=2 * cols * rows * pairs * contract, bytes_accessed=3 * pairs * contract * 2, transcendentals=0
        ),
        name="pack",
    )(where, irreps, mirror, amplitudes)
    return out[0], out[1:]


def product_kernel(holders, chunk_count, owned, slots, *refs):
    pieces = refs[: holders * chunk_count]
    integrals_ref = refs[holders * chunk_count]
    outs = refs[holders * chunk_count + 1 : holders * chunk_count + 1 + holders]
    rows_ref, sem = refs[-2:]
    group = chunk_count * slots

    @pl.when(pl.program_id(0) == 0)
    def _():
        copies = []
        for o in range(holders):
            for j in range(chunk_count):
                for i in range(owned):
                    n = len(copies)
                    copies.append(
                        pltpu.make_async_copy(
                            pieces[o * chunk_count + j].at[pl.ds(i * slots, slots)],
                            rows_ref.at[i, pl.ds(o * group + j * slots, slots)],
                            sem.at[n],
                        )
                    )
        for copy in copies:
            copy.start()
        for copy in copies:
            copy.wait()

    ladder = [
        lax.dot_general(rows_ref[i], integrals_ref[i], NN, preferred_element_type=F32) for i in range(owned)
    ]
    for o in range(holders):
        block = jnp.concatenate([ladder[i][o * group : (o + 1) * group] for i in range(owned)], axis=0)
        outs[o][...] = block.T.astype(BF16)


def product(pieces, integrals, holders, chunk_count, slots):
    owned, contract, share = integrals.shape
    tile = 256
    group = chunk_count * slots
    lanes = owned * group
    return pl.pallas_call(
        functools.partial(product_kernel, holders, chunk_count, owned, slots),
        grid=(pl.cdiv(share, tile),),
        in_specs=[pl.BlockSpec(memory_space=pl.ANY)] * (holders * chunk_count)
        + [pl.BlockSpec((owned, contract, tile), lambda s: (0, 0, s))],
        out_specs=[pl.BlockSpec((tile, lanes), lambda s: (s, 0))] * holders,
        out_shape=[jax.ShapeDtypeStruct((share, lanes), BF16)] * holders,
        scratch_shapes=[
            pltpu.VMEM((owned, holders * group, contract), BF16),
            pltpu.SemaphoreType.DMA((holders * chunk_count * owned,)),
        ],
        compiler_params=params(),
        cost_estimate=pl.CostEstimate(
            flops=2 * owned * holders * group * contract * share,
            bytes_accessed=2 * owned * contract * (share + holders * group),
            transcendentals=0,
        ),
        name="ladder",
    )(*pieces, integrals)


def gather_rows(mirror_ref, base, source, target, count):
    step = 16

    def some(n, carry):
        for u in range(step):
            at = n * step + u
            target[pl.ds(at, 1), :] = source[pl.ds(mirror_ref[base + at], 1), :]
        return carry

    lax.fori_loop(0, count // step, some, 0)


def symmetrize_kernel(holders, chunks, owned, half, where_ref, mirror_ref, *refs):
    parts = refs[:holders]
    outs = refs[holders : holders + len(chunks)]
    raw, wide, picked, sem = refs[holders + len(chunks) :]
    share = parts[0].shape[0]
    lanes = raw.shape[2]
    block = picked.shape[0]
    step = pl.program_id(0)

    @pl.when(step == 0)
    def _():
        copies = []
        for o in range(holders):
            copies.append(pltpu.make_async_copy(parts[o], raw.at[o], sem.at[o]))
        for copy in copies:
            copy.start()
        for o in range(holders):
            copies[o].wait()
            at = pl.multiple_of((where_ref[0] ^ o) * share, 8)
            wide[pl.ds(at, share), :] = raw[o].astype(F32)

    base = step * block
    gather_rows(mirror_ref, base, wide, picked, block)
    here = wide[pl.ds(pl.multiple_of(base, 128), block), :].astype(BF16)
    there = picked[...].astype(BF16)
    group = len(chunks) * 2 * half
    for j, k in enumerate(chunks):
        both = 2 if k == 0 else 1
        rows = outs[j].shape[0]
        row, lane = iota((rows, lanes), 0), iota((rows, lanes), 1)
        irrep, rest = row // (both * half), row % (both * half)
        side, rank = rest // half, rest % half
        start = irrep * group + j * 2 * half + rank
        mine = (lane == start + side * half).astype(F32).astype(BF16)
        other = (lane == start + (1 - side) * half).astype(F32).astype(BF16)
        outs[j][...] = (
            lax.dot_general(mine, here, NT, preferred_element_type=F32)
            + lax.dot_general(other, there, NT, preferred_element_type=F32)
        ).astype(BF16)


def block_of(slab):
    for tiles in (15, 10, 5, 3, 2, 1):
        block = tiles * 128
        if slab % block == 0:
            return block


def symmetrize(where, col_mirror, parts, chunks, owned, half):
    holders = len(parts)
    share, lanes = parts[0].shape
    slab = col_mirror.shape[0]
    block = block_of(slab)
    rows = [owned * half * (2 if k == 0 else 1) for k in chunks]
    return pl.pallas_call(
        functools.partial(symmetrize_kernel, holders, chunks, owned, half),
        grid_spec=pltpu.PrefetchScalarGridSpec(
            num_scalar_prefetch=2,
            grid=(slab // block,),
            in_specs=[pl.BlockSpec(memory_space=pl.ANY)] * holders,
            out_specs=[pl.BlockSpec((n, block), lambda s, w, m: (0, s)) for n in rows],
            scratch_shapes=[
                pltpu.VMEM((holders, share, lanes), BF16),
                pltpu.VMEM((slab, lanes), F32),
                pltpu.VMEM((block, lanes), F32),
                pltpu.SemaphoreType.DMA((holders,)),
            ],
        ),
        out_shape=[jax.ShapeDtypeStruct((n, slab), BF16) for n in rows],
        compiler_params=params(),
        cost_estimate=pl.CostEstimate(
            flops=4 * sum(rows) * lanes * slab + 40000 * slab, bytes_accessed=16 * slab * lanes, transcendentals=0
        ),
        name="symmetrize",
    )(where, col_mirror, *parts)


def finish_kernel(cols, owned, half, where_ref, mirror_ref, slot_ref, *refs):
    own_ref = refs[0]
    sums = refs[1:cols]
    out_ref, wide, picked = refs[cols:]
    step = pl.program_id(0)
    slab, lanes = wide.shape
    block = picked.shape[0]
    pairs = out_ref.shape[0]
    sent = owned * half
    used = (cols - 1) * sent

    @pl.when(step == 0)
    def _():
        def widen(n, carry):
            at = pl.ds(pl.multiple_of(n * block, 128), block)
            rows = [s[:, at].astype(F32) for s in sums]
            if lanes > used:
                rows.append(jnp.zeros((lanes - used, block), F32))
            wide[at, :] = jnp.concatenate(rows, axis=0).T
            return carry

        lax.fori_loop(0, slab // block, widen, 0)

    base = step * block
    gather_rows(mirror_ref, base, wide, picked, block)
    there = picked[...].astype(BF16)
    here = pl.ds(pl.multiple_of(base, 128), block)
    slot = jnp.broadcast_to(slot_ref[...], (pairs, pairs)).astype(F32).T.astype(I32)
    col = where_ref[1]
    own = own_ref.shape[0]
    slot_own = slot[:, :1]
    onehot = (slot_own == col * own + iota((pairs, own), 1)).astype(F32).astype(BF16)
    total = lax.dot_general(onehot, own_ref[...], NN, preferred_element_type=F32)
    for k in range(1, cols):
        at = iota((pairs, sent), 1)
        at = (col ^ k) * own + (at // half) * (2 * half) + at % half
        onehot = (slot_own == at).astype(F32).astype(BF16)
        total += lax.dot_general(onehot, sums[k - 1][:, here], NN, preferred_element_type=F32)
    at = iota((pairs, lanes), 1)
    rest = at % sent
    at = jnp.where(
        at < used, (col ^ (at // sent + 1)) * own + (rest // half) * (2 * half) + half + rest % half, -1
    )
    onehot = (slot_own == at).astype(F32).astype(BF16)
    total += lax.dot_general(onehot, there, NT, preferred_element_type=F32)
    out_ref[...] = total.astype(BF16)


def finish(where, col_mirror, slot, own, sums, owned, half):
    cols = len(sums) + 1
    slab = col_mirror.shape[0]
    pairs = slot.shape[1]
    block = block_of(slab)
    lanes = pl.cdiv(len(sums) * owned * half, 128) * 128
    return pl.pallas_call(
        functools.partial(finish_kernel, cols, owned, half),
        grid_spec=pltpu.PrefetchScalarGridSpec(
            num_scalar_prefetch=2,
            grid=(slab // block,),
            in_specs=[
                pl.BlockSpec((1, pairs), lambda s, w, m: (0, 0)),
                pl.BlockSpec((own.shape[0], block), lambda s, w, m: (0, s)),
            ]
            + [pl.BlockSpec((owned * half, slab), lambda s, w, m: (0, 0))] * len(sums),
            out_specs=pl.BlockSpec((pairs, block), lambda s, w, m: (0, s)),
            scratch_shapes=[pltpu.VMEM((slab, lanes), F32), pltpu.VMEM((block, lanes), F32)],
        ),
        out_shape=jax.ShapeDtypeStruct((pairs, slab), BF16),
        compiler_params=params(),
        cost_estimate=pl.CostEstimate(
            flops=2 * pairs * 256 * slab + 40000 * slab, bytes_accessed=8 * slab * lanes, transcendentals=0
        ),
        name="finish",
    )(where, col_mirror, slot, own, *sums)


def swap(array, axis, offset):
    return lax.ppermute(array, axis, [(i, i ^ offset) for i in range(lax.axis_size(axis))])


def gather_row_axis(chunk, order):
    held = {0: chunk}
    for bit in order:
        held.update({offset ^ bit: swap(array, "row", bit) for offset, array in list(held.items())})
    return held


def body(amplitudes, integrals, irreps, row_mirror, col_mirror):
    rows, cols = lax.axis_size("row"), lax.axis_size("col")
    owned = integrals.shape[0]
    pairs = amplitudes.shape[0]
    slots = pairs // 4
    half = slots // 2
    where = jnp.stack([lax.axis_index("row"), lax.axis_index("col")]).astype(I32)
    slot, packed = pack(where, irreps[None], row_mirror[None], amplitudes, cols, owned, half)
    chunks = [packed[0]] + [swap(packed[k], "col", k) for k in range(1, cols)]
    bits = [1 << b for b in range(rows.bit_length() - 1)]
    outer, core = bits[1:], bits[:1]
    size = max(1, 4 // owned)
    sums = {}
    for first in range(0, cols, size):
        batch = tuple(range(first, min(first + size, cols)))
        held = []
        for j, k in enumerate(batch):
            turn = j % len(outer)
            held.append(gather_row_axis(chunks[k], outer[turn:] + outer[:turn] + core))
        pieces = [held[j][o] for o in range(rows) for j in range(len(batch))]
        parts = product(pieces, integrals, rows, len(batch), slots)
        parts = [parts[0]] + [swap(parts[o], "row", o) for o in range(1, rows)]
        for k, part in zip(batch, symmetrize(where, col_mirror, parts, batch, owned, half)):
            sums[k] = part if k == 0 else swap(part, "col", k)
    return finish(where, col_mirror, slot, sums[0], [sums[k] for k in range(1, cols)], owned, half)


def solution(mesh):
    return jax.shard_map(
        body,
        mesh=mesh,
        in_specs=(
            P(("row", "col"), None),
            P("col", None, "row"),
            P(("row", "col")),
            P(("row", "col")),
            P(),
        ),
        out_specs=P(("row", "col"), None),
        check_vma=False,
    )
```

time: 418 us -> 274 us (0.66)
  blocking collectives: 107 us -> 0 us
  Pallas kernels: 0 us -> 97.3 us
  waiting for transfers between devices: 180 us -> 107 us
  local copies, waits for them, and re-layouts: 82.9 us -> 22.7 us
  starting transfers between devices: 5.11 us -> 44.6 us
  matrix products: 22 us -> 0 us
  between operations: 13.5 us -> 0.38 us
  other arithmetic: 6.13 us -> 0.64 us
    all_to_all x1 -> x0, waiting for transfers between devices: 108 us -> none  [body(): lax.all_to_all(result, 'col', split_axis=1, concat_axis=1, tiled=True)]
    all_to_all x2 -> x0, blocking collectives: 107 us -> none  [the longest x1 64 us: body(): lax.all_to_all(shares, 'row', split_axis=1, concat_axis=2, tiled=True)]
    ppermute x0 -> x48, waiting for transfers between devices: none -> 107 us  [swap(): lax.ppermute(array, axis, [(i, i ^ offset) for i in range(lax.axis_size(a...]
    pallas_call x0 -> x6, Pallas kernels: none -> 97.3 us  [the longest x2 40.6 us: symmetrize(): pl.pallas_call(functools.partial(symmetrize_kernel, holders, chunks, owne...]
    all_gather x1 -> x0, waiting for transfers between devices: 71.4 us -> none  [body(): lax.all_gather(arrived, 'row', axis=1, tiled=True)]
    ppermute x0 -> x48, starting transfers between devices: none -> 44.6 us  [swap(): lax.ppermute(array, axis, [(i, i ^ offset) for i in range(lax.axis_size(a...]
    gather x5 -> x0, local copies, waits for them, and re-layouts: 40.4 us -> none  [the longest x4 32.9 us: body(): mirrored = ladder[row_mirror][:, col_mirror]]
    unnamed x4 -> x79, local copies, waits for them, and re-layouts: 0.01 us -> 22.7 us
  transfers between devices with their start and end apart: 2 -> 48, of which waited for: 2 -> 14; matrix products, arithmetic and copies ran while one was open for 0% -> 7% of each run, Pallas kernels for 0% -> 26%
where the time goes in v1:
time: 274 us; the launch traced here: 273 us
  waiting for transfers between devices  107 us (39%)
  Pallas kernels  97.3 us (36%)
  starting transfers between devices  44.6 us (16%)
  local copies, waits for them, and re-layouts  22.7 us (8%)
    ppermute x48, waiting for transfers between devices, swap(): lax.ppermute(array, axis, [(i, i ^ offset) for i in range(lax.axis_size(a...  107 us
    ppermute x48, starting transfers between devices, swap(): lax.ppermute(array, axis, [(i, i ^ offset) for i in range(lax.axis_size(a...  44.6 us
    pallas_call x2, Pallas kernels, symmetrize(): pl.pallas_call(functools.partial(symmetrize_kernel, holders, chunks, owne...  40.6 us
    pallas_call x2, Pallas kernels, product(): pl.pallas_call(functools.partial(product_kernel, holders, chunk_count, ow...  31.3 us
    unnamed x79, local copies, waits for them, and re-layouts  22.7 us
    pallas_call x1, Pallas kernels, finish(): pl.pallas_call(functools.partial(finish_kernel, cols, owned, half), grid_...  22.1 us
  transfers between devices with their start and end apart: 48, of which 14 were waited for; matrix products, arithmetic and copies ran while one was open for 7% of the time, Pallas kernels for 26%

profile of v1, /device:TPU:0, one launch (start us, length us, event | category | flops | bytes accessed | tf_op | source)
XLA Modules:
  0.0 272.5 jit_solution(15928229760125647960)
XLA Ops:
  0.0 0.6 pad_add_fusion.where_ref
  0.6 3.3 %pack.1 = (s32[1,128]{1,0:T(1,128)}, bf16[64,3072]{1,0:T(8,128)(2,1)}, bf16[64,3072]{1,0:T(8,128)(2,1)}, bf16[64,3072]{1,0:T(8,128)(2,1)}, bf16[64,3072]{1,0:T(8,128)(2,1)}) custom-call(s32[2]{0:T(128)} %pad_add_fusion.where_ref, s32[1,128]{1,0:T(1,128)} %bitcast.4, s32[1,128]{1,0:T(1,128)} %bitcast.5, bf16[128,3072]{1,0:T(8,128)(2,1)} %amp_ref.1), custom_call_target="tpu_custom_call" | custom-call | flops 201326592 | bytes 2359296 | tf_op jit(solution)/shard_map/pack/pallas_call | solution.py:51
  4.0 4.0 %collective-permute-start.23 = (bf16[64,3072]{1,0:T(8,128)(2,1)}, bf16[64,3072]{1,0:T(8,128)(2,1)S(1)}, u32[]{:S(2)}, u32[]{:S(2)}) collective-permute-start(bf16[64,3072]{1,0:T(8,128)(2,1)} %get-tuple-element.43), channel_id=1, source_target_pairs={{0,2},{1,3},{2,0},{3,1},{4,6},{5,7},{6,4},{7,5},{8,10},{9,11},{10,... | collective-permute-start | bytes 1179656 | tf_op jit(solution)/shard_map/ppermute | solution.py:296
  8.0 1.3 collective-permute-start.24
  9.4 0.2 collective-permute-start
  9.6 1.5 collective-permute-start.3
  11.1 1.5 collective-permute-start.7
  12.6 22.5 %collective-permute-done.23.refs_0_ = bf16[64,3072]{1,0:T(8,128)(2,1)S(1)} collective-permute-done((bf16[64,3072]{1,0:T(8,128)(2,1)}, bf16[64,3072]{1,0:T(8,128)(2,1)S(1)}, u32[]{:S(2)}, u32[]{:S(2)}) %collective-permute-start.23) | collective-permute-done | bytes 393248 | tf_op jit(solution)/shard_map/ppermute | solution.py:296
  35.1 1.9 collective-permute-start.27
  37.0 1.5 collective-permute-start.32
  38.5 0.5 collective-permute-start.28
  39.1 0.2 collective-permute-start.31
  39.2 7.8 %collective-permute-done.27.refs_4_ = bf16[64,3072]{1,0:T(8,128)(2,1)S(1)} collective-permute-done((bf16[64,3072]{1,0:T(8,128)(2,1)S(1)}, bf16[64,3072]{1,0:T(8,128)(2,1)S(1)}, u32[]{:S(2)}, u32[]{:S(2)}) %collective-permute-start.27) | collective-permute-done | bytes 393248 | tf_op jit(solution)/shard_map/ppermute | solution.py:296
  47.1 1.9 collective-permute-done.32.refs_9_
  49.0 1.5 collective-permute-start.8
  50.5 4.8 %collective-permute-done.28.refs_5_ = bf16[64,3072]{1,0:T(8,128)(2,1)} collective-permute-done((bf16[64,3072]{1,0:T(8,128)(2,1)S(1)}, bf16[64,3072]{1,0:T(8,128)(2,1)}, u32[]{:S(2)}, u32[]{:S(2)}) %collective-permute-start.28) | collective-permute-done | bytes 393248 | tf_op jit(solution)/shard_map/ppermute | solution.py:296
  55.2 1.8 collective-permute-start.11
  57.0 0.5 collective-permute-done.31.refs_8_
  57.5 1.1 collective-permute-start.4
  58.6 0.2 collective-permute-start.9
  58.8 7.1 %collective-permute-done.8.refs_9_ = bf16[64,3072]{1,0:T(8,128)(2,1)S(1)} collective-permute-done((bf16[64,3072]{1,0:T(8,128)(2,1)S(1)}, bf16[64,3072]{1,0:T(8,128)(2,1)S(1)}, u32[]{:S(2)}, u32[]{:S(2)}) %collective-permute-start.8) | collective-permute-done | bytes 393248 | tf_op jit(solution)/shard_map/ppermute | solution.py:296
  65.8 1.5 collective-permute-start.35
  67.3 6.9 %collective-permute-done.11.refs_12_ = bf16[64,3072]{1,0:T(8,128)(2,1)S(1)} collective-permute-done((bf16[64,3072]{1,0:T(8,128)(2,1)S(1)}, bf16[64,3072]{1,0:T(8,128)(2,1)S(1)}, u32[]{:S(2)}, u32[]{:S(2)}) %collective-permute-start.11) | collective-permute-done | bytes 393248 | tf_op jit(solution)/shard_map/ppermute | solution.py:296
  74.2 0.2 collective-permute-start.36
  74.4 0.5 collective-permute-start.34
  75.0 7.0 %collective-permute-done.35.refs_12_ = bf16[64,3072]{1,0:T(8,128)(2,1)} collective-permute-done((bf16[64,3072]{1,0:T(8,128)(2,1)S(1)}, bf16[64,3072]{1,0:T(8,128)(2,1)}, u32[]{:S(2)}, u32[]{:S(2)}) %collective-permute-start.35) | collective-permute-done | bytes 393248 | tf_op jit(solution)/shard_map/ppermute | solution.py:296
  82.0 1.9 collective-permute-done.36.refs_13_
  83.9 0.5 collective-permute-start.12
  84.6 0.7 copy-done.18
  85.3 0.7 copy-done.20
  86.0 18.9 %copy.6.refs_16_ = bf16[2,3072,1200]{2,1,0:T(8,128)(2,1)} copy(bf16[2,3072,1200]{1,2,0:T(8,128)(2,1)} %param.6) | data formatting | bytes 29491200 | tf_op args[1]
  104.9 0.6 collective-permute-start.2
  105.6 0.4 collective-permute-start.13
  106.1 0.4 collective-permute-start.14
  106.5 15.7 %ladder.3 = (bf16[1200,128]{1,0:T(8,128)(2,1)}, bf16[1200,128]{1,0:T(8,128)(2,1)}, bf16[1200,128]{1,0:T(8,128)(2,1)}, bf16[1200,128]{1,0:T(8,128)(2,1)}, bf16[12...) custom-call(bf16[64,3072]{1,0:T(8,128)(2,1)} %copy-done.7, ...), custom_call_target="tpu_custom_call" | custom-call | flops 7549747200 | bytes 21037056 | tf_op jit(solution)/shard_map/ladder/pallas_call | solution.py:109
  122.3 0.2 collective-permute-start.39
  122.4 1.5 collective-permute-start.40
  123.9 0.3 collective-permute-start.41
  124.2 1.5 collective-permute-start.42
  125.7 0.2 collective-permute-start.43
  125.9 0.5 copy-done.22
  126.5 15.6 %ladder.2 = (bf16[1200,128]{1,0:T(8,128)(2,1)}, bf16[1200,128]{1,0:T(8,128)(2,1)}, bf16[1200,128]{1,0:T(8,128)(2,1)}, bf16[1200,128]{1,0:T(8,128)(2,1)}, bf16[12...) custom-call(bf16[64,3072]{1,0:T(8,128)(2,1)} %get-tuple-element.31.refs_0, ...), custom_call_target="tpu_custom_call" | custom-call | flops 7549747200 | bytes 21037056 | tf_op jit(solution)/shard_map/ladder/pallas_call | solution.py:109
  142.2 2.0 collective-permute-start.44
  144.2 0.4 collective-permute-start.45
  144.6 0.7 collective-permute-start.15
  145.3 1.5 collective-permute-start.16
  146.8 6.4 %collective-permute-done.44.refs_6_ = bf16[1200,128]{1,0:T(8,128)(2,1)S(1)} collective-permute-done((bf16[1200,128]{1,0:T(8,128)(2,1)S(1)}, bf16[1200,128]{1,0:T(8,128)(2,1)S(1)}, u32[]{:S(2)}, u32[]{:S(2)}) %collective-permute-start.44) | collective-permute-done | bytes 307232 | tf_op jit(solution)/shard_map/ppermute | solution.py:296
  153.2 1.0 collective-permute-start.18
  154.2 4.2 %collective-permute-done.45.refs_7_ = bf16[1200,128]{1,0:T(8,128)(2,1)S(1)} collective-permute-done((bf16[1200,128]{1,0:T(8,128)(2,1)S(1)}, bf16[1200,128]{1,0:T(8,128)(2,1)S(1)}, u32[]{:S(2)}, u32[]{:S(2)}) %collective-permute-start.45) | collective-permute-done | bytes 307232 | tf_op jit(solution)/shard_map/ppermute | solution.py:296
  158.4 1.9 collective-permute-start.19
  160.3 2.0 collective-permute-start.20
  162.3 3.7 %collective-permute-done.16.refs_2_ = bf16[1200,128]{1,0:T(8,128)(2,1)S(1)} collective-permute-done((bf16[1200,128]{1,0:T(8,128)(2,1)}, bf16[1200,128]{1,0:T(8,128)(2,1)S(1)}, u32[]{:S(2)}, u32[]{:S(2)}) %collective-permute-start.16) | collective-permute-done | bytes 307232 | tf_op jit(solution)/shard_map/ppermute | solution.py:296
  166.0 20.3 %symmetrize.3 = (bf16[32,9600]{1,0:T(8,128)(2,1)}, bf16[32,9600]{1,0:T(8,128)(2,1)}) custom-call(s32[2]{0:T(128)} %pad_add_fusion.where_ref, s32[9600]{0:T(1024)} %mirror_ref.5, bf16[1200,128]{1,0:T(8,128)(2,1)} %get-tuple-element.45.refs_0_, bf16[1200,128]{1,0:T(8,128)(2,1)} %copy-done.23, bf16[1200,128]{1,0:T(8,128)(2,1)} %copy-done.25, ...), custom_call_target="tpu_custom_call" | custom-call | flops 698572800 | bytes 19660800 | tf_op jit(solution)/shard_map/symmetrize/pallas_call | solution.py:196
  186.3 8.9 %collective-permute-start.46 = (bf16[32,9600]{1,0:T(8,128)(2,1)}, bf16[32,9600]{1,0:T(8,128)(2,1)S(1)}, u32[]{:S(2)}, u32[]{:S(2)}) collective-permute-start(bf16[32,9600]{1,0:T(8,128)(2,1)} %get-tuple-element.53), channel_id=1, source_target_pairs={{0,2},{1,3},{2,0},{3,1},{4,6},{5,7},{6,4},{7,5},{8,10},{9,11},{10,... | collective-permute-start | bytes 1843208 | tf_op jit(solution)/shard_map/ppermute | solution.py:296
  195.3 0.6 collective-permute-start.47
  196.0 0.6 copy-done.36
  196.6 0.1 copy-done.37
  196.7 0.1 copy-done.38
  196.8 20.3 %symmetrize.2 = (bf16[64,9600]{1,0:T(8,128)(2,1)}, bf16[32,9600]{1,0:T(8,128)(2,1)}) custom-call(s32[2]{0:T(128)} %pad_add_fusion.where_ref, s32[9600]{0:T(1024)} %mirror_ref.5, bf16[1200,128]{1,0:T(8,128)(2,1)} %get-tuple-element.33.refs_0_, bf16[1200,128]{1,0:T(8,128)(2,1)} %copy-done.30, bf16[1200,128]{1,0:T(8,128)(2,1)} %copy-done.31, ...), custom_call_target="tpu_custom_call" | custom-call | flops 855859200 | bytes 19660800 | tf_op jit(solution)/shard_map/symmetrize/pallas_call | solution.py:196
  217.1 0.2 collective-permute-start.22
  217.3 18.6 %collective-permute-done.46.refs_2_ = bf16[32,9600]{1,0:T(8,128)(2,1)S(1)} collective-permute-done((bf16[32,9600]{1,0:T(8,128)(2,1)}, bf16[32,9600]{1,0:T(8,128)(2,1)S(1)}, u32[]{:S(2)}, u32[]{:S(2)}) %collective-permute-start.46) | collective-permute-done | bytes 614432 | tf_op jit(solution)/shard_map/ppermute | solution.py:296
  235.9 13.7 %collective-permute-done.22.refs_1_ = bf16[32,9600]{1,0:T(8,128)(2,1)S(1)} collective-permute-done((bf16[32,9600]{1,0:T(8,128)(2,1)}, bf16[32,9600]{1,0:T(8,128)(2,1)S(1)}, u32[]{:S(2)}, u32[]{:S(2)}) %collective-permute-start.22) | collective-permute-done | bytes 614432 | tf_op jit(solution)/shard_map/ppermute | solution.py:296
  249.6 0.8 copy-done.2
  250.5 22.1 %finish.1 = bf16[128,9600]{1,0:T(8,128)(2,1)} custom-call(s32[2]{0:T(128)} %pad_add_fusion.where_ref, s32[9600]{0:T(1024)} %mirror_ref.5, s32[1,128]{1,0:T(1,128)} %get-tuple-element.30.slot_ref, bf16[64,9600]{1,0:T(8,128)(2,1)} %get-tuple-element.41.refs_0_, bf16[32,9600]{1,0:T(8,128)(2,1)} %copy-done.2, bf16[32,9600]{1,0:T(8,128)(2,1)} %copy-done, ...), custom_call_target="tpu_custom_call" | custom-call | flops 1013145600 | bytes 9830400 | tf_op jit(solution)/shard_map/finish/pallas_call | solution.py:273
  (118 shorter events, 0.7 us)
Async XLA Ops:
  4.0 31.1 %collective-permute-start.23 = (bf16[64,3072]{1,0:T(8,128)(2,1)}, bf16[64,3072]{1,0:T(8,128)(2,1)S(1)}, u32[]{:S(2)}, u32[]{:S(2)}) collective-permute-start(bf16[64,3072]{1,0:T(8,128)(2,1)} %get-tuple-element.43), channel_id=1, source_target_pairs={{0,2},{1,3},{2,0},{3,1},{4,6},{5,7},{6,4},{7,5},{8,10},{9,11},{10,... | collective-permute-start | bytes 1179656 | tf_op jit(solution)/shard_map/ppermute | solution.py:296
  8.0 27.1 %collective-permute-start.24 = (bf16[64,3072]{1,0:T(8,128)(2,1)}, bf16[64,3072]{1,0:T(8,128)(2,1)S(1)}, u32[]{:S(2)}, u32[]{:S(2)}) collective-permute-start(bf16[64,3072]{1,0:T(8,128)(2,1)} %get-tuple-element.44), channel_id=1, source_target_pairs={{0,3},{1,2},{2,1},{3,0},{4,7},{5,6},{6,5},{7,4},{8,11},{9,10},{10,... | collective-permute-start | bytes 1179656 | tf_op jit(solution)/shard_map/ppermute | solution.py:296
  9.4 27.6 %collective-permute-start = (bf16[64,3072]{1,0:T(8,128)(2,1)}, bf16[64,3072]{1,0:T(8,128)(2,1)S(1)}, u32[]{:S(2)}, u32[]{:S(2)}) collective-permute-start(bf16[64,3072]{1,0:T(8,128)(2,1)} %get-tuple-element.32), channel_id=1, source_target_pairs={{0,1},{1,0},{2,3},{3,2},{4,5},{5,4},{6,7},{7,6},{8,9},{9,8},{10,11... | collective-permute-start | bytes 1179656 | tf_op jit(solution)/shard_map/ppermute | solution.py:296
  9.6 28.9 %collective-permute-start.3 = (bf16[64,3072]{1,0:T(8,128)(2,1)}, bf16[64,3072]{1,0:T(8,128)(2,1)S(1)}, u32[]{:S(2)}, u32[]{:S(2)}) collective-permute-start(bf16[64,3072]{1,0:T(8,128)(2,1)} %get-tuple-element.31.refs_0_), channel_id=1, source_target_pairs={{0,8},{4,12},{8,0},{12,4},{16,24},{20,28},{24,16},{28,20},{1,9},{5... | collective-permute-start | bytes 1179656 | tf_op jit(solution)/shard_map/ppermute | solution.py:296
  11.1 28.0 %collective-permute-start.7 = (bf16[64,3072]{1,0:T(8,128)(2,1)}, bf16[64,3072]{1,0:T(8,128)(2,1)S(1)}, u32[]{:S(2)}, u32[]{:S(2)}) collective-permute-start(bf16[64,3072]{1,0:T(8,128)(2,1)} %get-tuple-element.31.refs_0_), channel_id=1, source_target_pairs={{0,16},{4,20},{8,24},{12,28},{16,0},{20,4},{24,8},{28,12},{1,17},{... | collective-permute-start | bytes 1179656 | tf_op jit(solution)/shard_map/ppermute | solution.py:296
  35.1 69.8 %copy-start.7 = (bf16[64,3072]{1,0:T(8,128)(2,1)}, bf16[64,3072]{1,0:T(8,128)(2,1)S(1)}, u32[]{:S(2)}) copy-start(bf16[64,3072]{1,0:T(8,128)(2,1)S(1)} %collective-permute-done.23.refs_0_) | copy-start | bytes 1179652
  35.1 4.2 %collective-permute-start.1 = (bf16[64,3072]{1,0:T(8,128)(2,1)}, bf16[64,3072]{1,0:T(8,128)(2,1)S(1)}, u32[]{:S(2)}, u32[]{:S(2)}) collective-permute-start(bf16[64,3072]{1,0:T(8,128)(2,1)} %get-tuple-element.31.refs_0_), channel_id=1, source_target_pairs={{0,4},{4,0},{8,12},{12,8},{16,20},{20,16},{24,28},{28,24},{1,5},{5... | collective-permute-start | bytes 1179656 | tf_op jit(solution)/shard_map/ppermute | solution.py:296
  35.1 69.8 %copy-start.8 = (bf16[64,3072]{1,0:T(8,128)(2,1)}, bf16[64,3072]{1,0:T(8,128)(2,1)S(1)}, u32[]{:S(2)}) copy-start(bf16[64,3072]{1,0:T(8,128)(2,1)S(1)} %collective-permute-done.24.refs_1_) | copy-start | bytes 1179652
  35.1 12.0 %collective-permute-start.27 = (bf16[64,3072]{1,0:T(8,128)(2,1)S(1)}, bf16[64,3072]{1,0:T(8,128)(2,1)S(1)}, u32[]{:S(2)}, u32[]{:S(2)}) collective-permute-start(bf16[64,3072]{1,0:T(8,128)(2,1)S(1)} %collective-permute-done.23.refs_0_), channel_id=1, source_target_pairs={{0,8},{4,12},{8,0},{12,4},{16,24},{20,28},{24,16},{28,20},{1,9},{5... | collective-permute-start | bytes 1179656 | tf_op jit(solution)/shard_map/ppermute | solution.py:296
  37.0 67.9 %copy-start.3 = (bf16[64,3072]{1,0:T(8,128)(2,1)}, bf16[64,3072]{1,0:T(8,128)(2,1)S(1)}, u32[]{:S(2)}) copy-start(bf16[64,3072]{1,0:T(8,128)(2,1)S(1)} %collective-permute-done.refs_1_) | copy-start | bytes 1179652
  37.0 12.0 %collective-permute-start.32 = (bf16[64,3072]{1,0:T(8,128)(2,1)S(1)}, bf16[64,3072]{1,0:T(8,128)(2,1)S(1)}, u32[]{:S(2)}, u32[]{:S(2)}) collective-permute-start(bf16[64,3072]{1,0:T(8,128)(2,1)S(1)} %collective-permute-done.24.refs_1_), channel_id=1, source_target_pairs={{0,16},{4,20},{8,24},{12,28},{16,0},{20,4},{24,8},{28,12},{1,17},{... | collective-permute-start | bytes 1179656 | tf_op jit(solution)/shard_map/ppermute | solution.py:296
  38.5 66.3 %copy-start.4 = (bf16[64,3072]{1,0:T(8,128)(2,1)}, bf16[64,3072]{1,0:T(8,128)(2,1)S(1)}, u32[]{:S(2)}) copy-start(bf16[64,3072]{1,0:T(8,128)(2,1)S(1)} %collective-permute-done.3.refs_4_) | copy-start | bytes 1179652
  38.5 16.7 %collective-permute-start.28 = (bf16[64,3072]{1,0:T(8,128)(2,1)S(1)}, bf16[64,3072]{1,0:T(8,128)(2,1)}, u32[]{:S(2)}, u32[]{:S(2)}) collective-permute-start(bf16[64,3072]{1,0:T(8,128)(2,1)S(1)} %collective-permute-done.24.refs_1_), channel_id=1, source_target_pairs={{0,8},{4,12},{8,0},{12,4},{16,24},{20,28},{24,16},{28,20},{1,9},{5... | collective-permute-start | bytes 1179656 | tf_op jit(solution)/shard_map/ppermute | solution.py:296
  39.1 65.8 %copy-start.5 = (bf16[64,3072]{1,0:T(8,128)(2,1)}, bf16[64,3072]{1,0:T(8,128)(2,1)S(1)}, u32[]{:S(2)}) copy-start(bf16[64,3072]{1,0:T(8,128)(2,1)S(1)} %collective-permute-done.7.refs_8_) | copy-start | bytes 1179652
  39.1 18.4 %collective-permute-start.31 = (bf16[64,3072]{1,0:T(8,128)(2,1)S(1)}, bf16[64,3072]{1,0:T(8,128)(2,1)}, u32[]{:S(2)}, u32[]{:S(2)}) collective-permute-start(bf16[64,3072]{1,0:T(8,128)(2,1)S(1)} %collective-permute-done.23.refs_0_), channel_id=1, source_target_pairs={{0,16},{4,20},{8,24},{12,28},{16,0},{20,4},{24,8},{28,12},{1,17},{... | collective-permute-start | bytes 1179656 | tf_op jit(solution)/shard_map/ppermute | solution.py:296
  39.2 65.7 %copy-start.6 = (bf16[64,3072]{1,0:T(8,128)(2,1)}, bf16[64,3072]{1,0:T(8,128)(2,1)S(1)}, u32[]{:S(2)}) copy-start(bf16[64,3072]{1,0:T(8,128)(2,1)S(1)} %collective-permute-done.1.refs_2_) | copy-start | bytes 1179652
  39.2 18.3 %collective-permute-start.25 = (bf16[64,3072]{1,0:T(8,128)(2,1)S(1)}, bf16[64,3072]{1,0:T(8,128)(2,1)}, u32[]{:S(2)}, u32[]{:S(2)}) collective-permute-start(bf16[64,3072]{1,0:T(8,128)(2,1)S(1)} %collective-permute-done.23.refs_0_), channel_id=1, source_target_pairs={{0,4},{4,0},{8,12},{12,8},{16,20},{20,16},{24,28},{28,24},{1,5},{5... | collective-permute-start | bytes 1179656 | tf_op jit(solution)/shard_map/ppermute | solution.py:296
  47.1 36.9 %copy-start.13 = (bf16[64,3072]{1,0:T(8,128)(2,1)}, bf16[64,3072]{1,0:T(8,128)(2,1)S(1)}, u32[]{:S(2)}) copy-start(bf16[64,3072]{1,0:T(8,128)(2,1)S(1)} %collective-permute-done.27.refs_4_) | copy-start | bytes 1179652
  47.1 11.5 %collective-permute-start.26 = (bf16[64,3072]{1,0:T(8,128)(2,1)S(1)}, bf16[64,3072]{1,0:T(8,128)(2,1)}, u32[]{:S(2)}, u32[]{:S(2)}) collective-permute-start(bf16[64,3072]{1,0:T(8,128)(2,1)S(1)} %collective-permute-done.24.refs_1_), channel_id=1, source_target_pairs={{0,4},{4,0},{8,12},{12,8},{16,20},{20,16},{24,28},{28,24},{1,5},{5... | collective-permute-start | bytes 1179656 | tf_op jit(solution)/shard_map/ppermute | solution.py:296
  49.0 35.6 %copy-start.15 = (bf16[64,3072]{1,0:T(8,128)(2,1)}, bf16[64,3072]{1,0:T(8,128)(2,1)S(1)}, u32[]{:S(2)}) copy-start(bf16[64,3072]{1,0:T(8,128)(2,1)S(1)} %collective-permute-done.32.refs_9_) | copy-start | bytes 1179652
  49.0 16.9 %collective-permute-start.8 = (bf16[64,3072]{1,0:T(8,128)(2,1)S(1)}, bf16[64,3072]{1,0:T(8,128)(2,1)S(1)}, u32[]{:S(2)}, u32[]{:S(2)}) collective-permute-start(bf16[64,3072]{1,0:T(8,128)(2,1)S(1)} %collective-permute-done.refs_1_), channel_id=1, source_target_pairs={{0,16},{4,20},{8,24},{12,28},{16,0},{20,4},{24,8},{28,12},{1,17},{... | collective-permute-start | bytes 1179656 | tf_op jit(solution)/shard_map/ppermute | solution.py:296
  55.2 19.0 %collective-permute-start.11 = (bf16[64,3072]{1,0:T(8,128)(2,1)S(1)}, bf16[64,3072]{1,0:T(8,128)(2,1)S(1)}, u32[]{:S(2)}, u32[]{:S(2)}) collective-permute-start(bf16[64,3072]{1,0:T(8,128)(2,1)S(1)} %collective-permute-done.3.refs_4_), channel_id=1, source_target_pairs={{0,16},{4,20},{8,24},{12,28},{16,0},{20,4},{24,8},{28,12},{1,17},{... | collective-permute-start | bytes 1179656 | tf_op jit(solution)/shard_map/ppermute | solution.py:296
  57.5 16.9 %collective-permute-start.5 = (bf16[64,3072]{1,0:T(8,128)(2,1)S(1)}, bf16[64,3072]{1,0:T(8,128)(2,1)S(1)}, u32[]{:S(2)}, u32[]{:S(2)}) collective-permute-start(bf16[64,3072]{1,0:T(8,128)(2,1)S(1)} %collective-permute-done.3.refs_4_), channel_id=1, source_target_pairs={{0,4},{4,0},{8,12},{12,8},{16,20},{20,16},{24,28},{28,24},{1,5},{5... | collective-permute-start | bytes 1179656 | tf_op jit(solution)/shard_map/ppermute | solution.py:296
  57.5 16.9 %collective-permute-start.4 = (bf16[64,3072]{1,0:T(8,128)(2,1)S(1)}, bf16[64,3072]{1,0:T(8,128)(2,1)S(1)}, u32[]{:S(2)}, u32[]{:S(2)}) collective-permute-start(bf16[64,3072]{1,0:T(8,128)(2,1)S(1)} %collective-permute-done.refs_1_), channel_id=1, source_target_pairs={{0,8},{4,12},{8,0},{12,4},{16,24},{20,28},{24,16},{28,20},{1,9},{5... | collective-permute-start | bytes 1179656 | tf_op jit(solution)/shard_map/ppermute | solution.py:296
  58.6 16.3 %collective-permute-start.9 = (bf16[64,3072]{1,0:T(8,128)(2,1)S(1)}, bf16[64,3072]{1,0:T(8,128)(2,1)S(1)}, u32[]{:S(2)}, u32[]{:S(2)}) collective-permute-start(bf16[64,3072]{1,0:T(8,128)(2,1)S(1)} %collective-permute-done.7.refs_8_), channel_id=1, source_target_pairs={{0,4},{4,0},{8,12},{12,8},{16,20},{20,16},{24,28},{28,24},{1,5},{5... | collective-permute-start | bytes 1179656 | tf_op jit(solution)/shard_map/ppermute | solution.py:296
  65.8 39.7 %copy-start.9 = (bf16[64,3072]{1,0:T(8,128)(2,1)}, bf16[64,3072]{1,0:T(8,128)(2,1)S(1)}, u32[]{:S(2)}) copy-start(bf16[64,3072]{1,0:T(8,128)(2,1)S(1)} %collective-permute-done.8.refs_9_) | copy-start | bytes 1179652
  65.8 16.2 %collective-permute-start.35 = (bf16[64,3072]{1,0:T(8,128)(2,1)S(1)}, bf16[64,3072]{1,0:T(8,128)(2,1)}, u32[]{:S(2)}, u32[]{:S(2)}) collective-permute-start(bf16[64,3072]{1,0:T(8,128)(2,1)S(1)} %collective-permute-done.27.refs_4_), channel_id=1, source_target_pairs={{0,16},{4,20},{8,24},{12,28},{16,0},{20,4},{24,8},{28,12},{1,17},{... | collective-permute-start | bytes 1179656 | tf_op jit(solution)/shard_map/ppermute | solution.py:296
  74.2 31.4 %copy-start.10 = (bf16[64,3072]{1,0:T(8,128)(2,1)}, bf16[64,3072]{1,0:T(8,128)(2,1)S(1)}, u32[]{:S(2)}) copy-start(bf16[64,3072]{1,0:T(8,128)(2,1)S(1)} %collective-permute-done.11.refs_12_) | copy-start | bytes 1179652
  74.2 9.7 %collective-permute-start.36 = (bf16[64,3072]{1,0:T(8,128)(2,1)S(1)}, bf16[64,3072]{1,0:T(8,128)(2,1)}, u32[]{:S(2)}, u32[]{:S(2)}) collective-permute-start(bf16[64,3072]{1,0:T(8,128)(2,1)S(1)} %collective-permute-done.32.refs_9_), channel_id=1, source_target_pairs={{0,8},{4,12},{8,0},{12,4},{16,24},{20,28},{24,16},{28,20},{1,9},{5... | collective-permute-start | bytes 1179656 | tf_op jit(solution)/shard_map/ppermute | solution.py:296
  74.4 30.5 %copy-start.11 = (bf16[64,3072]{1,0:T(8,128)(2,1)}, bf16[64,3072]{1,0:T(8,128)(2,1)S(1)}, u32[]{:S(2)}) copy-start(bf16[64,3072]{1,0:T(8,128)(2,1)S(1)} %collective-permute-done.5.refs_6_) | copy-start | bytes 1179652
  74.4 10.1 %collective-permute-start.29 = (bf16[64,3072]{1,0:T(8,128)(2,1)S(1)}, bf16[64,3072]{1,0:T(8,128)(2,1)S(1)}, u32[]{:S(2)}, u32[]{:S(2)}) collective-permute-start(bf16[64,3072]{1,0:T(8,128)(2,1)S(1)} %collective-permute-done.27.refs_4_), channel_id=1, source_target_pairs={{0,4},{4,0},{8,12},{12,8},{16,20},{20,16},{24,28},{28,24},{1,5},{5... | collective-permute-start | bytes 1179656 | tf_op jit(solution)/shard_map/ppermute | solution.py:296
  74.4 10.1 %collective-permute-start.34 = (bf16[64,3072]{1,0:T(8,128)(2,1)S(1)}, bf16[64,3072]{1,0:T(8,128)(2,1)S(1)}, u32[]{:S(2)}, u32[]{:S(2)}) collective-permute-start(bf16[64,3072]{1,0:T(8,128)(2,1)S(1)} %collective-permute-done.32.refs_9_), channel_id=1, source_target_pairs={{0,4},{4,0},{8,12},{12,8},{16,20},{20,16},{24,28},{28,24},{1,5},{5... | collective-permute-start | bytes 1179656 | tf_op jit(solution)/shard_map/ppermute | solution.py:296
  74.9 30.0 %collective-permute-start.30 = (bf16[64,3072]{1,0:T(8,128)(2,1)}, bf16[64,3072]{1,0:T(8,128)(2,1)}, u32[]{:S(2)}, u32[]{:S(2)}) collective-permute-start(bf16[64,3072]{1,0:T(8,128)(2,1)} %collective-permute-done.28.refs_5_), channel_id=1, source_target_pairs={{0,4},{4,0},{8,12},{12,8},{16,20},{20,16},{24,28},{28,24},{1,5},{5... | collective-permute-start | bytes 1179656 | tf_op jit(solution)/shard_map/ppermute | solution.py:296
  82.0 23.5 %collective-permute-start.33 = (bf16[64,3072]{1,0:T(8,128)(2,1)}, bf16[64,3072]{1,0:T(8,128)(2,1)}, u32[]{:S(2)}, u32[]{:S(2)}) collective-permute-start(bf16[64,3072]{1,0:T(8,128)(2,1)} %collective-permute-done.31.refs_8_), channel_id=1, source_target_pairs={{0,4},{4,0},{8,12},{12,8},{16,20},{20,16},{24,28},{28,24},{1,5},{5... | collective-permute-start | bytes 1179656 | tf_op jit(solution)/shard_map/ppermute | solution.py:296
  83.9 21.7 %collective-permute-start.12 = (bf16[64,3072]{1,0:T(8,128)(2,1)S(1)}, bf16[64,3072]{1,0:T(8,128)(2,1)}, u32[]{:S(2)}, u32[]{:S(2)}) collective-permute-start(bf16[64,3072]{1,0:T(8,128)(2,1)S(1)} %collective-permute-done.8.refs_9_), channel_id=1, source_target_pairs={{0,8},{4,12},{8,0},{12,4},{16,24},{20,28},{24,16},{28,20},{1,9},{5... | collective-permute-start | bytes 1179656 | tf_op jit(solution)/shard_map/ppermute | solution.py:296
  84.5 21.5 %collective-permute-start.37 = (bf16[64,3072]{1,0:T(8,128)(2,1)}, bf16[64,3072]{1,0:T(8,128)(2,1)}, u32[]{:S(2)}, u32[]{:S(2)}) collective-permute-start(bf16[64,3072]{1,0:T(8,128)(2,1)} %collective-permute-done.35.refs_12_), channel_id=1, source_target_pairs={{0,4},{4,0},{8,12},{12,8},{16,20},{20,16},{24,28},{28,24},{1,5},{5... | collective-permute-start | bytes 1179656 | tf_op jit(solution)/shard_map/ppermute | solution.py:296
  86.0 20.1 %collective-permute-start.38 = (bf16[64,3072]{1,0:T(8,128)(2,1)}, bf16[64,3072]{1,0:T(8,128)(2,1)}, u32[]{:S(2)}, u32[]{:S(2)}) collective-permute-start(bf16[64,3072]{1,0:T(8,128)(2,1)} %collective-permute-done.36.refs_13_), channel_id=1, source_target_pairs={{0,4},{4,0},{8,12},{12,8},{16,20},{20,16},{24,28},{28,24},{1,5},{5... | collective-permute-start | bytes 1179656 | tf_op jit(solution)/shard_map/ppermute | solution.py:296
  104.9 17.3 %collective-permute-start.2 = (bf16[64,3072]{1,0:T(8,128)(2,1)S(1)}, bf16[64,3072]{1,0:T(8,128)(2,1)S(1)}, u32[]{:S(2)}, u32[]{:S(2)}) collective-permute-start(bf16[64,3072]{1,0:T(8,128)(2,1)S(1)} %collective-permute-done.refs_1_), channel_id=1, source_target_pairs={{0,4},{4,0},{8,12},{12,8},{16,20},{20,16},{24,28},{28,24},{1,5},{5... | collective-permute-start | bytes 1179656 | tf_op jit(solution)/shard_map/ppermute | solution.py:296
  105.5 18.4 %collective-permute-start.10 = (bf16[64,3072]{1,0:T(8,128)(2,1)S(1)}, bf16[64,3072]{1,0:T(8,128)(2,1)S(1)}, u32[]{:S(2)}, u32[]{:S(2)}) collective-permute-start(bf16[64,3072]{1,0:T(8,128)(2,1)S(1)} %collective-permute-done.8.refs_9_), channel_id=1, source_target_pairs={{0,4},{4,0},{8,12},{12,8},{16,20},{20,16},{24,28},{28,24},{1,5},{5... | collective-permute-start | bytes 1179656 | tf_op jit(solution)/shard_map/ppermute | solution.py:296
  105.6 16.8 %collective-permute-start.13 = (bf16[64,3072]{1,0:T(8,128)(2,1)S(1)}, bf16[64,3072]{1,0:T(8,128)(2,1)S(1)}, u32[]{:S(2)}, u32[]{:S(2)}) collective-permute-start(bf16[64,3072]{1,0:T(8,128)(2,1)S(1)} %collective-permute-done.11.refs_12_), channel_id=1, source_target_pairs={{0,4},{4,0},{8,12},{12,8},{16,20},{20,16},{24,28},{28,24},{1,5},{5... | collective-permute-start | bytes 1179656 | tf_op jit(solution)/shard_map/ppermute | solution.py:296
  106.0 18.2 %collective-permute-start.6 = (bf16[64,3072]{1,0:T(8,128)(2,1)}, bf16[64,3072]{1,0:T(8,128)(2,1)S(1)}, u32[]{:S(2)}, u32[]{:S(2)}) collective-permute-start(bf16[64,3072]{1,0:T(8,128)(2,1)} %copy-done.12), channel_id=1, source_target_pairs={{0,4},{4,0},{8,12},{12,8},{16,20},{20,16},{24,28},{28,24},{1,5},{5... | collective-permute-start | bytes 1179656 | tf_op jit(solution)/shard_map/ppermute | solution.py:296
  106.1 19.6 %collective-permute-start.14 = (bf16[64,3072]{1,0:T(8,128)(2,1)}, bf16[64,3072]{1,0:T(8,128)(2,1)S(1)}, u32[]{:S(2)}, u32[]{:S(2)}) collective-permute-start(bf16[64,3072]{1,0:T(8,128)(2,1)} %collective-permute-done.12.refs_13_), channel_id=1, source_target_pairs={{0,4},{4,0},{8,12},{12,8},{16,20},{20,16},{24,28},{28,24},{1,5},{5... | collective-permute-start | bytes 1179656 | tf_op jit(solution)/shard_map/ppermute | solution.py:296
  122.2 21.9 %copy-start.24 = (bf16[1200,128]{1,0:T(8,128)(2,1)S(1)}, bf16[1200,128]{1,0:T(8,128)(2,1)}, u32[]{:S(2)}) copy-start(bf16[1200,128]{1,0:T(8,128)(2,1)} %get-tuple-element.52) | copy-start | bytes 921604
  122.3 19.9 %collective-permute-start.39 = (bf16[1200,128]{1,0:T(8,128)(2,1)}, bf16[1200,128]{1,0:T(8,128)(2,1)S(1)}, u32[]{:S(2)}, u32[]{:S(2)}) collective-permute-start(bf16[1200,128]{1,0:T(8,128)(2,1)} %get-tuple-element.46), channel_id=1, source_target_pairs={{0,4},{4,0},{8,12},{12,8},{16,20},{20,16},{24,28},{28,24},{1,5},{5... | collective-permute-start | bytes 921608 | tf_op jit(solution)/shard_map/ppermute | solution.py:296
  122.4 21.8 %collective-permute-start.40 = (bf16[1200,128]{1,0:T(8,128)(2,1)}, bf16[1200,128]{1,0:T(8,128)(2,1)S(1)}, u32[]{:S(2)}, u32[]{:S(2)}) collective-permute-start(bf16[1200,128]{1,0:T(8,128)(2,1)} %get-tuple-element.47), channel_id=1, source_target_pairs={{0,8},{4,12},{8,0},{12,4},{16,24},{20,28},{24,16},{28,20},{1,9},{5... | collective-permute-start | bytes 921608 | tf_op jit(solution)/shard_map/ppermute | solution.py:296
  123.9 20.7 %collective-permute-start.41 = (bf16[1200,128]{1,0:T(8,128)(2,1)}, bf16[1200,128]{1,0:T(8,128)(2,1)S(1)}, u32[]{:S(2)}, u32[]{:S(2)}) collective-permute-start(bf16[1200,128]{1,0:T(8,128)(2,1)} %get-tuple-element.48), channel_id=1, source_target_pairs={{0,12},{4,8},{8,4},{12,0},{16,28},{20,24},{24,20},{28,16},{1,13},{... | collective-permute-start | bytes 921608 | tf_op jit(solution)/shard_map/ppermute | solution.py:296
  124.2 21.1 %collective-permute-start.42 = (bf16[1200,128]{1,0:T(8,128)(2,1)}, bf16[1200,128]{1,0:T(8,128)(2,1)S(1)}, u32[]{:S(2)}, u32[]{:S(2)}) collective-permute-start(bf16[1200,128]{1,0:T(8,128)(2,1)} %get-tuple-element.49), channel_id=1, source_target_pairs={{0,16},{4,20},{8,24},{12,28},{16,0},{20,4},{24,8},{28,12},{1,17},{... | collective-permute-start | bytes 921608 | tf_op jit(solution)/shard_map/ppermute | solution.py:296
  125.7 21.1 %collective-permute-start.43 = (bf16[1200,128]{1,0:T(8,128)(2,1)}, bf16[1200,128]{1,0:T(8,128)(2,1)S(1)}, u32[]{:S(2)}, u32[]{:S(2)}) collective-permute-start(bf16[1200,128]{1,0:T(8,128)(2,1)} %get-tuple-element.50), channel_id=1, source_target_pairs={{0,20},{4,16},{8,28},{12,24},{16,4},{20,0},{24,12},{28,8},{1,21},{... | collective-permute-start | bytes 921608 | tf_op jit(solution)/shard_map/ppermute | solution.py:296
  142.1 23.8 %copy-start.23 = (bf16[1200,128]{1,0:T(8,128)(2,1)}, bf16[1200,128]{1,0:T(8,128)(2,1)S(1)}, u32[]{:S(2)}) copy-start(bf16[1200,128]{1,0:T(8,128)(2,1)S(1)} %collective-permute-done.39.refs_1_) | copy-start | bytes 921604
  142.2 11.1 %collective-permute-start.44 = (bf16[1200,128]{1,0:T(8,128)(2,1)S(1)}, bf16[1200,128]{1,0:T(8,128)(2,1)S(1)}, u32[]{:S(2)}, u32[]{:S(2)}) collective-permute-start(bf16[1200,128]{1,0:T(8,128)(2,1)S(1)} %copy-done.26), channel_id=1, source_target_pairs={{0,24},{4,28},{8,16},{12,20},{16,8},{20,12},{24,0},{28,4},{1,25},{... | collective-permute-start | bytes 921608 | tf_op jit(solution)/shard_map/ppermute | solution.py:296
  144.2 21.8 %copy-start.25 = (bf16[1200,128]{1,0:T(8,128)(2,1)}, bf16[1200,128]{1,0:T(8,128)(2,1)S(1)}, u32[]{:S(2)}) copy-start(bf16[1200,128]{1,0:T(8,128)(2,1)S(1)} %collective-permute-done.40.refs_2_) | copy-start | bytes 921604
  144.2 14.2 %collective-permute-start.45 = (bf16[1200,128]{1,0:T(8,128)(2,1)S(1)}, bf16[1200,128]{1,0:T(8,128)(2,1)S(1)}, u32[]{:S(2)}, u32[]{:S(2)}) collective-permute-start(bf16[1200,128]{1,0:T(8,128)(2,1)S(1)} %copy-done.24), channel_id=1, source_target_pairs={{0,28},{4,24},{8,20},{12,16},{16,12},{20,8},{24,4},{28,0},{1,29},{... | collective-permute-start | bytes 921608 | tf_op jit(solution)/shard_map/ppermute | solution.py:296
  144.6 15.7 %collective-permute-start.15 = (bf16[1200,128]{1,0:T(8,128)(2,1)}, bf16[1200,128]{1,0:T(8,128)(2,1)S(1)}, u32[]{:S(2)}, u32[]{:S(2)}) collective-permute-start(bf16[1200,128]{1,0:T(8,128)(2,1)} %get-tuple-element.34), channel_id=1, source_target_pairs={{0,4},{4,0},{8,12},{12,8},{16,20},{20,16},{24,28},{28,24},{1,5},{5... | collective-permute-start | bytes 921608 | tf_op jit(solution)/shard_map/ppermute | solution.py:296
  145.3 20.6 %collective-permute-start.16 = (bf16[1200,128]{1,0:T(8,128)(2,1)}, bf16[1200,128]{1,0:T(8,128)(2,1)S(1)}, u32[]{:S(2)}, u32[]{:S(2)}) collective-permute-start(bf16[1200,128]{1,0:T(8,128)(2,1)} %get-tuple-element.35), channel_id=1, source_target_pairs={{0,8},{4,12},{8,0},{12,4},{16,24},{20,28},{24,16},{28,20},{1,9},{5... | collective-permute-start | bytes 921608 | tf_op jit(solution)/shard_map/ppermute | solution.py:296
  146.8 39.5 %collective-permute-start.17 = (bf16[1200,128]{1,0:T(8,128)(2,1)}, bf16[1200,128]{1,0:T(8,128)(2,1)S(1)}, u32[]{:S(2)}, u32[]{:S(2)}) collective-permute-start(bf16[1200,128]{1,0:T(8,128)(2,1)} %get-tuple-element.36), channel_id=1, source_target_pairs={{0,12},{4,8},{8,4},{12,0},{16,28},{20,24},{24,20},{28,16},{1,13},{... | collective-permute-start | bytes 921608 | tf_op jit(solution)/shard_map/ppermute | solution.py:296
  153.2 42.0 %collective-permute-start.18 = (bf16[1200,128]{1,0:T(8,128)(2,1)}, bf16[1200,128]{1,0:T(8,128)(2,1)S(1)}, u32[]{:S(2)}, u32[]{:S(2)}) collective-permute-start(bf16[1200,128]{1,0:T(8,128)(2,1)} %get-tuple-element.37), channel_id=1, source_target_pairs={{0,16},{4,20},{8,24},{12,28},{16,0},{20,4},{24,8},{28,12},{1,17},{... | collective-permute-start | bytes 921608 | tf_op jit(solution)/shard_map/ppermute | solution.py:296
  158.4 37.4 %collective-permute-start.19 = (bf16[1200,128]{1,0:T(8,128)(2,1)}, bf16[1200,128]{1,0:T(8,128)(2,1)S(1)}, u32[]{:S(2)}, u32[]{:S(2)}) collective-permute-start(bf16[1200,128]{1,0:T(8,128)(2,1)} %get-tuple-element.38), channel_id=1, source_target_pairs={{0,20},{4,16},{8,28},{12,24},{16,4},{20,0},{24,12},{28,8},{1,21},{... | collective-permute-start | bytes 921608 | tf_op jit(solution)/shard_map/ppermute | solution.py:296
  160.3 35.6 %copy-start.30 = (bf16[1200,128]{1,0:T(8,128)(2,1)}, bf16[1200,128]{1,0:T(8,128)(2,1)S(1)}, u32[]{:S(2)}) copy-start(bf16[1200,128]{1,0:T(8,128)(2,1)S(1)} %collective-permute-done.15.refs_1_) | copy-start | bytes 921604
  160.3 35.6 %collective-permute-start.20 = (bf16[1200,128]{1,0:T(8,128)(2,1)}, bf16[1200,128]{1,0:T(8,128)(2,1)S(1)}, u32[]{:S(2)}, u32[]{:S(2)}) collective-permute-start(bf16[1200,128]{1,0:T(8,128)(2,1)} %get-tuple-element.39), channel_id=1, source_target_pairs={{0,24},{4,28},{8,16},{12,20},{16,8},{20,12},{24,0},{28,4},{1,25},{... | collective-permute-start | bytes 921608 | tf_op jit(solution)/shard_map/ppermute | solution.py:296
  166.0 29.9 %copy-start.31 = (bf16[1200,128]{1,0:T(8,128)(2,1)}, bf16[1200,128]{1,0:T(8,128)(2,1)S(1)}, u32[]{:S(2)}) copy-start(bf16[1200,128]{1,0:T(8,128)(2,1)S(1)} %collective-permute-done.16.refs_2_) | copy-start | bytes 921604
  166.0 29.9 %collective-permute-start.21 = (bf16[1200,128]{1,0:T(8,128)(2,1)}, bf16[1200,128]{1,0:T(8,128)(2,1)S(1)}, u32[]{:S(2)}, u32[]{:S(2)}) collective-permute-start(bf16[1200,128]{1,0:T(8,128)(2,1)} %get-tuple-element.40), channel_id=1, source_target_pairs={{0,28},{4,24},{8,20},{12,16},{16,12},{20,8},{24,4},{28,0},{1,29},{... | collective-permute-start | bytes 921608 | tf_op jit(solution)/shard_map/ppermute | solution.py:296
  186.3 49.6 %collective-permute-start.46 = (bf16[32,9600]{1,0:T(8,128)(2,1)}, bf16[32,9600]{1,0:T(8,128)(2,1)S(1)}, u32[]{:S(2)}, u32[]{:S(2)}) collective-permute-start(bf16[32,9600]{1,0:T(8,128)(2,1)} %get-tuple-element.53), channel_id=1, source_target_pairs={{0,2},{1,3},{2,0},{3,1},{4,6},{5,7},{6,4},{7,5},{8,10},{9,11},{10,... | collective-permute-start | bytes 1843208 | tf_op jit(solution)/shard_map/ppermute | solution.py:296
  195.3 40.6 %collective-permute-start.47 = (bf16[32,9600]{1,0:T(8,128)(2,1)}, bf16[32,9600]{1,0:T(8,128)(2,1)S(1)}, u32[]{:S(2)}, u32[]{:S(2)}) collective-permute-start(bf16[32,9600]{1,0:T(8,128)(2,1)} %get-tuple-element.54), channel_id=1, source_target_pairs={{0,3},{1,2},{2,1},{3,0},{4,7},{5,6},{6,5},{7,4},{8,11},{9,10},{10,... | collective-permute-start | bytes 1843208 | tf_op jit(solution)/shard_map/ppermute | solution.py:296
  217.1 32.5 %collective-permute-start.22 = (bf16[32,9600]{1,0:T(8,128)(2,1)}, bf16[32,9600]{1,0:T(8,128)(2,1)S(1)}, u32[]{:S(2)}, u32[]{:S(2)}) collective-permute-start(bf16[32,9600]{1,0:T(8,128)(2,1)} %get-tuple-element.42), channel_id=1, source_target_pairs={{0,1},{1,0},{2,3},{3,2},{4,5},{5,4},{6,7},{7,6},{8,9},{9,8},{10,11... | collective-permute-start | bytes 1843208 | tf_op jit(solution)/shard_map/ppermute | solution.py:296
  (23 other events, 172.9 us)

commit v2 on v1

--- a/solution.py
+++ b/solution.py
@@ -11,15 +11,16 @@
 F32, BF16, I32 = jnp.float32, jnp.bfloat16, jnp.int32
 NN = (((1,), (0,)), ((), ()))
 NT = (((1,), (1,)), ((), ()))
-VMEM_LIMIT = 56 * 1024 * 1024
+VMEM_LIMIT = 24 * 1024 * 1024
+LADDER_LIMIT = 56 * 1024 * 1024
 
 
 def iota(shape, dim):
     return lax.broadcasted_iota(I32, shape, dim)
 
 
-def params():
-    return pltpu.CompilerParams(vmem_limit_bytes=VMEM_LIMIT)
+def params(limit=VMEM_LIMIT):
+    return pltpu.CompilerParams(vmem_limit_bytes=limit)
 
 
 def pack_kernel(cols, owned, half, where_ref, irreps_ref, mirror_ref, amp_ref, slot_ref, *out_refs):
@@ -94,30 +95,30 @@
             copy.wait()
 
     ladder = [
-        lax.dot_general(rows_ref[i], integrals_ref[i], NN, preferred_element_type=F32) for i in range(owned)
+        lax.dot_general(integrals_ref[i], rows_ref[i], NT, preferred_element_type=F32) for i in range(owned)
     ]
     for o in range(holders):
-        block = jnp.concatenate([ladder[i][o * group : (o + 1) * group] for i in range(owned)], axis=0)
-        outs[o][...] = block.T.astype(BF16)
+        here = slice(o * group, (o + 1) * group)
+        outs[o][...] = jnp.concatenate([ladder[i][:, here] for i in range(owned)], axis=1).astype(BF16)
 
 
 def product(pieces, integrals, holders, chunk_count, slots):
-    owned, contract, share = integrals.shape
-    tile = 256
+    owned, share, contract = integrals.shape
+    tile = 240
     group = chunk_count * slots
     lanes = owned * group
     return pl.pallas_call(
         functools.partial(product_kernel, holders, chunk_count, owned, slots),
         grid=(pl.cdiv(share, tile),),
         in_specs=[pl.BlockSpec(memory_space=pl.ANY)] * (holders * chunk_count)
-        + [pl.BlockSpec((owned, contract, tile), lambda s: (0, 0, s))],
+        + [pl.BlockSpec((owned, tile, contract), lambda s: (0, s, 0))],
         out_specs=[pl.BlockSpec((tile, lanes), lambda s: (s, 0))] * holders,
         out_shape=[jax.ShapeDtypeStruct((share, lanes), BF16)] * holders,
         scratch_shapes=[
             pltpu.VMEM((owned, holders * group, contract), BF16),
             pltpu.SemaphoreType.DMA((holders * chunk_count * owned,)),
         ],
-        compiler_params=params(),
+        compiler_params=params(LADDER_LIMIT),
         cost_estimate=pl.CostEstimate(
             flops=2 * owned * holders * group * contract * share,
             bytes_accessed=2 * owned * contract * (share + holders * group),
@@ -128,12 +129,13 @@
 
 
 def gather_rows(mirror_ref, base, source, target, count):
-    step = 16
+    step = 64
 
     def some(n, carry):
+        at = n * step
+        rows = [source[pl.ds(mirror_ref[base + at + u], 1), :] for u in range(step)]
         for u in range(step):
-            at = n * step + u
-            target[pl.ds(at, 1), :] = source[pl.ds(mirror_ref[base + at], 1), :]
+            target[pl.ds(at + u, 1), :] = rows[u]
         return carry
 
     lax.fori_loop(0, count // step, some, 0)
@@ -163,21 +165,25 @@
     base = step * block
     gather_rows(mirror_ref, base, wide, picked, block)
     here = wide[pl.ds(pl.multiple_of(base, 128), block), :].astype(BF16)
-    there = picked[...].astype(BF16)
+    both = jnp.concatenate([here, picked[...].astype(BF16)], axis=1)
     group = len(chunks) * 2 * half
+    picks = []
     for j, k in enumerate(chunks):
-        both = 2 if k == 0 else 1
-        rows = outs[j].shape[0]
-        row, lane = iota((rows, lanes), 0), iota((rows, lanes), 1)
-        irrep, rest = row // (both * half), row % (both * half)
+        sides = 2 if k == 0 else 1
+        shape = (outs[j].shape[0], lanes)
+        row, lane = iota(shape, 0), iota(shape, 1)
+        irrep, rest = row // (sides * half), row % (sides * half)
         side, rank = rest // half, rest % half
         start = irrep * group + j * 2 * half + rank
-        mine = (lane == start + side * half).astype(F32).astype(BF16)
-        other = (lane == start + (1 - side) * half).astype(F32).astype(BF16)
-        outs[j][...] = (
-            lax.dot_general(mine, here, NT, preferred_element_type=F32)
-            + lax.dot_general(other, there, NT, preferred_element_type=F32)
-        ).astype(BF16)
+        mine = lane == start + side * half
+        other = lane == start + (1 - side) * half
+        picks.append(jnp.concatenate([mine.astype(F32), other.astype(F32)], axis=1))
+    pick = jnp.concatenate(picks, axis=0).astype(BF16)
+    total = lax.dot_general(pick, both, NT, preferred_element_type=F32).astype(BF16)
+    at = 0
+    for out in outs:
+        out[...] = total[at : at + out.shape[0]]
+        at += out.shape[0]
 
 
 def block_of(slab):
@@ -296,11 +302,37 @@
     return lax.ppermute(array, axis, [(i, i ^ offset) for i in range(lax.axis_size(axis))])
 
 
-def gather_row_axis(chunk, order):
-    held = {0: chunk}
+def after(arrays, earlier):
+    earlier = tuple(earlier)
+    return list(lax.optimization_barrier((tuple(arrays), earlier))[0]) if earlier else list(arrays)
+
+
+def spread(chunk, order):
+    return {0: chunk, **{bit: swap(chunk, "row", bit) for bit in order}}
+
+
+def forward(held, order):
+    reach = [0]
+    fresh = []
     for bit in order:
-        held.update({offset ^ bit: swap(array, "row", bit) for offset, array in list(held.items())})
-    return held
+        for offset in list(reach):
+            if offset ^ bit not in held:
+                held[offset ^ bit] = swap(held[offset], "row", bit)
+                fresh.append(offset ^ bit)
+            reach.append(offset ^ bit)
+    return fresh
+
+
+def share_cores(held, core, offsets):
+    for bit in core:
+        for offset in list(offsets):
+            held[offset ^ bit] = swap(held[offset], "row", bit)
+    return [held[offset ^ bit] for bit in core for offset in offsets]
+
+
+def gate(held, earlier):
+    offsets = list(held)
+    held.update(zip(offsets, after([held[o] for o in offsets], earlier)))
 
 
 def body(amplitudes, integrals, irreps, row_mirror, col_mirror):
@@ -311,22 +343,66 @@
     half = slots // 2
     where = jnp.stack([lax.axis_index("row"), lax.axis_index("col")]).astype(I32)
     slot, packed = pack(where, irreps[None], row_mirror[None], amplitudes, cols, owned, half)
-    chunks = [packed[0]] + [swap(packed[k], "col", k) for k in range(1, cols)]
     bits = [1 << b for b in range(rows.bit_length() - 1)]
     outer, core = bits[1:], bits[:1]
-    size = max(1, 4 // owned)
+    turns = max(1, cols // max(1, 4 // owned))
+    batches = [tuple(range(first, cols, turns)) for first in range(turns)]
+    integrals_t = jnp.swapaxes(integrals, 1, 2)
+
+    ready = {}
+    for k in range(cols):
+        early = () if k < 3 else (ready[k - 1],)
+        ready[k] = swap(after([packed[k]], early)[0], "col", k) if k else packed[0]
+
+    combined = range(2, rows, 2)
+    held, parts = {}, []
+    turned = []
+    for n, batch in enumerate(batches):
+        if n == 0:
+            for j, k in enumerate(batch):
+                chunk = ready[k]
+                if j:
+                    (chunk,) = after([chunk], [ready[k - 1], *turned])
+                held[k] = {0: chunk, **{o: swap(chunk, "row", o) for o in combined}}
+                turned = [held[k][o] for o in combined]
+                last = combined[-1]
+                share_cores(held[k], core, [o for o in held[k] if o != last])
+                if j and k + 1 < cols:
+                    (held[k][last],) = after([held[k][last]], [ready[k + 1]])
+                share_cores(held[k], core, [last])
+        else:
+            turned = []
+            for j, k in enumerate(batch):
+                turn = j % len(outer)
+                order = outer[turn:] + outer[:turn]
+                held[k] = spread(ready[k], order)
+            for j, k in enumerate(batch):
+                turn = j % len(outer)
+                order = outer[turn:] + outer[:turn]
+                gate(held[k], parts[-1][1:2])
+                first = list(held[k])
+                fresh = forward(held[k], order)
+                turned += [held[k][o] for o in fresh]
+                share_cores(held[k], core, first)
+                share_cores(held[k], core, fresh)
+        pieces = [held[k][o] for o in range(rows) for k in batch]
+        parts.append(product(pieces, integrals_t, rows, len(batch), slots))
+
+    far = sorted(range(1, rows), key=lambda o: (-(o >> 1).bit_count(), -o))
     sums = {}
-    for first in range(0, cols, size):
-        batch = tuple(range(first, min(first + size, cols)))
-        held = []
-        for j, k in enumerate(batch):
-            turn = j % len(outer)
-            held.append(gather_row_axis(chunks[k], outer[turn:] + outer[:turn] + core))
-        pieces = [held[j][o] for o in range(rows) for j in range(len(batch))]
-        parts = product(pieces, integrals, rows, len(batch), slots)
-        parts = [parts[0]] + [swap(parts[o], "row", o) for o in range(1, rows)]
-        for k, part in zip(batch, symmetrize(where, col_mirror, parts, batch, owned, half)):
-            sums[k] = part if k == 0 else swap(part, "col", k)
+    hidden = [part[:1] for part in parts[1:]]
+    last = turned
+    for n, (batch, part) in enumerate(zip(batches, parts)):
+        part = list(part)
+        for m, o in enumerate(far):
+            earlier = list(last) if n or m >= 2 else []
+            if m >= len(far) - 2 and n < len(hidden) + 1:
+                earlier += [part[f] for f in far[:2]] + list(hidden[n] if n < len(hidden) else totals[:1])
+            part[o] = swap(after([part[o]], earlier)[0], "row", o)
+        last = [part[o] for o in far]
+        totals = symmetrize(where, col_mirror, part, batch, owned, half)
+        for k, total in zip(batch, totals):
+            sums[k] = total if k == 0 else swap(total, "col", k)
     return finish(where, col_mirror, slot, sums[0], [sums[k] for k in range(1, cols)], owned, half)
 
 

time: 274 us -> 215 us (0.78)
  Pallas kernels: 97.3 us -> 73.9 us
  waiting for transfers between devices: 107 us -> 83.9 us
  local copies, waits for them, and re-layouts: 22.7 us -> 3.35 us
  starting transfers between devices: 44.6 us -> 52.9 us
    ppermute x48, waiting for transfers between devices: 107 us -> 83.9 us  [swap(): lax.ppermute(array, axis, [(i, i ^ offset) for i in range(lax.axis_size(a...]
    unnamed x79 -> x82, local copies, waits for them, and re-layouts: 22.7 us -> 3.35 us
    pallas_call x2, Pallas kernels: 40.6 us -> 25.9 us  [symmetrize(): pl.pallas_call(functools.partial(symmetrize_kernel, holders, chunks, owne...]
    ppermute x48, starting transfers between devices: 44.6 us -> 52.9 us  [swap(): lax.ppermute(array, axis, [(i, i ^ offset) for i in range(lax.axis_size(a...]
    pallas_call x1, Pallas kernels: 22.1 us -> 15.9 us  [finish(): pl.pallas_call(functools.partial(finish_kernel, cols, owned, half), grid_...]
  transfers between devices with their start and end apart: 48 -> 48, of which waited for: 14 -> 18; matrix products, arithmetic and copies ran while one was open for 7% -> 0% of each run, Pallas kernels for 26% -> 26%
where the time goes in v2:
time: 215 us
  waiting for transfers between devices  83.9 us (39%)
  Pallas kernels  73.9 us (34%)
  starting transfers between devices  52.9 us (25%)
  local copies, waits for them, and re-layouts  3.35 us (2%)
    ppermute x48, waiting for transfers between devices, swap(): lax.ppermute(array, axis, [(i, i ^ offset) for i in range(lax.axis_size(a...  83.9 us
    ppermute x48, starting transfers between devices, swap(): lax.ppermute(array, axis, [(i, i ^ offset) for i in range(lax.axis_size(a...  52.9 us
    pallas_call x2, Pallas kernels, product(): pl.pallas_call(functools.partial(product_kernel, holders, chunk_count, ow...  30.9 us
    pallas_call x2, Pallas kernels, symmetrize(): pl.pallas_call(functools.partial(symmetrize_kernel, holders, chunks, owne...  25.9 us
    pallas_call x1, Pallas kernels, finish(): pl.pallas_call(functools.partial(finish_kernel, cols, owned, half), grid_...  15.9 us
  transfers between devices with their start and end apart: 48, of which 18 were waited for; matrix products, arithmetic and copies ran while one was open for 0% of the time, Pallas kernels for 26%

profile of v2, /device:TPU:0, one launch (start us, length us, event | category | flops | bytes accessed | tf_op | source)
XLA Modules:
  0.0 214.6 jit_solution(1803673739426082866)
XLA Ops:
  0.1 1.1 copy-done
  1.2 0.7 copy-done.2
  1.9 0.7 copy-done.3
  2.5 1.2 pack.1
  3.7 4.1 %collective-permute-start = (bf16[64,3072]{1,0:T(8,128)(2,1)S(1)}, bf16[64,3072]{1,0:T(8,128)(2,1)S(1)}, u32[]{:S(2)}, u32[]{:S(2)}) collective-permute-start(bf16[64,3072]{1,0:T(8,128)(2,1)S(1)} %get-tuple-element.53), channel_id=1, source_target_pairs={{0,2},{1,3},{2,0},{3,1},{4,6},{5,7},{6,4},{7,5},{8,10},{9,11},{10,... | collective-permute-start | bytes 1179656 | tf_op jit(solution)/shard_map/ppermute | solution.py:302
  7.8 1.6 collective-permute-start.1
  9.4 2.4 %collective-permute-start.4 = (bf16[64,3072]{1,0:T(8,128)(2,1)S(1)}, bf16[64,3072]{1,0:T(8,128)(2,1)S(1)}, u32[]{:S(2)}, u32[]{:S(2)}) collective-permute-start(bf16[64,3072]{1,0:T(8,128)(2,1)S(1)} %get-tuple-element.52.refs_0_), channel_id=1, source_target_pairs={{0,24},{4,28},{8,16},{12,20},{16,8},{20,12},{24,0},{28,4},{1,25},{... | collective-permute-start | bytes 1179656 | tf_op jit(solution)/shard_map/ppermute | solution.py:302
  11.9 0.5 collective-permute-start.3
  12.4 0.5 collective-permute-start.2
  12.9 12.6 %collective-permute-done.refs_1_ = bf16[64,3072]{1,0:T(8,128)(2,1)S(1)} collective-permute-done((bf16[64,3072]{1,0:T(8,128)(2,1)S(1)}, bf16[64,3072]{1,0:T(8,128)(2,1)S(1)}, u32[]{:S(2)}, u32[]{:S(2)}) %collective-permute-start) | collective-permute-done | bytes 393248 | tf_op jit(solution)/shard_map/ppermute | solution.py:302
  25.5 3.4 %collective-permute-start.14 = (bf16[64,3072]{1,0:T(8,128)(2,1)S(1)}, bf16[64,3072]{1,0:T(8,128)(2,1)S(1)}, u32[]{:S(2)}, u32[]{:S(2)}) collective-permute-start(bf16[64,3072]{1,0:T(8,128)(2,1)S(1)} %get-tuple-element.57), channel_id=1, source_target_pairs={{0,3},{1,2},{2,1},{3,0},{4,7},{5,6},{6,5},{7,4},{8,11},{9,10},{10,... | collective-permute-start | bytes 1179656 | tf_op jit(solution)/shard_map/ppermute | solution.py:302
  28.9 0.1 collective-permute-done.3.refs_8_
  29.0 0.1 collective-permute-done.2.refs_4_
  29.1 2.4 %collective-permute-start.13 = (bf16[64,3072]{1,0:T(8,128)(2,1)S(1)}, bf16[64,3072]{1,0:T(8,128)(2,1)S(1)}, u32[]{:S(2)}, u32[]{:S(2)}) collective-permute-start(bf16[64,3072]{1,0:T(8,128)(2,1)S(1)} %collective-permute-done.refs_1_), channel_id=1, source_target_pairs={{0,24},{4,28},{8,16},{12,20},{16,8},{20,12},{24,0},{28,4},{1,25},{... | collective-permute-start | bytes 1179656 | tf_op jit(solution)/shard_map/ppermute | solution.py:302
  31.5 0.5 collective-permute-start.15
  32.0 6.3 %collective-permute-done.14.refs_1_ = bf16[64,3072]{1,0:T(8,128)(2,1)S(1)} collective-permute-done((bf16[64,3072]{1,0:T(8,128)(2,1)S(1)}, bf16[64,3072]{1,0:T(8,128)(2,1)S(1)}, u32[]{:S(2)}, u32[]{:S(2)}) %collective-permute-start.14) | collective-permute-done | bytes 393248 | tf_op jit(solution)/shard_map/ppermute | solution.py:302
  38.3 1.5 collective-permute-start.10
  39.9 1.3 collective-permute-done.13.refs_13_
  41.2 1.5 collective-permute-start.7
  42.7 0.5 collective-permute-start.8
  43.3 6.2 %collective-permute-done.10.refs_9_ = bf16[64,3072]{1,0:T(8,128)(2,1)S(1)} collective-permute-done((bf16[64,3072]{1,0:T(8,128)(2,1)S(1)}, bf16[64,3072]{1,0:T(8,128)(2,1)S(1)}, u32[]{:S(2)}, u32[]{:S(2)}) %collective-permute-start.10) | collective-permute-done | bytes 393248 | tf_op jit(solution)/shard_map/ppermute | solution.py:302
  49.5 1.7 collective-permute-done.7.refs_5_
  51.2 1.6 collective-permute-start.18
  52.9 0.8 collective-permute-start.17
  53.7 1.2 collective-permute-start.21
  54.9 0.5 collective-permute-start.20
  55.4 0.8 copy-done.36
  56.2 15.4 %ladder.2 = (bf16[1200,128]{1,0:T(8,128)(2,1)}, bf16[1200,128]{1,0:T(8,128)(2,1)}, bf16[1200,128]{1,0:T(8,128)(2,1)}, bf16[1200,128]{1,0:T(8,128)(2,1)}, bf16[12...) custom-call(bf16[64,3072]{1,0:T(8,128)(2,1)} %copy-done.4, ...), custom_call_target="tpu_custom_call" | custom-call | flops 7549747200 | bytes 21037056 | tf_op jit(solution)/shard_map/ladder/pallas_call | solution.py:110
  71.8 0.5 collective-permute-start.29
  72.5 1.5 collective-permute-start.19
  74.0 0.8 collective-permute-start.22
  74.9 0.5 collective-permute-start.28
  75.4 0.1 collective-permute-start.30
  75.5 8.4 %collective-permute-done.19.refs_12_ = bf16[64,3072]{1,0:T(8,128)(2,1)S(1)} collective-permute-done((bf16[64,3072]{1,0:T(8,128)(2,1)S(1)}, bf16[64,3072]{1,0:T(8,128)(2,1)S(1)}, u32[]{:S(2)}, u32[]{:S(2)}) %collective-permute-start.19) | collective-permute-done | bytes 393248 | tf_op jit(solution)/shard_map/ppermute | solution.py:302
  83.9 1.3 collective-permute-done.22.refs_13_
  85.2 1.5 collective-permute-start.23
  86.7 1.6 collective-permute-start.24
  88.3 0.2 collective-permute-start.35
  88.5 1.1 collective-permute-start.36
  89.7 1.0 collective-permute-start.37
  90.7 15.5 %ladder.3 = (bf16[1200,128]{1,0:T(8,128)(2,1)}, bf16[1200,128]{1,0:T(8,128)(2,1)}, bf16[1200,128]{1,0:T(8,128)(2,1)}, bf16[1200,128]{1,0:T(8,128)(2,1)}, bf16[12...) custom-call(bf16[64,3072]{1,0:T(8,128)(2,1)} %copy-done.7, ...), custom_call_target="tpu_custom_call" | custom-call | flops 7549747200 | bytes 21037056 | tf_op jit(solution)/shard_map/ladder/pallas_call | solution.py:110
  106.3 0.1 collective-permute-start.33
  106.4 1.2 collective-permute-start.34
  107.6 0.5 collective-permute-done.35.refs_3_
  108.1 1.0 collective-permute-done.36.refs_4_
  109.1 6.5 %collective-permute-done.37.refs_5_ = bf16[1200,128]{1,0:T(8,128)(2,1)S(1)} collective-permute-done((bf16[1200,128]{1,0:T(8,128)(2,1)}, bf16[1200,128]{1,0:T(8,128)(2,1)S(1)}, u32[]{:S(2)}, u32[]{:S(2)}) %collective-permute-start.37) | collective-permute-done | bytes 307232 | tf_op jit(solution)/shard_map/ppermute | solution.py:302
  115.7 0.4 collective-permute-done.34.refs_2_
  116.1 0.7 collective-permute-start.38
  116.8 1.5 collective-permute-start.39
  118.3 1.3 collective-permute-start.42
  119.6 0.6 collective-permute-start.43
  120.2 0.7 collective-permute-start.44
  120.9 13.0 %symmetrize.2 = (bf16[64,9600]{1,0:T(8,128)(2,1)S(1)}, bf16[32,9600]{1,0:T(8,128)(2,1)S(1)}) custom-call(s32[2]{0:T(128)S(1)} %pad_add_fusion.where_ref, s32[9600]{0:T(1024)S(1)} %copy-done.1, bf16[1200,128]{1,0:T(8,128)(2,1)S(1)} %copy-done.6, bf16[1200,128]{1,0:T(8,128)(2,1)S(1)} %collective-permute-done.33.refs_1_, ...), custom_call_target="tpu_custom_call" | custom-call | flops 855859200 | bytes 19660800 | tf_op jit(solution)/shard_map/symmetrize/pallas_call | solution.py:202
  133.9 0.9 collective-permute-start.40
  134.9 0.8 collective-permute-start.41
  135.7 3.9 %collective-permute-done.42.refs_3_ = bf16[1200,128]{1,0:T(8,128)(2,1)S(1)} collective-permute-done((bf16[1200,128]{1,0:T(8,128)(2,1)}, bf16[1200,128]{1,0:T(8,128)(2,1)S(1)}, u32[]{:S(2)}, u32[]{:S(2)}) %collective-permute-start.42) | collective-permute-done | bytes 307232 | tf_op jit(solution)/shard_map/ppermute | solution.py:302
  139.6 5.8 %collective-permute-start.46 = (bf16[32,9600]{1,0:T(8,128)(2,1)S(1)}, bf16[32,9600]{1,0:T(8,128)(2,1)S(1)}, u32[]{:S(2)}, u32[]{:S(2)}) collective-permute-start(bf16[32,9600]{1,0:T(8,128)(2,1)S(1)} %get-tuple-element.95), channel_id=1, source_target_pairs={{0,2},{1,3},{2,0},{3,1},{4,6},{5,7},{6,4},{7,5},{8,10},{9,11},{10,... | collective-permute-start | bytes 1843208 | tf_op jit(solution)/shard_map/ppermute | solution.py:302
  145.5 0.8 collective-permute-done.44.refs_5_
  146.3 12.9 %symmetrize.3 = (bf16[32,9600]{1,0:T(8,128)(2,1)S(1)}, bf16[32,9600]{1,0:T(8,128)(2,1)S(1)}) custom-call(s32[2]{0:T(128)S(1)} %pad_add_fusion.where_ref, s32[9600]{0:T(1024)S(1)} %copy-done.1, bf16[1200,128]{1,0:T(8,128)(2,1)S(1)} %copy-done.5, bf16[1200,128]{1,0:T(8,128)(2,1)S(1)} %collective-permute-done.40.refs_1_, ...), custom_call_target="tpu_custom_call" | custom-call | flops 698572800 | bytes 19660800 | tf_op jit(solution)/shard_map/symmetrize/pallas_call | solution.py:202
  159.3 5.4 %collective-permute-start.45 = (bf16[32,9600]{1,0:T(8,128)(2,1)S(1)}, bf16[32,9600]{1,0:T(8,128)(2,1)S(1)}, u32[]{:S(2)}, u32[]{:S(2)}) collective-permute-start(bf16[32,9600]{1,0:T(8,128)(2,1)S(1)} %get-tuple-element.94), channel_id=1, source_target_pairs={{0,1},{1,0},{2,3},{3,2},{4,5},{5,4},{6,7},{7,6},{8,9},{9,8},{10,11... | collective-permute-start | bytes 1843208 | tf_op jit(solution)/shard_map/ppermute | solution.py:302
  164.7 1.5 collective-permute-start.47
  166.2 7.2 %collective-permute-done.46.refs_2_ = bf16[32,9600]{1,0:T(8,128)(2,1)S(1)} collective-permute-done((bf16[32,9600]{1,0:T(8,128)(2,1)S(1)}, bf16[32,9600]{1,0:T(8,128)(2,1)S(1)}, u32[]{:S(2)}, u32[]{:S(2)}) %collective-permute-start.46) | collective-permute-done | bytes 614432 | tf_op jit(solution)/shard_map/ppermute | solution.py:302
  173.4 25.4 %collective-permute-done.45.refs_1_ = bf16[32,9600]{1,0:T(8,128)(2,1)S(1)} collective-permute-done((bf16[32,9600]{1,0:T(8,128)(2,1)S(1)}, bf16[32,9600]{1,0:T(8,128)(2,1)S(1)}, u32[]{:S(2)}, u32[]{:S(2)}) %collective-permute-start.45) | collective-permute-done | bytes 614432 | tf_op jit(solution)/shard_map/ppermute | solution.py:302
  198.7 15.9 %finish.1 = bf16[128,9600]{1,0:T(8,128)(2,1)} custom-call(s32[2]{0:T(128)S(1)} %pad_add_fusion.where_ref, s32[9600]{0:T(1024)S(1)} %copy-done.1, s32[1,128]{1,0:T(1,128)S(1)} %get-tuple-element.51.slot_ref, bf16[64,9600]{1,0:T(8,128)(2,1)S(1)} %get-tuple-element.79.refs_0_, bf16[32,9600]{1,0:T(8,128)(2,1)S(1)} %collective-permute-done.45.refs_1_, ...), custom_call_target="tpu_custom_call" | custom-call | flops 1013145600 | bytes 9830400 | tf_op jit(solution)/shard_map/finish/pallas_call | solution.py:279
  (121 shorter events, 0.7 us)
Async XLA Ops:
  3.7 52.4 %copy-start.4 = (bf16[64,3072]{1,0:T(8,128)(2,1)}, bf16[64,3072]{1,0:T(8,128)(2,1)S(1)}, u32[]{:S(2)}) copy-start(bf16[64,3072]{1,0:T(8,128)(2,1)S(1)} %get-tuple-element.52.refs_0_) | copy-start | bytes 1179652
  3.7 21.7 %collective-permute-start = (bf16[64,3072]{1,0:T(8,128)(2,1)S(1)}, bf16[64,3072]{1,0:T(8,128)(2,1)S(1)}, u32[]{:S(2)}, u32[]{:S(2)}) collective-permute-start(bf16[64,3072]{1,0:T(8,128)(2,1)S(1)} %get-tuple-element.53), channel_id=1, source_target_pairs={{0,2},{1,3},{2,0},{3,1},{4,6},{5,7},{6,4},{7,5},{8,10},{9,11},{10,... | collective-permute-start | bytes 1179656 | tf_op jit(solution)/shard_map/ppermute | solution.py:302
  7.8 21.1 %collective-permute-start.1 = (bf16[64,3072]{1,0:T(8,128)(2,1)S(1)}, bf16[64,3072]{1,0:T(8,128)(2,1)S(1)}, u32[]{:S(2)}, u32[]{:S(2)}) collective-permute-start(bf16[64,3072]{1,0:T(8,128)(2,1)S(1)} %get-tuple-element.54), channel_id=1, source_target_pairs={{0,1},{1,0},{2,3},{3,2},{4,5},{5,4},{6,7},{7,6},{8,9},{9,8},{10,11... | collective-permute-start | bytes 1179656 | tf_op jit(solution)/shard_map/ppermute | solution.py:302
  9.4 19.5 %collective-permute-start.4 = (bf16[64,3072]{1,0:T(8,128)(2,1)S(1)}, bf16[64,3072]{1,0:T(8,128)(2,1)S(1)}, u32[]{:S(2)}, u32[]{:S(2)}) collective-permute-start(bf16[64,3072]{1,0:T(8,128)(2,1)S(1)} %get-tuple-element.52.refs_0_), channel_id=1, source_target_pairs={{0,24},{4,28},{8,16},{12,20},{16,8},{20,12},{24,0},{28,4},{1,25},{... | collective-permute-start | bytes 1179656 | tf_op jit(solution)/shard_map/ppermute | solution.py:302
  11.9 17.2 %collective-permute-start.3 = (bf16[64,3072]{1,0:T(8,128)(2,1)S(1)}, bf16[64,3072]{1,0:T(8,128)(2,1)S(1)}, u32[]{:S(2)}, u32[]{:S(2)}) collective-permute-start(bf16[64,3072]{1,0:T(8,128)(2,1)S(1)} %get-tuple-element.52.refs_0_), channel_id=1, source_target_pairs={{0,16},{4,20},{8,24},{12,28},{16,0},{20,4},{24,8},{28,12},{1,17},{... | collective-permute-start | bytes 1179656 | tf_op jit(solution)/shard_map/ppermute | solution.py:302
  12.4 16.8 %collective-permute-start.2 = (bf16[64,3072]{1,0:T(8,128)(2,1)S(1)}, bf16[64,3072]{1,0:T(8,128)(2,1)S(1)}, u32[]{:S(2)}, u32[]{:S(2)}) collective-permute-start(bf16[64,3072]{1,0:T(8,128)(2,1)S(1)} %get-tuple-element.52.refs_0_), channel_id=1, source_target_pairs={{0,8},{4,12},{8,0},{12,4},{16,24},{20,28},{24,16},{28,20},{1,9},{5... | collective-permute-start | bytes 1179656 | tf_op jit(solution)/shard_map/ppermute | solution.py:302
  25.5 30.6 %copy-start.12 = (bf16[64,3072]{1,0:T(8,128)(2,1)}, bf16[64,3072]{1,0:T(8,128)(2,1)S(1)}, u32[]{:S(2)}) copy-start(bf16[64,3072]{1,0:T(8,128)(2,1)S(1)} %collective-permute-done.refs_1_) | copy-start | bytes 1179652
  25.5 12.8 %collective-permute-start.14 = (bf16[64,3072]{1,0:T(8,128)(2,1)S(1)}, bf16[64,3072]{1,0:T(8,128)(2,1)S(1)}, u32[]{:S(2)}, u32[]{:S(2)}) collective-permute-start(bf16[64,3072]{1,0:T(8,128)(2,1)S(1)} %get-tuple-element.57), channel_id=1, source_target_pairs={{0,3},{1,2},{2,1},{3,0},{4,7},{5,6},{6,5},{7,4},{8,11},{9,10},{10,... | collective-permute-start | bytes 1179656 | tf_op jit(solution)/shard_map/ppermute | solution.py:302
  28.9 42.8 %copy-start.7 = (bf16[64,3072]{1,0:T(8,128)(2,1)}, bf16[64,3072]{1,0:T(8,128)(2,1)S(1)}, u32[]{:S(2)}) copy-start(bf16[64,3072]{1,0:T(8,128)(2,1)S(1)} %collective-permute-done.1.refs_0_) | copy-start | bytes 1179652
  28.9 27.2 %copy-start.14 = (bf16[64,3072]{1,0:T(8,128)(2,1)}, bf16[64,3072]{1,0:T(8,128)(2,1)S(1)}, u32[]{:S(2)}) copy-start(bf16[64,3072]{1,0:T(8,128)(2,1)S(1)} %collective-permute-done.4.refs_12_) | copy-start | bytes 1179652
  29.0 27.1 %copy-start.15 = (bf16[64,3072]{1,0:T(8,128)(2,1)}, bf16[64,3072]{1,0:T(8,128)(2,1)S(1)}, u32[]{:S(2)}) copy-start(bf16[64,3072]{1,0:T(8,128)(2,1)S(1)} %collective-permute-done.3.refs_8_) | copy-start | bytes 1179652
  29.1 27.0 %copy-start.16 = (bf16[64,3072]{1,0:T(8,128)(2,1)}, bf16[64,3072]{1,0:T(8,128)(2,1)S(1)}, u32[]{:S(2)}) copy-start(bf16[64,3072]{1,0:T(8,128)(2,1)S(1)} %collective-permute-done.2.refs_4_) | copy-start | bytes 1179652
  29.1 12.0 %collective-permute-start.13 = (bf16[64,3072]{1,0:T(8,128)(2,1)S(1)}, bf16[64,3072]{1,0:T(8,128)(2,1)S(1)}, u32[]{:S(2)}, u32[]{:S(2)}) collective-permute-start(bf16[64,3072]{1,0:T(8,128)(2,1)S(1)} %collective-permute-done.refs_1_), channel_id=1, source_target_pairs={{0,24},{4,28},{8,16},{12,20},{16,8},{20,12},{24,0},{28,4},{1,25},{... | collective-permute-start | bytes 1179656 | tf_op jit(solution)/shard_map/ppermute | solution.py:302
  31.5 11.1 %collective-permute-start.5 = (bf16[64,3072]{1,0:T(8,128)(2,1)S(1)}, bf16[64,3072]{1,0:T(8,128)(2,1)S(1)}, u32[]{:S(2)}, u32[]{:S(2)}) collective-permute-start(bf16[64,3072]{1,0:T(8,128)(2,1)S(1)} %get-tuple-element.52.refs_0_), channel_id=1, source_target_pairs={{0,4},{4,0},{8,12},{12,8},{16,20},{20,16},{24,28},{28,24},{1,5},{5... | collective-permute-start | bytes 1179656 | tf_op jit(solution)/shard_map/ppermute | solution.py:302
  31.5 11.2 %collective-permute-start.15 = (bf16[64,3072]{1,0:T(8,128)(2,1)S(1)}, bf16[64,3072]{1,0:T(8,128)(2,1)S(1)}, u32[]{:S(2)}, u32[]{:S(2)}) collective-permute-start(bf16[64,3072]{1,0:T(8,128)(2,1)S(1)} %collective-permute-done.4.refs_12_), channel_id=1, source_target_pairs={{0,4},{4,0},{8,12},{12,8},{16,20},{20,16},{24,28},{28,24},{1,5},{5... | collective-permute-start | bytes 1179656 | tf_op jit(solution)/shard_map/ppermute | solution.py:302
  32.0 11.2 %collective-permute-start.11 = (bf16[64,3072]{1,0:T(8,128)(2,1)S(1)}, bf16[64,3072]{1,0:T(8,128)(2,1)S(1)}, u32[]{:S(2)}, u32[]{:S(2)}) collective-permute-start(bf16[64,3072]{1,0:T(8,128)(2,1)S(1)} %collective-permute-done.3.refs_8_), channel_id=1, source_target_pairs={{0,4},{4,0},{8,12},{12,8},{16,20},{20,16},{24,28},{28,24},{1,5},{5... | collective-permute-start | bytes 1179656 | tf_op jit(solution)/shard_map/ppermute | solution.py:302
  38.3 36.5 %copy-start.8 = (bf16[64,3072]{1,0:T(8,128)(2,1)}, bf16[64,3072]{1,0:T(8,128)(2,1)S(1)}, u32[]{:S(2)}) copy-start(bf16[64,3072]{1,0:T(8,128)(2,1)S(1)} %collective-permute-done.14.refs_1_) | copy-start | bytes 1179652
  38.3 11.1 %collective-permute-start.10 = (bf16[64,3072]{1,0:T(8,128)(2,1)S(1)}, bf16[64,3072]{1,0:T(8,128)(2,1)S(1)}, u32[]{:S(2)}, u32[]{:S(2)}) collective-permute-start(bf16[64,3072]{1,0:T(8,128)(2,1)S(1)} %collective-permute-done.refs_1_), channel_id=1, source_target_pairs={{0,16},{4,20},{8,24},{12,28},{16,0},{20,4},{24,8},{28,12},{1,17},{... | collective-permute-start | bytes 1179656 | tf_op jit(solution)/shard_map/ppermute | solution.py:302
  41.2 10.0 %collective-permute-start.7 = (bf16[64,3072]{1,0:T(8,128)(2,1)S(1)}, bf16[64,3072]{1,0:T(8,128)(2,1)S(1)}, u32[]{:S(2)}, u32[]{:S(2)}) collective-permute-start(bf16[64,3072]{1,0:T(8,128)(2,1)S(1)} %collective-permute-done.refs_1_), channel_id=1, source_target_pairs={{0,8},{4,12},{8,0},{12,4},{16,24},{20,28},{24,16},{28,20},{1,9},{5... | collective-permute-start | bytes 1179656 | tf_op jit(solution)/shard_map/ppermute | solution.py:302
  42.7 8.6 %collective-permute-start.6 = (bf16[64,3072]{1,0:T(8,128)(2,1)S(1)}, bf16[64,3072]{1,0:T(8,128)(2,1)S(1)}, u32[]{:S(2)}, u32[]{:S(2)}) collective-permute-start(bf16[64,3072]{1,0:T(8,128)(2,1)S(1)} %collective-permute-done.refs_1_), channel_id=1, source_target_pairs={{0,4},{4,0},{8,12},{12,8},{16,20},{20,16},{24,28},{28,24},{1,5},{5... | collective-permute-start | bytes 1179656 | tf_op jit(solution)/shard_map/ppermute | solution.py:302
  42.7 10.2 %collective-permute-start.8 = (bf16[64,3072]{1,0:T(8,128)(2,1)S(1)}, bf16[64,3072]{1,0:T(8,128)(2,1)S(1)}, u32[]{:S(2)}, u32[]{:S(2)}) collective-permute-start(bf16[64,3072]{1,0:T(8,128)(2,1)S(1)} %collective-permute-done.2.refs_4_), channel_id=1, source_target_pairs={{0,4},{4,0},{8,12},{12,8},{16,20},{20,16},{24,28},{28,24},{1,5},{5... | collective-permute-start | bytes 1179656 | tf_op jit(solution)/shard_map/ppermute | solution.py:302
  43.2 10.5 %collective-permute-start.16 = (bf16[64,3072]{1,0:T(8,128)(2,1)S(1)}, bf16[64,3072]{1,0:T(8,128)(2,1)S(1)}, u32[]{:S(2)}, u32[]{:S(2)}) collective-permute-start(bf16[64,3072]{1,0:T(8,128)(2,1)S(1)} %collective-permute-done.13.refs_13_), channel_id=1, source_target_pairs={{0,4},{4,0},{8,12},{12,8},{16,20},{20,16},{24,28},{28,24},{1,5},{5... | collective-permute-start | bytes 1179656 | tf_op jit(solution)/shard_map/ppermute | solution.py:302
  49.5 5.4 %collective-permute-start.12 = (bf16[64,3072]{1,0:T(8,128)(2,1)S(1)}, bf16[64,3072]{1,0:T(8,128)(2,1)}, u32[]{:S(2)}, u32[]{:S(2)}) collective-permute-start(bf16[64,3072]{1,0:T(8,128)(2,1)S(1)} %collective-permute-done.10.refs_9_), channel_id=1, source_target_pairs={{0,4},{4,0},{8,12},{12,8},{16,20},{20,16},{24,28},{28,24},{1,5},{5... | collective-permute-start | bytes 1179656 | tf_op jit(solution)/shard_map/ppermute | solution.py:302
  51.2 4.2 %collective-permute-start.9 = (bf16[64,3072]{1,0:T(8,128)(2,1)S(1)}, bf16[64,3072]{1,0:T(8,128)(2,1)S(1)}, u32[]{:S(2)}, u32[]{:S(2)}) collective-permute-start(bf16[64,3072]{1,0:T(8,128)(2,1)S(1)} %collective-permute-done.7.refs_5_), channel_id=1, source_target_pairs={{0,4},{4,0},{8,12},{12,8},{16,20},{20,16},{24,28},{28,24},{1,5},{5... | collective-permute-start | bytes 1179656 | tf_op jit(solution)/shard_map/ppermute | solution.py:302
  51.2 20.5 %collective-permute-start.18 = (bf16[64,3072]{1,0:T(8,128)(2,1)S(1)}, bf16[64,3072]{1,0:T(8,128)(2,1)S(1)}, u32[]{:S(2)}, u32[]{:S(2)}) collective-permute-start(bf16[64,3072]{1,0:T(8,128)(2,1)S(1)} %collective-permute-done.1.refs_0_), channel_id=1, source_target_pairs={{0,16},{4,20},{8,24},{12,28},{16,0},{20,4},{24,8},{28,12},{1,17},{... | collective-permute-start | bytes 1179656 | tf_op jit(solution)/shard_map/ppermute | solution.py:302
  52.9 18.9 %collective-permute-start.17 = (bf16[64,3072]{1,0:T(8,128)(2,1)S(1)}, bf16[64,3072]{1,0:T(8,128)(2,1)S(1)}, u32[]{:S(2)}, u32[]{:S(2)}) collective-permute-start(bf16[64,3072]{1,0:T(8,128)(2,1)S(1)} %collective-permute-done.1.refs_0_), channel_id=1, source_target_pairs={{0,8},{4,12},{8,0},{12,4},{16,24},{20,28},{24,16},{28,20},{1,9},{5... | collective-permute-start | bytes 1179656 | tf_op jit(solution)/shard_map/ppermute | solution.py:302
  53.7 18.8 %collective-permute-start.21 = (bf16[64,3072]{1,0:T(8,128)(2,1)S(1)}, bf16[64,3072]{1,0:T(8,128)(2,1)S(1)}, u32[]{:S(2)}, u32[]{:S(2)}) collective-permute-start(bf16[64,3072]{1,0:T(8,128)(2,1)S(1)} %collective-permute-done.14.refs_1_), channel_id=1, source_target_pairs={{0,8},{4,12},{8,0},{12,4},{16,24},{20,28},{24,16},{28,20},{1,9},{5... | collective-permute-start | bytes 1179656 | tf_op jit(solution)/shard_map/ppermute | solution.py:302
  54.9 19.1 %collective-permute-start.20 = (bf16[64,3072]{1,0:T(8,128)(2,1)S(1)}, bf16[64,3072]{1,0:T(8,128)(2,1)S(1)}, u32[]{:S(2)}, u32[]{:S(2)}) collective-permute-start(bf16[64,3072]{1,0:T(8,128)(2,1)S(1)} %collective-permute-done.14.refs_1_), channel_id=1, source_target_pairs={{0,16},{4,20},{8,24},{12,28},{16,0},{20,4},{24,8},{28,12},{1,17},{... | collective-permute-start | bytes 1179656 | tf_op jit(solution)/shard_map/ppermute | solution.py:302
  71.7 18.9 %copy-start.9 = (bf16[64,3072]{1,0:T(8,128)(2,1)}, bf16[64,3072]{1,0:T(8,128)(2,1)S(1)}, u32[]{:S(2)}) copy-start(bf16[64,3072]{1,0:T(8,128)(2,1)S(1)} %collective-permute-done.18.refs_8_) | copy-start | bytes 1179652
  71.7 18.9 %copy-start.10 = (bf16[64,3072]{1,0:T(8,128)(2,1)}, bf16[64,3072]{1,0:T(8,128)(2,1)S(1)}, u32[]{:S(2)}) copy-start(bf16[64,3072]{1,0:T(8,128)(2,1)S(1)} %collective-permute-done.17.refs_4_) | copy-start | bytes 1179652
  71.7 3.1 %collective-permute-start.25 = (bf16[64,3072]{1,0:T(8,128)(2,1)S(1)}, bf16[64,3072]{1,0:T(8,128)(2,1)S(1)}, u32[]{:S(2)}, u32[]{:S(2)}) collective-permute-start(bf16[64,3072]{1,0:T(8,128)(2,1)S(1)} %collective-permute-done.1.refs_0_), channel_id=1, source_target_pairs={{0,4},{4,0},{8,12},{12,8},{16,20},{20,16},{24,28},{28,24},{1,5},{5... | collective-permute-start | bytes 1179656 | tf_op jit(solution)/shard_map/ppermute | solution.py:302
  71.8 3.1 %collective-permute-start.29 = (bf16[64,3072]{1,0:T(8,128)(2,1)S(1)}, bf16[64,3072]{1,0:T(8,128)(2,1)S(1)}, u32[]{:S(2)}, u32[]{:S(2)}) collective-permute-start(bf16[64,3072]{1,0:T(8,128)(2,1)S(1)} %collective-permute-done.18.refs_8_), channel_id=1, source_target_pairs={{0,4},{4,0},{8,12},{12,8},{16,20},{20,16},{24,28},{28,24},{1,5},{5... | collective-permute-start | bytes 1179656 | tf_op jit(solution)/shard_map/ppermute | solution.py:302
  72.3 3.1 %collective-permute-start.27 = (bf16[64,3072]{1,0:T(8,128)(2,1)S(1)}, bf16[64,3072]{1,0:T(8,128)(2,1)S(1)}, u32[]{:S(2)}, u32[]{:S(2)}) collective-permute-start(bf16[64,3072]{1,0:T(8,128)(2,1)S(1)} %collective-permute-done.17.refs_4_), channel_id=1, source_target_pairs={{0,4},{4,0},{8,12},{12,8},{16,20},{20,16},{24,28},{28,24},{1,5},{5... | collective-permute-start | bytes 1179656 | tf_op jit(solution)/shard_map/ppermute | solution.py:302
  72.5 11.4 %collective-permute-start.19 = (bf16[64,3072]{1,0:T(8,128)(2,1)S(1)}, bf16[64,3072]{1,0:T(8,128)(2,1)S(1)}, u32[]{:S(2)}, u32[]{:S(2)}) collective-permute-start(bf16[64,3072]{1,0:T(8,128)(2,1)S(1)} %collective-permute-done.17.refs_4_), channel_id=1, source_target_pairs={{0,16},{4,20},{8,24},{12,28},{16,0},{20,4},{24,8},{28,12},{1,17},{... | collective-permute-start | bytes 1179656 | tf_op jit(solution)/shard_map/ppermute | solution.py:302
  74.0 11.2 %collective-permute-start.22 = (bf16[64,3072]{1,0:T(8,128)(2,1)S(1)}, bf16[64,3072]{1,0:T(8,128)(2,1)S(1)}, u32[]{:S(2)}, u32[]{:S(2)}) collective-permute-start(bf16[64,3072]{1,0:T(8,128)(2,1)S(1)} %collective-permute-done.20.refs_9_), channel_id=1, source_target_pairs={{0,8},{4,12},{8,0},{12,4},{16,24},{20,28},{24,16},{28,20},{1,9},{5... | collective-permute-start | bytes 1179656 | tf_op jit(solution)/shard_map/ppermute | solution.py:302
  74.8 10.4 %collective-permute-start.26 = (bf16[64,3072]{1,0:T(8,128)(2,1)S(1)}, bf16[64,3072]{1,0:T(8,128)(2,1)S(1)}, u32[]{:S(2)}, u32[]{:S(2)}) collective-permute-start(bf16[64,3072]{1,0:T(8,128)(2,1)S(1)} %collective-permute-done.14.refs_1_), channel_id=1, source_target_pairs={{0,4},{4,0},{8,12},{12,8},{16,20},{20,16},{24,28},{28,24},{1,5},{5... | collective-permute-start | bytes 1179656 | tf_op jit(solution)/shard_map/ppermute | solution.py:302
  74.9 11.8 %collective-permute-start.28 = (bf16[64,3072]{1,0:T(8,128)(2,1)S(1)}, bf16[64,3072]{1,0:T(8,128)(2,1)S(1)}, u32[]{:S(2)}, u32[]{:S(2)}) collective-permute-start(bf16[64,3072]{1,0:T(8,128)(2,1)S(1)} %collective-permute-done.21.refs_5_), channel_id=1, source_target_pairs={{0,4},{4,0},{8,12},{12,8},{16,20},{20,16},{24,28},{28,24},{1,5},{5... | collective-permute-start | bytes 1179656 | tf_op jit(solution)/shard_map/ppermute | solution.py:302
  75.4 12.9 %collective-permute-start.30 = (bf16[64,3072]{1,0:T(8,128)(2,1)S(1)}, bf16[64,3072]{1,0:T(8,128)(2,1)S(1)}, u32[]{:S(2)}, u32[]{:S(2)}) collective-permute-start(bf16[64,3072]{1,0:T(8,128)(2,1)S(1)} %collective-permute-done.20.refs_9_), channel_id=1, source_target_pairs={{0,4},{4,0},{8,12},{12,8},{16,20},{20,16},{24,28},{28,24},{1,5},{5... | collective-permute-start | bytes 1179656 | tf_op jit(solution)/shard_map/ppermute | solution.py:302
  83.9 4.7 %collective-permute-start.31 = (bf16[64,3072]{1,0:T(8,128)(2,1)S(1)}, bf16[64,3072]{1,0:T(8,128)(2,1)S(1)}, u32[]{:S(2)}, u32[]{:S(2)}) collective-permute-start(bf16[64,3072]{1,0:T(8,128)(2,1)S(1)} %collective-permute-done.19.refs_12_), channel_id=1, source_target_pairs={{0,4},{4,0},{8,12},{12,8},{16,20},{20,16},{24,28},{28,24},{1,5},{5... | collective-permute-start | bytes 1179656 | tf_op jit(solution)/shard_map/ppermute | solution.py:302
  85.2 4.5 %collective-permute-start.32 = (bf16[64,3072]{1,0:T(8,128)(2,1)S(1)}, bf16[64,3072]{1,0:T(8,128)(2,1)S(1)}, u32[]{:S(2)}, u32[]{:S(2)}) collective-permute-start(bf16[64,3072]{1,0:T(8,128)(2,1)S(1)} %collective-permute-done.22.refs_13_), channel_id=1, source_target_pairs={{0,4},{4,0},{8,12},{12,8},{16,20},{20,16},{24,28},{28,24},{1,5},{5... | collective-permute-start | bytes 1179656 | tf_op jit(solution)/shard_map/ppermute | solution.py:302
  85.2 21.1 %collective-permute-start.23 = (bf16[1200,128]{1,0:T(8,128)(2,1)}, bf16[1200,128]{1,0:T(8,128)(2,1)S(1)}, u32[]{:S(2)}, u32[]{:S(2)}) collective-permute-start(bf16[1200,128]{1,0:T(8,128)(2,1)} %get-tuple-element.63), channel_id=1, source_target_pairs={{0,28},{4,24},{8,20},{12,16},{16,12},{20,8},{24,4},{28,0},{1,29},{... | collective-permute-start | bytes 921608 | tf_op jit(solution)/shard_map/ppermute | solution.py:302
  86.7 19.6 %copy-start.38 = (bf16[1200,128]{1,0:T(8,128)(2,1)S(1)}, bf16[1200,128]{1,0:T(8,128)(2,1)}, u32[]{:S(2)}) copy-start(bf16[1200,128]{1,0:T(8,128)(2,1)} %get-tuple-element.70) | copy-start | bytes 921604
  86.7 19.8 %copy-start.37 = (bf16[1200,128]{1,0:T(8,128)(2,1)S(1)}, bf16[1200,128]{1,0:T(8,128)(2,1)}, u32[]{:S(2)}) copy-start(bf16[1200,128]{1,0:T(8,128)(2,1)} %get-tuple-element.72) | copy-start | bytes 921604
  86.7 34.2 %copy-start.1 = (s32[9600]{0:T(1024)S(1)}, s32[9600]{0:T(1024)}, u32[]{:S(2)}) copy-start(s32[9600]{0:T(1024)} %mirror_ref.5) | copy-start | bytes 115204
  86.7 34.2 %copy-start.6 = (bf16[1200,128]{1,0:T(8,128)(2,1)S(1)}, bf16[1200,128]{1,0:T(8,128)(2,1)}, u32[]{:S(2)}) copy-start(bf16[1200,128]{1,0:T(8,128)(2,1)} %get-tuple-element.59.refs_0_) | copy-start | bytes 921604
  86.7 19.6 %collective-permute-start.24 = (bf16[1200,128]{1,0:T(8,128)(2,1)}, bf16[1200,128]{1,0:T(8,128)(2,1)S(1)}, u32[]{:S(2)}, u32[]{:S(2)}) collective-permute-start(bf16[1200,128]{1,0:T(8,128)(2,1)} %get-tuple-element.64), channel_id=1, source_target_pairs={{0,24},{4,28},{8,16},{12,20},{16,8},{20,12},{24,0},{28,4},{1,25},{... | collective-permute-start | bytes 921608 | tf_op jit(solution)/shard_map/ppermute | solution.py:302
  88.3 19.8 %collective-permute-start.35 = (bf16[1200,128]{1,0:T(8,128)(2,1)}, bf16[1200,128]{1,0:T(8,128)(2,1)S(1)}, u32[]{:S(2)}, u32[]{:S(2)}) collective-permute-start(bf16[1200,128]{1,0:T(8,128)(2,1)} %get-tuple-element.74), channel_id=1, source_target_pairs={{0,12},{4,8},{8,4},{12,0},{16,28},{20,24},{24,20},{28,16},{1,13},{... | collective-permute-start | bytes 921608 | tf_op jit(solution)/shard_map/ppermute | solution.py:302
  88.5 20.6 %collective-permute-start.36 = (bf16[1200,128]{1,0:T(8,128)(2,1)}, bf16[1200,128]{1,0:T(8,128)(2,1)S(1)}, u32[]{:S(2)}, u32[]{:S(2)}) collective-permute-start(bf16[1200,128]{1,0:T(8,128)(2,1)} %get-tuple-element.76), channel_id=1, source_target_pairs={{0,16},{4,20},{8,24},{12,28},{16,0},{20,4},{24,8},{28,12},{1,17},{... | collective-permute-start | bytes 921608 | tf_op jit(solution)/shard_map/ppermute | solution.py:302
  89.7 26.0 %collective-permute-start.37 = (bf16[1200,128]{1,0:T(8,128)(2,1)}, bf16[1200,128]{1,0:T(8,128)(2,1)S(1)}, u32[]{:S(2)}, u32[]{:S(2)}) collective-permute-start(bf16[1200,128]{1,0:T(8,128)(2,1)} %get-tuple-element.78), channel_id=1, source_target_pairs={{0,20},{4,16},{8,28},{12,24},{16,4},{20,0},{24,12},{28,8},{1,21},{... | collective-permute-start | bytes 921608 | tf_op jit(solution)/shard_map/ppermute | solution.py:302
  106.2 27.7 %copy-start.40 = (bf16[1200,128]{1,0:T(8,128)(2,1)S(1)}, bf16[1200,128]{1,0:T(8,128)(2,1)}, u32[]{:S(2)}) copy-start(bf16[1200,128]{1,0:T(8,128)(2,1)} %get-tuple-element.85) | copy-start | bytes 921604
  106.2 28.6 %copy-start.39 = (bf16[1200,128]{1,0:T(8,128)(2,1)S(1)}, bf16[1200,128]{1,0:T(8,128)(2,1)}, u32[]{:S(2)}) copy-start(bf16[1200,128]{1,0:T(8,128)(2,1)} %get-tuple-element.87) | copy-start | bytes 921604
  106.2 40.1 %copy-start.5 = (bf16[1200,128]{1,0:T(8,128)(2,1)S(1)}, bf16[1200,128]{1,0:T(8,128)(2,1)}, u32[]{:S(2)}) copy-start(bf16[1200,128]{1,0:T(8,128)(2,1)} %get-tuple-element.69.refs_0_) | copy-start | bytes 921604
  106.3 9.4 %collective-permute-start.33 = (bf16[1200,128]{1,0:T(8,128)(2,1)S(1)}, bf16[1200,128]{1,0:T(8,128)(2,1)S(1)}, u32[]{:S(2)}, u32[]{:S(2)}) collective-permute-start(bf16[1200,128]{1,0:T(8,128)(2,1)S(1)} %copy-done.38), channel_id=1, source_target_pairs={{0,4},{4,0},{8,12},{12,8},{16,20},{20,16},{24,28},{28,24},{1,5},{5... | collective-permute-start | bytes 921608 | tf_op jit(solution)/shard_map/ppermute | solution.py:302
  106.4 9.6 %collective-permute-start.34 = (bf16[1200,128]{1,0:T(8,128)(2,1)S(1)}, bf16[1200,128]{1,0:T(8,128)(2,1)S(1)}, u32[]{:S(2)}, u32[]{:S(2)}) collective-permute-start(bf16[1200,128]{1,0:T(8,128)(2,1)S(1)} %copy-done.37), channel_id=1, source_target_pairs={{0,8},{4,12},{8,0},{12,4},{16,24},{20,28},{24,16},{28,20},{1,9},{5... | collective-permute-start | bytes 921608 | tf_op jit(solution)/shard_map/ppermute | solution.py:302
  116.1 17.8 %collective-permute-start.38 = (bf16[1200,128]{1,0:T(8,128)(2,1)}, bf16[1200,128]{1,0:T(8,128)(2,1)S(1)}, u32[]{:S(2)}, u32[]{:S(2)}) collective-permute-start(bf16[1200,128]{1,0:T(8,128)(2,1)} %get-tuple-element.82), channel_id=1, source_target_pairs={{0,28},{4,24},{8,20},{12,16},{16,12},{20,8},{24,4},{28,0},{1,29},{... | collective-permute-start | bytes 921608 | tf_op jit(solution)/shard_map/ppermute | solution.py:302
  116.8 17.1 %collective-permute-start.39 = (bf16[1200,128]{1,0:T(8,128)(2,1)}, bf16[1200,128]{1,0:T(8,128)(2,1)S(1)}, u32[]{:S(2)}, u32[]{:S(2)}) collective-permute-start(bf16[1200,128]{1,0:T(8,128)(2,1)} %get-tuple-element.84), channel_id=1, source_target_pairs={{0,24},{4,28},{8,16},{12,20},{16,8},{20,12},{24,0},{28,4},{1,25},{... | collective-permute-start | bytes 921608 | tf_op jit(solution)/shard_map/ppermute | solution.py:302
  118.3 21.3 %collective-permute-start.42 = (bf16[1200,128]{1,0:T(8,128)(2,1)}, bf16[1200,128]{1,0:T(8,128)(2,1)S(1)}, u32[]{:S(2)}, u32[]{:S(2)}) collective-permute-start(bf16[1200,128]{1,0:T(8,128)(2,1)} %get-tuple-element.89), channel_id=1, source_target_pairs={{0,12},{4,8},{8,4},{12,0},{16,28},{20,24},{24,20},{28,16},{1,13},{... | collective-permute-start | bytes 921608 | tf_op jit(solution)/shard_map/ppermute | solution.py:302
  119.6 25.8 %collective-permute-start.43 = (bf16[1200,128]{1,0:T(8,128)(2,1)}, bf16[1200,128]{1,0:T(8,128)(2,1)S(1)}, u32[]{:S(2)}, u32[]{:S(2)}) collective-permute-start(bf16[1200,128]{1,0:T(8,128)(2,1)} %get-tuple-element.91), channel_id=1, source_target_pairs={{0,16},{4,20},{8,24},{12,28},{16,0},{20,4},{24,8},{28,12},{1,17},{... | collective-permute-start | bytes 921608 | tf_op jit(solution)/shard_map/ppermute | solution.py:302
  120.2 26.1 %collective-permute-start.44 = (bf16[1200,128]{1,0:T(8,128)(2,1)}, bf16[1200,128]{1,0:T(8,128)(2,1)S(1)}, u32[]{:S(2)}, u32[]{:S(2)}) collective-permute-start(bf16[1200,128]{1,0:T(8,128)(2,1)} %get-tuple-element.93), channel_id=1, source_target_pairs={{0,20},{4,16},{8,28},{12,24},{16,4},{20,0},{24,12},{28,8},{1,21},{... | collective-permute-start | bytes 921608 | tf_op jit(solution)/shard_map/ppermute | solution.py:302
  133.9 12.4 %collective-permute-start.40 = (bf16[1200,128]{1,0:T(8,128)(2,1)S(1)}, bf16[1200,128]{1,0:T(8,128)(2,1)S(1)}, u32[]{:S(2)}, u32[]{:S(2)}) collective-permute-start(bf16[1200,128]{1,0:T(8,128)(2,1)S(1)} %copy-done.40), channel_id=1, source_target_pairs={{0,4},{4,0},{8,12},{12,8},{16,20},{20,16},{24,28},{28,24},{1,5},{5... | collective-permute-start | bytes 921608 | tf_op jit(solution)/shard_map/ppermute | solution.py:302
  134.9 11.5 %collective-permute-start.41 = (bf16[1200,128]{1,0:T(8,128)(2,1)S(1)}, bf16[1200,128]{1,0:T(8,128)(2,1)S(1)}, u32[]{:S(2)}, u32[]{:S(2)}) collective-permute-start(bf16[1200,128]{1,0:T(8,128)(2,1)S(1)} %copy-done.39), channel_id=1, source_target_pairs={{0,8},{4,12},{8,0},{12,4},{16,24},{20,28},{24,16},{28,20},{1,9},{5... | collective-permute-start | bytes 921608 | tf_op jit(solution)/shard_map/ppermute | solution.py:302
  139.6 33.8 %collective-permute-start.46 = (bf16[32,9600]{1,0:T(8,128)(2,1)S(1)}, bf16[32,9600]{1,0:T(8,128)(2,1)S(1)}, u32[]{:S(2)}, u32[]{:S(2)}) collective-permute-start(bf16[32,9600]{1,0:T(8,128)(2,1)S(1)} %get-tuple-element.95), channel_id=1, source_target_pairs={{0,2},{1,3},{2,0},{3,1},{4,6},{5,7},{6,4},{7,5},{8,10},{9,11},{10,... | collective-permute-start | bytes 1843208 | tf_op jit(solution)/shard_map/ppermute | solution.py:302
  159.3 39.5 %collective-permute-start.45 = (bf16[32,9600]{1,0:T(8,128)(2,1)S(1)}, bf16[32,9600]{1,0:T(8,128)(2,1)S(1)}, u32[]{:S(2)}, u32[]{:S(2)}) collective-permute-start(bf16[32,9600]{1,0:T(8,128)(2,1)S(1)} %get-tuple-element.94), channel_id=1, source_target_pairs={{0,1},{1,0},{2,3},{3,2},{4,5},{5,4},{6,7},{7,6},{8,9},{9,8},{10,11... | collective-permute-start | bytes 1843208 | tf_op jit(solution)/shard_map/ppermute | solution.py:302
  164.7 34.1 %collective-permute-start.47 = (bf16[32,9600]{1,0:T(8,128)(2,1)S(1)}, bf16[32,9600]{1,0:T(8,128)(2,1)S(1)}, u32[]{:S(2)}, u32[]{:S(2)}) collective-permute-start(bf16[32,9600]{1,0:T(8,128)(2,1)S(1)} %get-tuple-element.96), channel_id=1, source_target_pairs={{0,3},{1,2},{2,1},{3,0},{4,7},{5,6},{6,5},{7,4},{8,11},{9,10},{10,... | collective-permute-start | bytes 1843208 | tf_op jit(solution)/shard_map/ppermute | solution.py:302
  (25 other events, 190.1 us)

commit v3 on v2

v3 whole, which is shorter than its diff:
```python
import functools

import jax
import jax.numpy as jnp
from jax import lax
from jax.experimental import pallas as pl
from jax.experimental.pallas import tpu as pltpu
from jax.sharding import PartitionSpec as P

IRREPS = 8
F32, BF16, I32 = jnp.float32, jnp.bfloat16, jnp.int32
NN = (((1,), (0,)), ((), ()))
NT = (((1,), (1,)), ((), ()))
VMEM_LIMIT = 24 * 1024 * 1024
LADDER_LIMIT = 56 * 1024 * 1024
TILE = 128


def iota(shape, dim):
    return lax.broadcasted_iota(I32, shape, dim)


def params(limit=VMEM_LIMIT):
    return pltpu.CompilerParams(vmem_limit_bytes=limit)


def pack_kernel(cols, owned, half, where_ref, irreps_ref, mirror_ref, amp_ref, slot_ref, *out_refs):
    pairs = irreps_ref.shape[1]
    square = (pairs, pairs)
    irreps = jnp.broadcast_to(irreps_ref[...], square)
    mirror = jnp.broadcast_to(mirror_ref[...], square)
    irreps_t = irreps.astype(F32).T.astype(I32)
    mirror_t = mirror.astype(F32).T.astype(I32)
    down, across = iota(square, 0), iota(square, 1)
    first = jnp.minimum(across, mirror)
    counted = (mirror_t > down) & (irreps_t == irreps) & (down < first)
    rank = jnp.sum(counted.astype(I32), axis=0, keepdims=True)
    partner = (across[:1] != first[:1]).astype(I32)
    slot = irreps_ref[...] * (2 * half) + partner * half + rank
    slot_ref[...] = slot
    rows = owned * 2 * half
    amp = amp_ref[...]
    for k in range(cols):
        base = (where_ref[1] ^ k) * rows
        onehot = (slot == base + iota((rows, pairs), 0)).astype(F32).astype(BF16)
        out_refs[k][...] = lax.dot_general(onehot, amp, NN, preferred_element_type=F32).astype(BF16)


def pack(where, irreps, mirror, amplitudes, cols, owned, half):
    pairs, contract = amplitudes.shape
    rows = owned * 2 * half
    whole = lambda shape: pl.BlockSpec(shape, lambda i, w: (0, 0))
    out = pl.pallas_call(
        functools.partial(pack_kernel, cols, owned, half),
        grid_spec=pltpu.PrefetchScalarGridSpec(
            num_scalar_prefetch=1,
            grid=(1,),
            in_specs=[whole((1, pairs)), whole((1, pairs)), whole((pairs, contract))],
            out_specs=[whole((1, pairs))] + [whole((rows, contract))] * cols,
        ),
        out_shape=[jax.ShapeDtypeStruct((1, pairs), I32)]
        + [jax.ShapeDtypeStruct((rows, contract), BF16)] * cols,
        compiler_params=params(),
        cost_estimate=pl.CostEstimate(
            flops=2 * cols * rows * pairs * contract, bytes_accessed=3 * pairs * contract * 2, transcendentals=0
        ),
        name="pack",
    )(where, irreps, mirror, amplitudes)
    return out[0], out[1:]


def product_kernel(holders, chunk_count, owned, slots, places, array_count, *refs):
    arrays = refs[:array_count]
    integrals_ref, rows_ref, sem = refs[array_count], *refs[-2:]
    outs = refs[array_count + 1 : -2]
    group = chunk_count * slots

    @pl.when(pl.program_id(0) == 0)
    def _():
        copies = []
        for i in range(owned):
            for (o, j), (at, row) in places.items():
                n = len(copies)
                copies.append(
                    pltpu.make_async_copy(
                        arrays[at].at[pl.ds(row + i * slots, slots)],
                        rows_ref.at[i, pl.ds(o * group + j * slots, slots)],
                        sem.at[n],
                    )
                )
        for copy in copies:
            copy.start()
        for copy in copies:
            copy.wait()

    ladder = [
        lax.dot_general(integrals_ref[i], rows_ref[i], NT, preferred_element_type=F32) for i in range(owned)
    ]
    for o in range(holders):
        here = slice(o * group, (o + 1) * group)
        block = jnp.concatenate([ladder[i][:, here] for i in range(owned)], axis=1).astype(BF16)
        if len(outs) == 2:
            outs[o % 2][o // 2] = block
        else:
            outs[o][...] = block


def product(arrays, places, integrals, holders, chunk_count, slots, joined):
    owned, share, contract = integrals.shape
    tile = 240
    group = chunk_count * slots
    lanes = owned * group
    if joined:
        spec = pl.BlockSpec((holders // 2, tile, lanes), lambda s: (0, s, 0))
        out = jax.ShapeDtypeStruct((holders // 2, share, lanes), BF16)
    else:
        spec = pl.BlockSpec((tile, lanes), lambda s: (s, 0))
        out = jax.ShapeDtypeStruct((share, lanes), BF16)
    return pl.pallas_call(
        functools.partial(product_kernel, holders, chunk_count, owned, slots, places, len(arrays)),
        grid=(pl.cdiv(share, tile),),
        in_specs=[pl.BlockSpec(memory_space=pl.ANY)] * len(arrays)
        + [pl.BlockSpec((owned, tile, contract), lambda s: (0, s, 0))],
        out_specs=[spec] * (2 if joined else holders),
        out_shape=[out] * (2 if joined else holders),
        scratch_shapes=[
            pltpu.VMEM((owned, holders * group, contract), BF16),
            pltpu.SemaphoreType.DMA((holders * chunk_count * owned,)),
        ],
        compiler_params=params(LADDER_LIMIT),
        cost_estimate=pl.CostEstimate(
            flops=2 * owned * holders * group * contract * share,
            bytes_accessed=2 * owned * contract * (share + holders * group),
            transcendentals=0,
        ),
        name="ladder",
    )(*arrays, integrals)


def gather_rows(mirror_ref, base, source, target):
    rows = [source[pl.ds(mirror_ref[base + u], 1), :] for u in range(target.shape[0])]
    for u, row in enumerate(rows):
        target[u : u + 1, :] = row


def runs_of(slab):
    tiles = slab // TILE
    return next(n for n in (15, 5, 3, 4, 2, 1) if tiles % n == 0), 1


def symmetrize_kernel(places, array_count, chunks, owned, half, run, turns, where_ref, mirror_ref, *refs):
    holders = len(places)
    parts, refs = refs[:array_count], refs[array_count:]
    outs, refs = refs[: len(chunks)], refs[len(chunks) :]
    raw, wide, sem, *picked = refs
    share, lanes = raw.shape[1:]
    step = pl.program_id(0)

    @pl.when(step == 0)
    def _():
        copies = []
        for o in range(holders):
            at, index = places[o]
            part = parts[at] if index is None else parts[at].at[index]
            copies.append(pltpu.make_async_copy(part, raw.at[o], sem.at[o]))
        for copy in copies:
            copy.start()
        for o in range(holders):
            copies[o].wait()
            at = pl.multiple_of((where_ref[0] ^ o) * share, 8)
            wide[pl.ds(at, share), :] = raw[o].astype(F32)

    group = len(chunks) * 2 * half
    picks = []
    for j, k in enumerate(chunks):
        sides = 2 if k == 0 else 1
        shape = (outs[j].shape[0], lanes)
        row, lane = iota(shape, 0), iota(shape, 1)
        irrep, rest = row // (sides * half), row % (sides * half)
        side, rank = rest // half, rest % half
        start = irrep * group + j * 2 * half + rank
        mine = lane == start + side * half
        other = lane == start + (1 - side) * half
        picks.append(jnp.concatenate([mine.astype(F32), other.astype(F32)], axis=1))
    pick = jnp.concatenate(picks, axis=0).astype(BF16)

    def some(n, carry):
        for i in range(run):
            inside = pl.multiple_of((n * run + i) * TILE, TILE)
            base = step * (turns * run * TILE) + inside
            gather_rows(mirror_ref, base, wide, picked[i])
            here = wide[pl.ds(pl.multiple_of(base, TILE), TILE), :]
            both = jnp.concatenate([here, picked[i][...]], axis=1).astype(BF16)
            total = lax.dot_general(pick, both, NT, preferred_element_type=F32).astype(BF16)
            at = 0
            for out in outs:
                out[:, pl.ds(inside, TILE)] = total[at : at + out.shape[0]]
                at += out.shape[0]
        return carry

    lax.fori_loop(0, turns, some, 0)


def symmetrize(where, col_mirror, parts, places, chunks, owned, half):
    holders = len(places)
    share, lanes = parts[0].shape[-2:]
    slab = col_mirror.shape[0]
    run, turns = runs_of(slab)
    block = run * turns * TILE
    rows = [owned * half * (2 if k == 0 else 1) for k in chunks]
    return pl.pallas_call(
        functools.partial(symmetrize_kernel, places, len(parts), chunks, owned, half, run, turns),
        grid_spec=pltpu.PrefetchScalarGridSpec(
            num_scalar_prefetch=2,
            grid=(slab // block,),
            in_specs=[pl.BlockSpec(memory_space=pl.ANY)] * len(parts),
            out_specs=[pl.BlockSpec((n, block), lambda s, w, m: (0, s)) for n in rows],
            scratch_shapes=[
                pltpu.VMEM((holders, share, lanes), BF16),
                pltpu.VMEM((slab, lanes), F32),
                pltpu.SemaphoreType.DMA((holders,)),
            ]
            + [pltpu.VMEM((TILE, lanes), F32)] * run,
        ),
        out_shape=[jax.ShapeDtypeStruct((n, slab), BF16) for n in rows],
        compiler_params=params(),
        cost_estimate=pl.CostEstimate(
            flops=4 * sum(rows) * lanes * slab + 40000 * slab, bytes_accessed=16 * slab * lanes, transcendentals=0
        ),
        name="symmetrize",
    )(where, col_mirror, *parts)


def finish_kernel(cols, owned, half, run, turns, where_ref, mirror_ref, slot_ref, *refs):
    own_ref = refs[0]
    sums = refs[1:cols]
    out_ref, wide = refs[cols : cols + 2]
    picked = refs[cols + 2 :]
    step = pl.program_id(0)
    slab, lanes = wide.shape
    pairs = out_ref.shape[0]
    sent = owned * half
    used = (cols - 1) * sent
    block = run * turns * TILE

    @pl.when(step == 0)
    def _():
        def widen(n, carry):
            for i in range(run):
                at = pl.ds(pl.multiple_of((n * run + i) * TILE, TILE), TILE)
                rows = [s[:, at].astype(F32) for s in sums]
                if lanes > used:
                    rows.append(jnp.zeros((lanes - used, TILE), F32))
                wide[at, :] = jnp.concatenate(rows, axis=0).T
            return carry

        lax.fori_loop(0, slab // TILE // run, widen, 0)

    slot = jnp.broadcast_to(slot_ref[...], (pairs, pairs)).astype(F32).T.astype(I32)[:, :1]
    col = where_ref[1]
    own = own_ref.shape[0]
    onehots = [slot == col * own + iota((pairs, own), 1)]
    at = iota((pairs, used), 1)
    rest = at % sent
    first = (col ^ (at // sent + 1)) * own + (rest // half) * (2 * half) + rest % half
    onehots.append(slot == first)
    straight = jnp.concatenate([h.astype(F32) for h in onehots], axis=1).astype(BF16)
    second = [(slot == first + half).astype(F32)]
    if lanes > used:
        second.append(jnp.zeros((pairs, lanes - used), F32))
    crossed = jnp.concatenate(second, axis=1).astype(BF16)

    def some(n, carry):
        for i in range(run):
            inside = pl.multiple_of((n * run + i) * TILE, TILE)
            base = pl.multiple_of(step * block + inside, TILE)
            gather_rows(mirror_ref, base, wide, picked[i])
            rows = [own_ref[:, pl.ds(inside, TILE)]] + [s[:, pl.ds(base, TILE)] for s in sums]
            total = lax.dot_general(straight, jnp.concatenate(rows, axis=0), NN, preferred_element_type=F32)
            total += lax.dot_general(crossed, picked[i][...].astype(BF16), NT, preferred_element_type=F32)
            out_ref[:, pl.ds(inside, TILE)] = total.astype(BF16)
        return carry

    lax.fori_loop(0, turns, some, 0)


def finish(where, col_mirror, slot, own, sums, owned, half):
    cols = len(sums) + 1
    slab = col_mirror.shape[0]
    pairs = slot.shape[1]
    run, turns = runs_of(slab)
    block = run * turns * TILE
    lanes = pl.cdiv(len(sums) * owned * half, 128) * 128
    return pl.pallas_call(
        functools.partial(finish_kernel, cols, owned, half, run, turns),
        grid_spec=pltpu.PrefetchScalarGridSpec(
            num_scalar_prefetch=2,
            grid=(slab // block,),
            in_specs=[
                pl.BlockSpec((1, pairs), lambda s, w, m: (0, 0)),
                pl.BlockSpec((own.shape[0], block), lambda s, w, m: (0, s)),
            ]
            + [pl.BlockSpec((owned * half, slab), lambda s, w, m: (0, 0))] * len(sums),
            out_specs=pl.BlockSpec((pairs, block), lambda s, w, m: (0, s)),
            scratch_shapes=[pltpu.VMEM((slab, lanes), F32)] + [pltpu.VMEM((TILE, lanes), F32)] * run,
        ),
        out_shape=jax.ShapeDtypeStruct((pairs, slab), BF16),
        compiler_params=params(),
        cost_estimate=pl.CostEstimate(
            flops=2 * pairs * 256 * slab + 40000 * slab, bytes_accessed=8 * slab * lanes, transcendentals=0
        ),
        name="finish",
    )(where, col_mirror, slot, own, *sums)


def swap(array, axis, offset):
    return lax.ppermute(array, axis, [(i, i ^ offset) for i in range(lax.axis_size(axis))])


def after(arrays, earlier):
    earlier = tuple(earlier)
    return list(lax.optimization_barrier((tuple(arrays), earlier))[0]) if earlier else list(arrays)


def forward(held, order):
    reach = [0]
    fresh = []
    for bit in order:
        for offset in list(reach):
            if offset ^ bit not in held:
                held[offset ^ bit] = swap(held[offset], "row", bit)
                fresh.append(offset ^ bit)
            reach.append(offset ^ bit)
    return fresh


class Rows:
    def __init__(self):
        self.arrays, self.places = [], {}

    def add(self, keys, pieces):
        joined = jnp.concatenate(pieces) if len(pieces) > 1 else pieces[0]
        size = pieces[0].shape[0]
        for core, array in enumerate((joined, swap(joined, "row", 1))):
            for n, (offset, j) in enumerate(keys):
                self.places[offset ^ core, j] = (len(self.arrays), n * size)
            self.arrays.append(array)
        return self.arrays[-1]


def body(amplitudes, integrals, irreps, row_mirror, col_mirror):
    rows, cols = lax.axis_size("row"), lax.axis_size("col")
    owned = integrals.shape[0]
    pairs = amplitudes.shape[0]
    slots = pairs // 4
    half = slots // 2
    where = jnp.stack([lax.axis_index("row"), lax.axis_index("col")]).astype(I32)
    slot, packed = pack(where, irreps[None], row_mirror[None], amplitudes, cols, owned, half)
    outer = [1 << b for b in range(1, rows.bit_length() - 1)]
    combined = range(2, rows, 2)
    turns = max(1, cols // max(1, 4 // owned))
    batches = [tuple(range(first, cols, turns)) for first in range(turns)]
    integrals_t = jnp.swapaxes(integrals, 1, 2)

    ready = {}
    for k in range(cols):
        early = () if k < 3 else (ready[k - 1],)
        ready[k] = swap(after([packed[k]], early)[0], "col", k) if k else packed[0]

    parts = []
    for n, batch in enumerate(batches):
        gathered = Rows()
        held = []
        if n == 0:
            inner = []
            for j, k in enumerate(batch):
                (chunk,) = after([ready[k]], [ready[k - 1], *inner[:1]] if j else [])
                held = {0: chunk, **{o: swap(chunk, "row", o) for o in combined}}
                inner = [held[o] for o in combined[::-1]]
                if j == 0:
                    gathered.add([(o, j) for o in held], list(held.values()))
                    continue
                near, far = outer, [o for o in held if o not in outer]
                gathered.add([(o, j) for o in near], [held[o] for o in near])
                early = [ready[k + 1]] if k + 1 < cols else []
                gathered.add([(o, j) for o in far], after([held[o] for o in far], early))
        else:
            keys, pieces, fresh = [], [], []
            for j, k in enumerate(batch):
                held.append({0: ready[k], **{bit: swap(ready[k], "row", bit) for bit in outer}})
            for j, k in enumerate(batch):
                offsets = list(held[j])
                held[j] = dict(zip(offsets, after([held[j][o] for o in offsets], parts[-1][:1])))
                turn = j % len(outer)
                keys += [(o, j) for o in offsets]
                fresh += [(o, j) for o in forward(held[j], outer[turn:] + outer[:turn])]
            gathered.add(keys, [held[j][o] for o, j in keys])
            gathered.add(fresh, [held[j][o] for o, j in fresh])
        arrays = after(gathered.arrays, [part[1] for part in parts[-1:]])
        joined = n + 1 < turns
        part = list(product(arrays, gathered.places, integrals_t, rows, len(batch), slots, joined))
        if joined:
            part[1] = swap(part[1], "row", 1)
        parts.append(part)

    sums = {}
    totals, last = (), ()
    for n, (batch, part) in enumerate(zip(batches, parts)):
        if n + 1 < turns:
            pieces = list(part)
            for o in combined:
                both = jnp.concatenate([array[o // 2 : o // 2 + 1] for array in part])
                pieces.append(swap(both, "row", o))
            last = pieces[2:]
            places = [(o, 0) if o < 2 else (o // 2 + 1, o % 2) for o in range(rows)]
        else:
            far = sorted(range(1, rows), key=lambda o: (-(o >> 1).bit_count(), -o))
            pieces = list(part)
            for m, o in enumerate(far):
                early = [*totals, *(pieces[f] for f in far[:2])] if m >= len(far) - 2 else last
                pieces[o] = swap(after([pieces[o]], early)[0], "row", o)
            places = [(o, None) for o in range(rows)]
        totals = symmetrize(where, col_mirror, pieces, places, batch, owned, half)
        for k, total in zip(batch, totals):
            sums[k] = total if k == 0 else swap(total, "col", k)
        totals = totals[:1]
    return finish(where, col_mirror, slot, sums[0], [sums[k] for k in range(1, cols)], owned, half)


def solution(mesh):
    return jax.shard_map(
        body,
        mesh=mesh,
        in_specs=(
            P(("row", "col"), None),
            P("col", None, "row"),
            P(("row", "col")),
            P(("row", "col")),
            P(),
        ),
        out_specs=P(("row", "col"), None),
        check_vma=False,
    )
```

time: 215 us -> 206 us (0.958)
  starting transfers between devices: 52.9 us -> 44.3 us
  Pallas kernels: 73.9 us -> 71.2 us
    ppermute x48 -> x34, starting transfers between devices: 52.9 us -> 44.3 us  [swap(): lax.ppermute(array, axis, [(i, i ^ offset) for i in range(lax.axis_size(a...]
    pallas_call x3, Pallas kernels: 41.8 us -> 39 us  [the longest x2 25.3 us: symmetrize(): pl.pallas_call(functools.partial(symmetrize_kernel, places, len(parts), c...]
    unnamed x82 -> x51, local copies, waits for them, and re-layouts: 3.35 us -> 4.89 us
    ppermute x48 -> x34, waiting for transfers between devices: 83.9 us -> 84 us  [swap(): lax.ppermute(array, axis, [(i, i ^ offset) for i in range(lax.axis_size(a...]
  transfers between devices with their start and end apart: 48 -> 34, of which waited for: 18 -> 14; matrix products, arithmetic and copies ran while one was open for 0% -> 0% of each run, Pallas kernels for 26% -> 27%
where the time goes in v3:
time: 206 us; the launch traced here: 205 us
  waiting for transfers between devices  84 us (41%)
  Pallas kernels  71.2 us (35%)
  starting transfers between devices  44.3 us (22%)
  local copies, waits for them, and re-layouts  5.15 us (2%)
    ppermute x34, waiting for transfers between devices, swap(): lax.ppermute(array, axis, [(i, i ^ offset) for i in range(lax.axis_size(a...  84 us
    ppermute x34, starting transfers between devices, swap(): lax.ppermute(array, axis, [(i, i ^ offset) for i in range(lax.axis_size(a...  44.3 us
    pallas_call x2, Pallas kernels, product(): pl.pallas_call(functools.partial(product_kernel, holders, chunk_count, ow...  31 us
    pallas_call x2, Pallas kernels, symmetrize(): pl.pallas_call(functools.partial(symmetrize_kernel, places, len(parts), c...  25.3 us
    pallas_call x1, Pallas kernels, finish(): pl.pallas_call(functools.partial(finish_kernel, cols, owned, half, run, t...  13.7 us
    unnamed x51, local copies, waits for them, and re-layouts  4.89 us
  transfers between devices with their start and end apart: 34, of which 14 were waited for; matrix products, arithmetic and copies ran while one was open for 0% of the time, Pallas kernels for 27%

profile of v3, /device:TPU:0, one launch (start us, length us, event | category | flops | bytes accessed | tf_op | source)
XLA Modules:
  0.0 205.3 jit_solution(4047596561154022777)
XLA Ops:
  0.0 0.1 pad_add_fusion.where_ref
  0.1 1.1 copy-done.1
  1.2 0.7 copy-done.3
  1.9 0.7 copy-done.4
  2.5 1.2 pack.1
  3.7 4.0 %collective-permute-start.2 = (bf16[64,3072]{1,0:T(8,128)(2,1)S(1)}, bf16[64,3072]{1,0:T(8,128)(2,1)S(1)}, u32[]{:S(2)}, u32[]{:S(2)}) collective-permute-start(bf16[64,3072]{1,0:T(8,128)(2,1)S(1)} %get-tuple-element.46), channel_id=1, source_target_pairs={{0,24},{4,28},{8,16},{12,20},{16,8},{20,12},{24,0},{28,4},{1,25},{... | collective-permute-start | bytes 1179656 | tf_op jit(solution)/shard_map/ppermute | solution.py:317
  7.7 1.6 collective-permute-start.5
  9.3 2.6 %collective-permute-start.4 = (bf16[64,3072]{1,0:T(8,128)(2,1)S(1)}, bf16[64,3072]{1,0:T(8,128)(2,1)S(1)}, u32[]{:S(2)}, u32[]{:S(2)}) collective-permute-start(bf16[64,3072]{1,0:T(8,128)(2,1)S(1)} %get-tuple-element.47), channel_id=1, source_target_pairs={{0,2},{1,3},{2,0},{3,1},{4,6},{5,7},{6,4},{7,5},{8,10},{9,11},{10,... | collective-permute-start | bytes 1179656 | tf_op jit(solution)/shard_map/ppermute | solution.py:317
  11.9 0.5 collective-permute-start
  12.4 0.5 collective-permute-start.1
  12.9 4.8 %collective-permute-done.2 = bf16[64,3072]{1,0:T(8,128)(2,1)S(1)} collective-permute-done((bf16[64,3072]{1,0:T(8,128)(2,1)S(1)}, bf16[64,3072]{1,0:T(8,128)(2,1)S(1)}, u32[]{:S(2)}, u32[]{:S(2)}) %collective-permute-start.2) | collective-permute-done | bytes 393248 | tf_op jit(solution)/shard_map/ppermute | solution.py:317
  17.7 8.9 %collective-permute-done.5 = bf16[64,3072]{1,0:T(8,128)(2,1)S(1)} collective-permute-done((bf16[64,3072]{1,0:T(8,128)(2,1)S(1)}, bf16[64,3072]{1,0:T(8,128)(2,1)S(1)}, u32[]{:S(2)}, u32[]{:S(2)}) %collective-permute-start.5) | collective-permute-done | bytes 393248 | tf_op jit(solution)/shard_map/ppermute | solution.py:317
  26.6 2.4 %collective-permute-done.4 = bf16[64,3072]{1,0:T(8,128)(2,1)S(1)} collective-permute-done((bf16[64,3072]{1,0:T(8,128)(2,1)S(1)}, bf16[64,3072]{1,0:T(8,128)(2,1)S(1)}, u32[]{:S(2)}, u32[]{:S(2)}) %collective-permute-start.4) | collective-permute-done | bytes 393248 | tf_op jit(solution)/shard_map/ppermute | solution.py:317
  28.9 0.5 collective-permute-start.9
  29.4 1.5 collective-permute-start.6
  30.9 1.5 collective-permute-start.7
  32.4 2.5 %collective-permute-start.10 = (bf16[64,3072]{1,0:T(8,128)(2,1)S(1)}, bf16[64,3072]{1,0:T(8,128)(2,1)S(1)}, u32[]{:S(2)}, u32[]{:S(2)}) collective-permute-start(bf16[64,3072]{1,0:T(8,128)(2,1)S(1)} %get-tuple-element.51), channel_id=1, source_target_pairs={{0,3},{1,2},{2,1},{3,0},{4,7},{5,6},{6,5},{7,4},{8,11},{9,10},{10,... | collective-permute-start | bytes 1179656 | tf_op jit(solution)/shard_map/ppermute | solution.py:317
  35.0 0.1 collective-permute-start.3
  35.1 6.3 %collective-permute-done.9 = bf16[64,3072]{1,0:T(8,128)(2,1)S(1)} collective-permute-done((bf16[64,3072]{1,0:T(8,128)(2,1)S(1)}, bf16[64,3072]{1,0:T(8,128)(2,1)S(1)}, u32[]{:S(2)}, u32[]{:S(2)}) %collective-permute-start.9) | collective-permute-done | bytes 393248 | tf_op jit(solution)/shard_map/ppermute | solution.py:317
  41.4 0.7 collective-permute-done.10
  42.2 0.1 collective-permute-start.11
  42.3 2.4 %collective-permute-done.6 = bf16[64,3072]{1,0:T(8,128)(2,1)S(1)} collective-permute-done((bf16[64,3072]{1,0:T(8,128)(2,1)S(1)}, bf16[64,3072]{1,0:T(8,128)(2,1)S(1)}, u32[]{:S(2)}, u32[]{:S(2)}) %collective-permute-start.6) | collective-permute-done | bytes 393248 | tf_op jit(solution)/shard_map/ppermute | solution.py:317
  44.7 0.9 collective-permute-done.7
  45.6 0.1 collective-permute-start.8
  45.7 0.6 collective-permute-start.16
  46.3 0.7 collective-permute-start.17
  47.0 1.4 collective-permute-start.18
  48.4 1.4 collective-permute-start.19
  49.8 1.2 copy-done.11
  51.0 15.6 %ladder.2 = (bf16[4,1200,128]{2,1,0:T(8,128)(2,1)}, bf16[4,1200,128]{2,1,0:T(8,128)(2,1)}) custom-call(bf16[256,3072]{1,0:T(8,128)(2,1)} %copy-done.9, bf16[256,3072]{1,0:T(8,128)(2,1)} %copy-done.11, bf16[128,3072]{1,0:T(8,128)(2,1)} %copy-done.6, bf16[128,3072]{1,0:T(8,128)(2,1)} %copy-done.14, bf16[128,3072]{1,0:T(8,128)(2,1)} %copy-done.8, ...), custom_call_target="tpu_custom_call" | custom-call | flops 7549747200 | bytes 21037056 | tf_op jit(solution)/shard_map/ladder/pallas_call | solution.py:119
  66.7 0.7 collective-permute-start.22
  67.4 0.7 collective-permute-start.21
  68.1 0.1 collective-permute-start.12
  68.4 0.6 collective-permute-start.20
  68.9 0.1 fusion
  69.0 8.5 %collective-permute-done.21 = bf16[64,3072]{1,0:T(8,128)(2,1)S(1)} collective-permute-done((bf16[64,3072]{1,0:T(8,128)(2,1)S(1)}, bf16[64,3072]{1,0:T(8,128)(2,1)S(1)}, u32[]{:S(2)}, u32[]{:S(2)}) %collective-permute-start.21) | collective-permute-done | bytes 393248 | tf_op jit(solution)/shard_map/ppermute | solution.py:317
  77.6 0.1 collective-permute-start.23
  77.7 0.1 fusion.1
  77.7 0.1 pad_maximum_fusion.2
  77.8 1.6 collective-permute-start.15
  79.4 0.1 pad_maximum_fusion.1
  79.4 1.4 collective-permute-start.14
  80.8 0.1 pad_maximum_fusion
  80.9 0.7 collective-permute-start.13
  81.6 0.9 copy-done.12
  82.5 15.4 %ladder.3 = (bf16[1200,128]{1,0:T(8,128)(2,1)}, bf16[1200,128]{1,0:T(8,128)(2,1)}, bf16[1200,128]{1,0:T(8,128)(2,1)}, bf16[1200,128]{1,0:T(8,128)(2,1)}, bf16[12...) custom-call(bf16[384,3072]{1,0:T(8,128)(2,1)} %copy-done.10, ...), custom_call_target="tpu_custom_call" | custom-call | flops 7549747200 | bytes 21037056 | tf_op jit(solution)/shard_map/ladder/pallas_call | solution.py:119
  98.0 10.2 %collective-permute-done.14.refs_3_ = bf16[2,1200,128]{2,1,0:T(8,128)(2,1)S(1)} collective-permute-done((bf16[2,1200,128]{2,1,0:T(8,128)(2,1)S(1)}, bf16[2,1200,128]{2,1,0:T(8,128)(2,1)S(1)}, u32[]{:S(2)}, u32[]{:S(2)}) %collective-permute-start.14) | collective-permute-done | bytes 614432 | tf_op jit(solution)/shard_map/ppermute | solution.py:317
  108.2 1.5 collective-permute-start.25
  109.7 0.8 collective-permute-start.24
  110.5 12.6 %symmetrize.2 = (bf16[64,9600]{1,0:T(8,128)(2,1)S(1)}, bf16[32,9600]{1,0:T(8,128)(2,1)S(1)}) custom-call(s32[2]{0:T(128)S(1)} %pad_add_fusion.where_ref, s32[9600]{0:T(1024)S(1)} %copy-done.2, bf16[4,1200,128]{2,1,0:T(8,128)(2,1)S(1)} %copy-done, bf16[4,1200,128]{2,1,0:T(8,128)(2,1)S(1)} %collective-permute-done.12.refs_1_, ...), custom_call_target="tpu_custom_call" | custom-call | flops 855859200 | bytes 19660800 | tf_op jit(solution)/shard_map/symmetrize/pallas_call | solution.py:211
  123.1 1.1 collective-permute-start.30
  124.2 1.4 collective-permute-start.29
  125.6 1.2 collective-permute-start.27
  126.8 0.7 collective-permute-start.26
  127.5 4.3 %collective-permute-done.30.refs_5_ = bf16[1200,128]{1,0:T(8,128)(2,1)S(1)} collective-permute-done((bf16[1200,128]{1,0:T(8,128)(2,1)S(1)}, bf16[1200,128]{1,0:T(8,128)(2,1)S(1)}, u32[]{:S(2)}, u32[]{:S(2)}) %collective-permute-start.30) | collective-permute-done | bytes 307232 | tf_op jit(solution)/shard_map/ppermute | solution.py:317
  131.8 5.6 %collective-permute-start.32 = (bf16[32,9600]{1,0:T(8,128)(2,1)S(1)}, bf16[32,9600]{1,0:T(8,128)(2,1)S(1)}, u32[]{:S(2)}, u32[]{:S(2)}) collective-permute-start(bf16[32,9600]{1,0:T(8,128)(2,1)S(1)} %get-tuple-element.83), channel_id=1, source_target_pairs={{0,2},{1,3},{2,0},{3,1},{4,6},{5,7},{6,4},{7,5},{8,10},{9,11},{10,... | collective-permute-start | bytes 1843208 | tf_op jit(solution)/shard_map/ppermute | solution.py:317
  137.4 1.9 collective-permute-done.29.refs_4_
  139.4 1.7 collective-permute-done.27.refs_2_
  141.1 12.6 %symmetrize.3 = (bf16[32,9600]{1,0:T(8,128)(2,1)S(1)}, bf16[32,9600]{1,0:T(8,128)(2,1)S(1)}) custom-call(s32[2]{0:T(128)S(1)} %pad_add_fusion.where_ref, s32[9600]{0:T(1024)S(1)} %copy-done.2, bf16[1200,128]{1,0:T(8,128)(2,1)S(1)} %copy-done.5, bf16[1200,128]{1,0:T(8,128)(2,1)S(1)} %collective-permute-done.26.refs_1_, ...), custom_call_target="tpu_custom_call" | custom-call | flops 698572800 | bytes 19660800 | tf_op jit(solution)/shard_map/symmetrize/pallas_call | solution.py:211
  153.7 5.2 %collective-permute-start.31 = (bf16[32,9600]{1,0:T(8,128)(2,1)S(1)}, bf16[32,9600]{1,0:T(8,128)(2,1)S(1)}, u32[]{:S(2)}, u32[]{:S(2)}) collective-permute-start(bf16[32,9600]{1,0:T(8,128)(2,1)S(1)} %get-tuple-element.82), channel_id=1, source_target_pairs={{0,1},{1,0},{2,3},{3,2},{4,5},{5,4},{6,7},{7,6},{8,9},{9,8},{10,11... | collective-permute-start | bytes 1843208 | tf_op jit(solution)/shard_map/ppermute | solution.py:317
  158.9 1.7 collective-permute-start.33
  160.6 4.4 %collective-permute-done.32.refs_2_ = bf16[32,9600]{1,0:T(8,128)(2,1)S(1)} collective-permute-done((bf16[32,9600]{1,0:T(8,128)(2,1)S(1)}, bf16[32,9600]{1,0:T(8,128)(2,1)S(1)}, u32[]{:S(2)}, u32[]{:S(2)}) %collective-permute-start.32) | collective-permute-done | bytes 614432 | tf_op jit(solution)/shard_map/ppermute | solution.py:317
  165.0 26.6 %collective-permute-done.31.refs_1_ = bf16[32,9600]{1,0:T(8,128)(2,1)S(1)} collective-permute-done((bf16[32,9600]{1,0:T(8,128)(2,1)S(1)}, bf16[32,9600]{1,0:T(8,128)(2,1)S(1)}, u32[]{:S(2)}, u32[]{:S(2)}) %collective-permute-start.31) | collective-permute-done | bytes 614432 | tf_op jit(solution)/shard_map/ppermute | solution.py:317
  191.6 13.7 %finish.1 = bf16[128,9600]{1,0:T(8,128)(2,1)} custom-call(s32[2]{0:T(128)S(1)} %pad_add_fusion.where_ref, s32[9600]{0:T(1024)S(1)} %copy-done.2, s32[1,128]{1,0:T(1,128)S(1)} %get-tuple-element.45.slot_ref, bf16[64,9600]{1,0:T(8,128)(2,1)S(1)} %get-tuple-element.56.refs_0_, bf16[32,9600]{1,0:T(8,128)(2,1)S(1)} %collective-permute-done.31.refs_1_, ...), custom_call_target="tpu_custom_call" | custom-call | flops 1013145600 | bytes 9830400 | tf_op jit(solution)/shard_map/finish/pallas_call | solution.py:294
  (72 shorter events, 0.6 us)
Async XLA Ops:
  0.1 1.1 copy-start.1
  1.2 0.7 copy-start.3
  1.9 0.7 copy-start.4
  3.7 14.0 %collective-permute-start.2 = (bf16[64,3072]{1,0:T(8,128)(2,1)S(1)}, bf16[64,3072]{1,0:T(8,128)(2,1)S(1)}, u32[]{:S(2)}, u32[]{:S(2)}) collective-permute-start(bf16[64,3072]{1,0:T(8,128)(2,1)S(1)} %get-tuple-element.46), channel_id=1, source_target_pairs={{0,24},{4,28},{8,16},{12,20},{16,8},{20,12},{24,0},{28,4},{1,25},{... | collective-permute-start | bytes 1179656 | tf_op jit(solution)/shard_map/ppermute | solution.py:317
  7.7 18.9 %collective-permute-start.5 = (bf16[64,3072]{1,0:T(8,128)(2,1)S(1)}, bf16[64,3072]{1,0:T(8,128)(2,1)S(1)}, u32[]{:S(2)}, u32[]{:S(2)}) collective-permute-start(bf16[64,3072]{1,0:T(8,128)(2,1)S(1)} %get-tuple-element.48), channel_id=1, source_target_pairs={{0,1},{1,0},{2,3},{3,2},{4,5},{5,4},{6,7},{7,6},{8,9},{9,8},{10,11... | collective-permute-start | bytes 1179656 | tf_op jit(solution)/shard_map/ppermute | solution.py:317
  9.3 19.7 %collective-permute-start.4 = (bf16[64,3072]{1,0:T(8,128)(2,1)S(1)}, bf16[64,3072]{1,0:T(8,128)(2,1)S(1)}, u32[]{:S(2)}, u32[]{:S(2)}) collective-permute-start(bf16[64,3072]{1,0:T(8,128)(2,1)S(1)} %get-tuple-element.47), channel_id=1, source_target_pairs={{0,2},{1,3},{2,0},{3,1},{4,6},{5,7},{6,4},{7,5},{8,10},{9,11},{10,... | collective-permute-start | bytes 1179656 | tf_op jit(solution)/shard_map/ppermute | solution.py:317
  11.9 20.6 %collective-permute-start = (bf16[64,3072]{1,0:T(8,128)(2,1)S(1)}, bf16[64,3072]{1,0:T(8,128)(2,1)S(1)}, u32[]{:S(2)}, u32[]{:S(2)}) collective-permute-start(bf16[64,3072]{1,0:T(8,128)(2,1)S(1)} %get-tuple-element.46), channel_id=1, source_target_pairs={{0,8},{4,12},{8,0},{12,4},{16,24},{20,28},{24,16},{28,20},{1,9},{5... | collective-permute-start | bytes 1179656 | tf_op jit(solution)/shard_map/ppermute | solution.py:317
  12.4 22.5 %collective-permute-start.1 = (bf16[64,3072]{1,0:T(8,128)(2,1)S(1)}, bf16[64,3072]{1,0:T(8,128)(2,1)S(1)}, u32[]{:S(2)}, u32[]{:S(2)}) collective-permute-start(bf16[64,3072]{1,0:T(8,128)(2,1)S(1)} %get-tuple-element.46), channel_id=1, source_target_pairs={{0,16},{4,20},{8,24},{12,28},{16,0},{20,4},{24,8},{28,12},{1,17},{... | collective-permute-start | bytes 1179656 | tf_op jit(solution)/shard_map/ppermute | solution.py:317
  28.9 12.5 %collective-permute-start.9 = (bf16[64,3072]{1,0:T(8,128)(2,1)S(1)}, bf16[64,3072]{1,0:T(8,128)(2,1)S(1)}, u32[]{:S(2)}, u32[]{:S(2)}) collective-permute-start(bf16[64,3072]{1,0:T(8,128)(2,1)S(1)} %collective-permute-done.4), channel_id=1, source_target_pairs={{0,24},{4,28},{8,16},{12,20},{16,8},{20,12},{24,0},{28,4},{1,25},{... | collective-permute-start | bytes 1179656 | tf_op jit(solution)/shard_map/ppermute | solution.py:317
  29.4 15.2 %collective-permute-start.6 = (bf16[64,3072]{1,0:T(8,128)(2,1)S(1)}, bf16[64,3072]{1,0:T(8,128)(2,1)S(1)}, u32[]{:S(2)}, u32[]{:S(2)}) collective-permute-start(bf16[64,3072]{1,0:T(8,128)(2,1)S(1)} %collective-permute-done.4), channel_id=1, source_target_pairs={{0,8},{4,12},{8,0},{12,4},{16,24},{20,28},{24,16},{28,20},{1,9},{5... | collective-permute-start | bytes 1179656 | tf_op jit(solution)/shard_map/ppermute | solution.py:317
  30.9 14.7 %collective-permute-start.7 = (bf16[64,3072]{1,0:T(8,128)(2,1)S(1)}, bf16[64,3072]{1,0:T(8,128)(2,1)S(1)}, u32[]{:S(2)}, u32[]{:S(2)}) collective-permute-start(bf16[64,3072]{1,0:T(8,128)(2,1)S(1)} %collective-permute-done.4), channel_id=1, source_target_pairs={{0,16},{4,20},{8,24},{12,28},{16,0},{20,4},{24,8},{28,12},{1,17},{... | collective-permute-start | bytes 1179656 | tf_op jit(solution)/shard_map/ppermute | solution.py:317
  32.4 9.7 %collective-permute-start.10 = (bf16[64,3072]{1,0:T(8,128)(2,1)S(1)}, bf16[64,3072]{1,0:T(8,128)(2,1)S(1)}, u32[]{:S(2)}, u32[]{:S(2)}) collective-permute-start(bf16[64,3072]{1,0:T(8,128)(2,1)S(1)} %get-tuple-element.51), channel_id=1, source_target_pairs={{0,3},{1,2},{2,1},{3,0},{4,7},{5,6},{6,5},{7,4},{8,11},{9,10},{10,... | collective-permute-start | bytes 1179656 | tf_op jit(solution)/shard_map/ppermute | solution.py:317
  35.0 16.0 %copy-start.9 = (bf16[256,3072]{1,0:T(8,128)(2,1)}, bf16[256,3072]{1,0:T(8,128)(2,1)S(1)}, u32[]{:S(2)}) copy-start(bf16[256,3072]{1,0:T(8,128)(2,1)S(1)} %constant_dynamic-update-slice_fusion.refs_0_) | copy-start | bytes 4718596
  35.0 14.8 %collective-permute-start.3 = (bf16[256,3072]{1,0:T(8,128)(2,1)S(1)}, bf16[256,3072]{1,0:T(8,128)(2,1)S(1)}, u32[]{:S(2)}, u32[]{:S(2)}) collective-permute-start(bf16[256,3072]{1,0:T(8,128)(2,1)S(1)} %constant_dynamic-update-slice_fusion.refs_0_), channel_id=1, source_target_pairs={{0,4},{4,0},{8,12},{12,8},{16,20},{20,16},{24,28},{28,24},{1,5},{5... | collective-permute-start | bytes 4718600 | tf_op jit(solution)/shard_map/ppermute | solution.py:317
  42.2 8.8 %copy-start.8 = (bf16[128,3072]{1,0:T(8,128)(2,1)}, bf16[128,3072]{1,0:T(8,128)(2,1)S(1)}, u32[]{:S(2)}) copy-start(bf16[128,3072]{1,0:T(8,128)(2,1)S(1)} %constant_dynamic-update-slice_fusion.6.refs_4_) | copy-start | bytes 2359300
  42.2 4.8 %collective-permute-start.11 = (bf16[128,3072]{1,0:T(8,128)(2,1)S(1)}, bf16[128,3072]{1,0:T(8,128)(2,1)S(1)}, u32[]{:S(2)}, u32[]{:S(2)}) collective-permute-start(bf16[128,3072]{1,0:T(8,128)(2,1)S(1)} %constant_dynamic-update-slice_fusion.6.refs_4_), channel_id=1, source_target_pairs={{0,4},{4,0},{8,12},{12,8},{16,20},{20,16},{24,28},{28,24},{1,5},{5... | collective-permute-start | bytes 2359304 | tf_op jit(solution)/shard_map/ppermute | solution.py:317
  45.6 5.4 %copy-start.6 = (bf16[128,3072]{1,0:T(8,128)(2,1)}, bf16[128,3072]{1,0:T(8,128)(2,1)S(1)}, u32[]{:S(2)}) copy-start(bf16[128,3072]{1,0:T(8,128)(2,1)S(1)} %constant_dynamic-update-slice_fusion.4.refs_2_) | copy-start | bytes 2359300
  45.6 2.8 %collective-permute-start.8 = (bf16[128,3072]{1,0:T(8,128)(2,1)S(1)}, bf16[128,3072]{1,0:T(8,128)(2,1)S(1)}, u32[]{:S(2)}, u32[]{:S(2)}) collective-permute-start(bf16[128,3072]{1,0:T(8,128)(2,1)S(1)} %constant_dynamic-update-slice_fusion.4.refs_2_), channel_id=1, source_target_pairs={{0,4},{4,0},{8,12},{12,8},{16,20},{20,16},{24,28},{28,24},{1,5},{5... | collective-permute-start | bytes 2359304 | tf_op jit(solution)/shard_map/ppermute | solution.py:317
  45.7 21.7 %collective-permute-start.16 = (bf16[64,3072]{1,0:T(8,128)(2,1)S(1)}, bf16[64,3072]{1,0:T(8,128)(2,1)S(1)}, u32[]{:S(2)}, u32[]{:S(2)}) collective-permute-start(bf16[64,3072]{1,0:T(8,128)(2,1)S(1)} %collective-permute-done.5), channel_id=1, source_target_pairs={{0,8},{4,12},{8,0},{12,4},{16,24},{20,28},{24,16},{28,20},{1,9},{5... | collective-permute-start | bytes 1179656 | tf_op jit(solution)/shard_map/ppermute | solution.py:317
  46.3 21.1 %collective-permute-start.17 = (bf16[64,3072]{1,0:T(8,128)(2,1)S(1)}, bf16[64,3072]{1,0:T(8,128)(2,1)S(1)}, u32[]{:S(2)}, u32[]{:S(2)}) collective-permute-start(bf16[64,3072]{1,0:T(8,128)(2,1)S(1)} %collective-permute-done.5), channel_id=1, source_target_pairs={{0,16},{4,20},{8,24},{12,28},{16,0},{20,4},{24,8},{28,12},{1,17},{... | collective-permute-start | bytes 1179656 | tf_op jit(solution)/shard_map/ppermute | solution.py:317
  47.0 4.0 %copy-start.13 = (bf16[128,3072]{1,0:T(8,128)(2,1)}, bf16[128,3072]{1,0:T(8,128)(2,1)S(1)}, u32[]{:S(2)}) copy-start(bf16[128,3072]{1,0:T(8,128)(2,1)S(1)} %collective-permute-done.11.refs_5_) | copy-start | bytes 2359300
  47.0 19.7 %collective-permute-start.18 = (bf16[64,3072]{1,0:T(8,128)(2,1)S(1)}, bf16[64,3072]{1,0:T(8,128)(2,1)S(1)}, u32[]{:S(2)}, u32[]{:S(2)}) collective-permute-start(bf16[64,3072]{1,0:T(8,128)(2,1)S(1)} %collective-permute-done.10), channel_id=1, source_target_pairs={{0,8},{4,12},{8,0},{12,4},{16,24},{20,28},{24,16},{28,20},{1,9},{5... | collective-permute-start | bytes 1179656 | tf_op jit(solution)/shard_map/ppermute | solution.py:317
  48.4 2.6 %copy-start.14 = (bf16[128,3072]{1,0:T(8,128)(2,1)}, bf16[128,3072]{1,0:T(8,128)(2,1)S(1)}, u32[]{:S(2)}) copy-start(bf16[128,3072]{1,0:T(8,128)(2,1)S(1)} %collective-permute-done.8.refs_3_) | copy-start | bytes 2359300
  48.4 18.2 %collective-permute-start.19 = (bf16[64,3072]{1,0:T(8,128)(2,1)S(1)}, bf16[64,3072]{1,0:T(8,128)(2,1)S(1)}, u32[]{:S(2)}, u32[]{:S(2)}) collective-permute-start(bf16[64,3072]{1,0:T(8,128)(2,1)S(1)} %collective-permute-done.10), channel_id=1, source_target_pairs={{0,16},{4,20},{8,24},{12,28},{16,0},{20,4},{24,8},{28,12},{1,17},{... | collective-permute-start | bytes 1179656 | tf_op jit(solution)/shard_map/ppermute | solution.py:317
  49.8 1.2 copy-start.11
  66.7 2.2 %copy-start = (bf16[4,1200,128]{2,1,0:T(8,128)(2,1)S(1)}, bf16[4,1200,128]{2,1,0:T(8,128)(2,1)}, u32[]{:S(2)}) copy-start(bf16[4,1200,128]{2,1,0:T(8,128)(2,1)} %get-tuple-element.54.refs_0_) | copy-start | bytes 3686404
  66.7 10.8 %collective-permute-start.22 = (bf16[64,3072]{1,0:T(8,128)(2,1)S(1)}, bf16[64,3072]{1,0:T(8,128)(2,1)S(1)}, u32[]{:S(2)}, u32[]{:S(2)}) collective-permute-start(bf16[64,3072]{1,0:T(8,128)(2,1)S(1)} %collective-permute-done.19), channel_id=1, source_target_pairs={{0,8},{4,12},{8,0},{12,4},{16,24},{20,28},{24,16},{28,20},{1,9},{5... | collective-permute-start | bytes 1179656 | tf_op jit(solution)/shard_map/ppermute | solution.py:317
  67.4 10.1 %collective-permute-start.21 = (bf16[64,3072]{1,0:T(8,128)(2,1)S(1)}, bf16[64,3072]{1,0:T(8,128)(2,1)S(1)}, u32[]{:S(2)}, u32[]{:S(2)}) collective-permute-start(bf16[64,3072]{1,0:T(8,128)(2,1)S(1)} %collective-permute-done.16), channel_id=1, source_target_pairs={{0,16},{4,20},{8,24},{12,28},{16,0},{20,4},{24,8},{28,12},{1,17},{... | collective-permute-start | bytes 1179656 | tf_op jit(solution)/shard_map/ppermute | solution.py:317
  68.1 9.5 %collective-permute-start.12 = (bf16[4,1200,128]{2,1,0:T(8,128)(2,1)}, bf16[4,1200,128]{2,1,0:T(8,128)(2,1)S(1)}, u32[]{:S(2)}, u32[]{:S(2)}) collective-permute-start(bf16[4,1200,128]{2,1,0:T(8,128)(2,1)} %get-tuple-element.55), channel_id=1, source_target_pairs={{0,4},{4,0},{8,12},{12,8},{16,20},{20,16},{24,28},{28,24},{1,5},{5... | collective-permute-start | bytes 3686408 | tf_op jit(solution)/shard_map/ppermute | solution.py:317
  68.3 9.4 %copy-start.10 = (bf16[384,3072]{1,0:T(8,128)(2,1)}, bf16[384,3072]{1,0:T(8,128)(2,1)S(1)}, u32[]{:S(2)}) copy-start(bf16[384,3072]{1,0:T(8,128)(2,1)S(1)} %constant_dynamic-update-slice_fusion.8.refs_0_) | copy-start | bytes 7077892
  68.4 13.3 %collective-permute-start.20 = (bf16[384,3072]{1,0:T(8,128)(2,1)S(1)}, bf16[384,3072]{1,0:T(8,128)(2,1)}, u32[]{:S(2)}, u32[]{:S(2)}) collective-permute-start(bf16[384,3072]{1,0:T(8,128)(2,1)S(1)} %constant_dynamic-update-slice_fusion.8.refs_0_), channel_id=1, source_target_pairs={{0,4},{4,0},{8,12},{12,8},{16,20},{20,16},{24,28},{28,24},{1,5},{5... | collective-permute-start | bytes 7077896 | tf_op jit(solution)/shard_map/ppermute | solution.py:317
  77.6 3.3 %copy-start.7 = (bf16[128,3072]{1,0:T(8,128)(2,1)}, bf16[128,3072]{1,0:T(8,128)(2,1)S(1)}, u32[]{:S(2)}) copy-start(bf16[128,3072]{1,0:T(8,128)(2,1)S(1)} %constant_dynamic-update-slice_fusion.14.refs_2_) | copy-start | bytes 2359300
  77.6 4.1 %collective-permute-start.23 = (bf16[128,3072]{1,0:T(8,128)(2,1)S(1)}, bf16[128,3072]{1,0:T(8,128)(2,1)S(1)}, u32[]{:S(2)}, u32[]{:S(2)}) collective-permute-start(bf16[128,3072]{1,0:T(8,128)(2,1)S(1)} %constant_dynamic-update-slice_fusion.14.refs_2_), channel_id=1, source_target_pairs={{0,4},{4,0},{8,12},{12,8},{16,20},{20,16},{24,28},{28,24},{1,5},{5... | collective-permute-start | bytes 2359304 | tf_op jit(solution)/shard_map/ppermute | solution.py:317
  77.8 20.2 %collective-permute-start.15 = (bf16[2,1200,128]{2,1,0:T(8,128)(2,1)S(1)}, bf16[2,1200,128]{2,1,0:T(8,128)(2,1)S(1)}, u32[]{:S(2)}, u32[]{:S(2)}) collective-permute-start(bf16[2,1200,128]{2,1,0:T(8,128)(2,1)S(1)} %pad_maximum_fusion.2), channel_id=1, source_target_pairs={{0,24},{4,28},{8,16},{12,20},{16,8},{20,12},{24,0},{28,4},{1,25},{... | collective-permute-start | bytes 1843208 | tf_op jit(solution)/shard_map/ppermute | solution.py:317
  79.4 28.7 %collective-permute-start.14 = (bf16[2,1200,128]{2,1,0:T(8,128)(2,1)S(1)}, bf16[2,1200,128]{2,1,0:T(8,128)(2,1)S(1)}, u32[]{:S(2)}, u32[]{:S(2)}) collective-permute-start(bf16[2,1200,128]{2,1,0:T(8,128)(2,1)S(1)} %pad_maximum_fusion.1), channel_id=1, source_target_pairs={{0,16},{4,20},{8,24},{12,28},{16,0},{20,4},{24,8},{28,12},{1,17},{... | collective-permute-start | bytes 1843208 | tf_op jit(solution)/shard_map/ppermute | solution.py:317
  80.9 29.6 %copy-start.2 = (s32[9600]{0:T(1024)S(1)}, s32[9600]{0:T(1024)}, u32[]{:S(2)}) copy-start(s32[9600]{0:T(1024)} %mirror_ref.5) | copy-start | bytes 115204
  80.9 27.3 %collective-permute-start.13 = (bf16[2,1200,128]{2,1,0:T(8,128)(2,1)S(1)}, bf16[2,1200,128]{2,1,0:T(8,128)(2,1)S(1)}, u32[]{:S(2)}, u32[]{:S(2)}) collective-permute-start(bf16[2,1200,128]{2,1,0:T(8,128)(2,1)S(1)} %pad_maximum_fusion), channel_id=1, source_target_pairs={{0,8},{4,12},{8,0},{12,4},{16,24},{20,28},{24,16},{28,20},{1,9},{5... | collective-permute-start | bytes 1843208 | tf_op jit(solution)/shard_map/ppermute | solution.py:317
  81.6 0.9 copy-start.12
  98.0 25.2 %copy-start.19 = (bf16[1200,128]{1,0:T(8,128)(2,1)S(1)}, bf16[1200,128]{1,0:T(8,128)(2,1)}, u32[]{:S(2)}) copy-start(bf16[1200,128]{1,0:T(8,128)(2,1)} %get-tuple-element.81) | copy-start | bytes 921604
  98.0 26.2 %copy-start.18 = (bf16[1200,128]{1,0:T(8,128)(2,1)S(1)}, bf16[1200,128]{1,0:T(8,128)(2,1)}, u32[]{:S(2)}) copy-start(bf16[1200,128]{1,0:T(8,128)(2,1)} %get-tuple-element.79) | copy-start | bytes 921604
  98.0 27.6 %copy-start.17 = (bf16[1200,128]{1,0:T(8,128)(2,1)S(1)}, bf16[1200,128]{1,0:T(8,128)(2,1)}, u32[]{:S(2)}) copy-start(bf16[1200,128]{1,0:T(8,128)(2,1)} %get-tuple-element.77) | copy-start | bytes 921604
  98.0 27.6 %copy-start.16 = (bf16[1200,128]{1,0:T(8,128)(2,1)S(1)}, bf16[1200,128]{1,0:T(8,128)(2,1)}, u32[]{:S(2)}) copy-start(bf16[1200,128]{1,0:T(8,128)(2,1)} %get-tuple-element.75) | copy-start | bytes 921604
  98.0 28.8 %copy-start.15 = (bf16[1200,128]{1,0:T(8,128)(2,1)S(1)}, bf16[1200,128]{1,0:T(8,128)(2,1)}, u32[]{:S(2)}) copy-start(bf16[1200,128]{1,0:T(8,128)(2,1)} %get-tuple-element.73) | copy-start | bytes 921604
  98.0 43.1 %copy-start.5 = (bf16[1200,128]{1,0:T(8,128)(2,1)S(1)}, bf16[1200,128]{1,0:T(8,128)(2,1)}, u32[]{:S(2)}) copy-start(bf16[1200,128]{1,0:T(8,128)(2,1)} %get-tuple-element.67.refs_0_) | copy-start | bytes 921604
  108.2 17.4 %collective-permute-start.25 = (bf16[1200,128]{1,0:T(8,128)(2,1)}, bf16[1200,128]{1,0:T(8,128)(2,1)S(1)}, u32[]{:S(2)}, u32[]{:S(2)}) collective-permute-start(bf16[1200,128]{1,0:T(8,128)(2,1)} %get-tuple-element.72), channel_id=1, source_target_pairs={{0,24},{4,28},{8,16},{12,20},{16,8},{20,12},{24,0},{28,4},{1,25},{... | collective-permute-start | bytes 921608 | tf_op jit(solution)/shard_map/ppermute | solution.py:317
  109.7 15.9 %collective-permute-start.24 = (bf16[1200,128]{1,0:T(8,128)(2,1)}, bf16[1200,128]{1,0:T(8,128)(2,1)S(1)}, u32[]{:S(2)}, u32[]{:S(2)}) collective-permute-start(bf16[1200,128]{1,0:T(8,128)(2,1)} %get-tuple-element.70), channel_id=1, source_target_pairs={{0,28},{4,24},{8,20},{12,16},{16,12},{20,8},{24,4},{28,0},{1,29},{... | collective-permute-start | bytes 921608 | tf_op jit(solution)/shard_map/ppermute | solution.py:317
  123.1 8.7 %collective-permute-start.30 = (bf16[1200,128]{1,0:T(8,128)(2,1)S(1)}, bf16[1200,128]{1,0:T(8,128)(2,1)S(1)}, u32[]{:S(2)}, u32[]{:S(2)}) collective-permute-start(bf16[1200,128]{1,0:T(8,128)(2,1)S(1)} %copy-done.19), channel_id=1, source_target_pairs={{0,20},{4,16},{8,28},{12,24},{16,4},{20,0},{24,12},{28,8},{1,21},{... | collective-permute-start | bytes 921608 | tf_op jit(solution)/shard_map/ppermute | solution.py:317
  124.2 15.1 %collective-permute-start.29 = (bf16[1200,128]{1,0:T(8,128)(2,1)S(1)}, bf16[1200,128]{1,0:T(8,128)(2,1)S(1)}, u32[]{:S(2)}, u32[]{:S(2)}) collective-permute-start(bf16[1200,128]{1,0:T(8,128)(2,1)S(1)} %copy-done.18), channel_id=1, source_target_pairs={{0,16},{4,20},{8,24},{12,28},{16,0},{20,4},{24,8},{28,12},{1,17},{... | collective-permute-start | bytes 921608 | tf_op jit(solution)/shard_map/ppermute | solution.py:317
  125.6 13.8 %collective-permute-start.28 = (bf16[1200,128]{1,0:T(8,128)(2,1)S(1)}, bf16[1200,128]{1,0:T(8,128)(2,1)S(1)}, u32[]{:S(2)}, u32[]{:S(2)}) collective-permute-start(bf16[1200,128]{1,0:T(8,128)(2,1)S(1)} %copy-done.17), channel_id=1, source_target_pairs={{0,12},{4,8},{8,4},{12,0},{16,28},{20,24},{24,20},{28,16},{1,13},{... | collective-permute-start | bytes 921608 | tf_op jit(solution)/shard_map/ppermute | solution.py:317
  125.6 15.4 %collective-permute-start.27 = (bf16[1200,128]{1,0:T(8,128)(2,1)S(1)}, bf16[1200,128]{1,0:T(8,128)(2,1)S(1)}, u32[]{:S(2)}, u32[]{:S(2)}) collective-permute-start(bf16[1200,128]{1,0:T(8,128)(2,1)S(1)} %copy-done.16), channel_id=1, source_target_pairs={{0,8},{4,12},{8,0},{12,4},{16,24},{20,28},{24,16},{28,20},{1,9},{5... | collective-permute-start | bytes 921608 | tf_op jit(solution)/shard_map/ppermute | solution.py:317
  126.8 14.3 %collective-permute-start.26 = (bf16[1200,128]{1,0:T(8,128)(2,1)S(1)}, bf16[1200,128]{1,0:T(8,128)(2,1)S(1)}, u32[]{:S(2)}, u32[]{:S(2)}) collective-permute-start(bf16[1200,128]{1,0:T(8,128)(2,1)S(1)} %copy-done.15), channel_id=1, source_target_pairs={{0,4},{4,0},{8,12},{12,8},{16,20},{20,16},{24,28},{28,24},{1,5},{5... | collective-permute-start | bytes 921608 | tf_op jit(solution)/shard_map/ppermute | solution.py:317
  131.8 33.1 %collective-permute-start.32 = (bf16[32,9600]{1,0:T(8,128)(2,1)S(1)}, bf16[32,9600]{1,0:T(8,128)(2,1)S(1)}, u32[]{:S(2)}, u32[]{:S(2)}) collective-permute-start(bf16[32,9600]{1,0:T(8,128)(2,1)S(1)} %get-tuple-element.83), channel_id=1, source_target_pairs={{0,2},{1,3},{2,0},{3,1},{4,6},{5,7},{6,4},{7,5},{8,10},{9,11},{10,... | collective-permute-start | bytes 1843208 | tf_op jit(solution)/shard_map/ppermute | solution.py:317
  153.7 37.9 %collective-permute-start.31 = (bf16[32,9600]{1,0:T(8,128)(2,1)S(1)}, bf16[32,9600]{1,0:T(8,128)(2,1)S(1)}, u32[]{:S(2)}, u32[]{:S(2)}) collective-permute-start(bf16[32,9600]{1,0:T(8,128)(2,1)S(1)} %get-tuple-element.82), channel_id=1, source_target_pairs={{0,1},{1,0},{2,3},{3,2},{4,5},{5,4},{6,7},{7,6},{8,9},{9,8},{10,11... | collective-permute-start | bytes 1843208 | tf_op jit(solution)/shard_map/ppermute | solution.py:317
  158.9 32.8 %collective-permute-start.33 = (bf16[32,9600]{1,0:T(8,128)(2,1)S(1)}, bf16[32,9600]{1,0:T(8,128)(2,1)S(1)}, u32[]{:S(2)}, u32[]{:S(2)}) collective-permute-start(bf16[32,9600]{1,0:T(8,128)(2,1)S(1)} %get-tuple-element.84), channel_id=1, source_target_pairs={{0,3},{1,2},{2,1},{3,0},{4,7},{5,6},{6,5},{7,4},{8,11},{9,10},{10,... | collective-permute-start | bytes 1843208 | tf_op jit(solution)/shard_map/ppermute | solution.py:317

commit v4 on v3

--- a/solution.py
+++ b/solution.py
@@ -1,4 +1,5 @@
 import functools
+import math
 
 import jax
 import jax.numpy as jnp
@@ -148,7 +149,7 @@
     return next(n for n in (15, 5, 3, 4, 2, 1) if tiles % n == 0), 1
 
 
-def symmetrize_kernel(places, array_count, chunks, owned, half, run, turns, where_ref, mirror_ref, *refs):
+def symmetrize_kernel(places, array_count, chunks, owned, half, run, turns, offset, where_ref, mirror_ref, *refs):
     holders = len(places)
     parts, refs = refs[:array_count], refs[array_count:]
     outs, refs = refs[: len(chunks)], refs[len(chunks) :]
@@ -187,7 +188,7 @@
     def some(n, carry):
         for i in range(run):
             inside = pl.multiple_of((n * run + i) * TILE, TILE)
-            base = step * (turns * run * TILE) + inside
+            base = (step + offset) * (turns * run * TILE) + inside
             gather_rows(mirror_ref, base, wide, picked[i])
             here = wide[pl.ds(pl.multiple_of(base, TILE), TILE), :]
             both = jnp.concatenate([here, picked[i][...]], axis=1).astype(BF16)
@@ -201,7 +202,7 @@
     lax.fori_loop(0, turns, some, 0)
 
 
-def symmetrize(where, col_mirror, parts, places, chunks, owned, half):
+def symmetrize(where, col_mirror, parts, places, chunks, owned, half, first, blocks):
     holders = len(places)
     share, lanes = parts[0].shape[-2:]
     slab = col_mirror.shape[0]
@@ -209,10 +210,10 @@
     block = run * turns * TILE
     rows = [owned * half * (2 if k == 0 else 1) for k in chunks]
     return pl.pallas_call(
-        functools.partial(symmetrize_kernel, places, len(parts), chunks, owned, half, run, turns),
+        functools.partial(symmetrize_kernel, places, len(parts), chunks, owned, half, run, turns, first),
         grid_spec=pltpu.PrefetchScalarGridSpec(
             num_scalar_prefetch=2,
-            grid=(slab // block,),
+            grid=(blocks,),
             in_specs=[pl.BlockSpec(memory_space=pl.ANY)] * len(parts),
             out_specs=[pl.BlockSpec((n, block), lambda s, w, m: (0, s)) for n in rows],
             scratch_shapes=[
@@ -222,33 +223,42 @@
             ]
             + [pltpu.VMEM((TILE, lanes), F32)] * run,
         ),
-        out_shape=[jax.ShapeDtypeStruct((n, slab), BF16) for n in rows],
+        out_shape=[jax.ShapeDtypeStruct((n, blocks * block), BF16) for n in rows],
         compiler_params=params(),
         cost_estimate=pl.CostEstimate(
-            flops=4 * sum(rows) * lanes * slab + 40000 * slab, bytes_accessed=16 * slab * lanes, transcendentals=0
+            flops=(4 * sum(rows) * lanes + 40000) * blocks * block, bytes_accessed=1 * slab * lanes, transcendentals=0
         ),
         name="symmetrize",
     )(where, col_mirror, *parts)
 
 
-def finish_kernel(cols, owned, half, run, turns, where_ref, mirror_ref, slot_ref, *refs):
-    own_ref = refs[0]
-    sums = refs[1:cols]
-    out_ref, wide = refs[cols : cols + 2]
-    picked = refs[cols + 2 :]
+def finish_kernel(cols, owned, half, run, turns, spans, where_ref, mirror_ref, slot_ref, *refs):
+    count = len(spans)
+    parts = refs[:count]
+    out_ref, rows_ref, wide, sem, *picked = refs[count:]
     step = pl.program_id(0)
     slab, lanes = wide.shape
     pairs = out_ref.shape[0]
     sent = owned * half
+    own = 2 * sent
     used = (cols - 1) * sent
     block = run * turns * TILE
 
     @pl.when(step == 0)
     def _():
+        copies = []
+        for m, (k, start, size) in enumerate(spans):
+            at = pl.ds(own + (k - 1) * sent, sent) if k else pl.ds(0, own)
+            copies.append(pltpu.make_async_copy(parts[m], rows_ref.at[at, pl.ds(start, size)], sem.at[m]))
+        for copy in copies:
+            copy.start()
+        for copy in copies:
+            copy.wait()
+
         def widen(n, carry):
             for i in range(run):
                 at = pl.ds(pl.multiple_of((n * run + i) * TILE, TILE), TILE)
-                rows = [s[:, at].astype(F32) for s in sums]
+                rows = [rows_ref[own:, at].astype(F32)]
                 if lanes > used:
                     rows.append(jnp.zeros((lanes - used, TILE), F32))
                 wide[at, :] = jnp.concatenate(rows, axis=0).T
@@ -258,7 +268,6 @@
 
     slot = jnp.broadcast_to(slot_ref[...], (pairs, pairs)).astype(F32).T.astype(I32)[:, :1]
     col = where_ref[1]
-    own = own_ref.shape[0]
     onehots = [slot == col * own + iota((pairs, own), 1)]
     at = iota((pairs, used), 1)
     rest = at % sent
@@ -275,8 +284,7 @@
             inside = pl.multiple_of((n * run + i) * TILE, TILE)
             base = pl.multiple_of(step * block + inside, TILE)
             gather_rows(mirror_ref, base, wide, picked[i])
-            rows = [own_ref[:, pl.ds(inside, TILE)]] + [s[:, pl.ds(base, TILE)] for s in sums]
-            total = lax.dot_general(straight, jnp.concatenate(rows, axis=0), NN, preferred_element_type=F32)
+            total = lax.dot_general(straight, rows_ref[:, pl.ds(base, TILE)], NN, preferred_element_type=F32)
             total += lax.dot_general(crossed, picked[i][...].astype(BF16), NT, preferred_element_type=F32)
             out_ref[:, pl.ds(inside, TILE)] = total.astype(BF16)
         return carry
@@ -284,25 +292,26 @@
     lax.fori_loop(0, turns, some, 0)
 
 
-def finish(where, col_mirror, slot, own, sums, owned, half):
-    cols = len(sums) + 1
+def finish(where, col_mirror, slot, sums, spans, cols, owned, half):
     slab = col_mirror.shape[0]
     pairs = slot.shape[1]
     run, turns = runs_of(slab)
     block = run * turns * TILE
-    lanes = pl.cdiv(len(sums) * owned * half, 128) * 128
+    lanes = pl.cdiv((cols - 1) * owned * half, 128) * 128
     return pl.pallas_call(
-        functools.partial(finish_kernel, cols, owned, half, run, turns),
+        functools.partial(finish_kernel, cols, owned, half, run, turns, spans),
         grid_spec=pltpu.PrefetchScalarGridSpec(
             num_scalar_prefetch=2,
             grid=(slab // block,),
-            in_specs=[
-                pl.BlockSpec((1, pairs), lambda s, w, m: (0, 0)),
-                pl.BlockSpec((own.shape[0], block), lambda s, w, m: (0, s)),
+            in_specs=[pl.BlockSpec((1, pairs), lambda s, w, m: (0, 0))]
+            + [pl.BlockSpec(memory_space=pl.ANY)] * len(sums),
+            out_specs=pl.BlockSpec((pairs, block), lambda s, w, m: (0, s)),
+            scratch_shapes=[
+                pltpu.VMEM(((cols + 1) * owned * half, slab), BF16),
+                pltpu.VMEM((slab, lanes), F32),
+                pltpu.SemaphoreType.DMA((len(sums),)),
             ]
-            + [pl.BlockSpec((owned * half, slab), lambda s, w, m: (0, 0))] * len(sums),
-            out_specs=pl.BlockSpec((pairs, block), lambda s, w, m: (0, s)),
-            scratch_shapes=[pltpu.VMEM((slab, lanes), F32)] + [pltpu.VMEM((TILE, lanes), F32)] * run,
+            + [pltpu.VMEM((TILE, lanes), F32)] * run,
         ),
         out_shape=jax.ShapeDtypeStruct((pairs, slab), BF16),
         compiler_params=params(),
@@ -310,7 +319,7 @@
             flops=2 * pairs * 256 * slab + 40000 * slab, bytes_accessed=8 * slab * lanes, transcendentals=0
         ),
         name="finish",
-    )(where, col_mirror, slot, own, *sums)
+    )(where, col_mirror, slot, *sums)
 
 
 def swap(array, axis, offset):
@@ -404,7 +413,13 @@
         parts.append(part)
 
     sums = {}
-    totals, last = (), ()
+    results, totals, last, behind = (), (), (), []
+    block = TILE * math.prod(runs_of(col_mirror.shape[0]))
+    blocks = col_mirror.shape[0] // block
+    cuts = []
+    for n in range(turns):
+        cut = (2 if n + 1 < turns else 3) * blocks // 5
+        cuts.append([part for part in ((0, cut), (cut, blocks - cut)) if part[1]])
     for n, (batch, part) in enumerate(zip(batches, parts)):
         if n + 1 < turns:
             pieces = list(part)
@@ -414,17 +429,27 @@
             last = pieces[2:]
             places = [(o, 0) if o < 2 else (o // 2 + 1, o % 2) for o in range(rows)]
         else:
-            far = sorted(range(1, rows), key=lambda o: (-(o >> 1).bit_count(), -o))
+            far = sorted(range(1, rows), key=lambda o: (-(o >> 1).bit_count(), -(o % 2), -o))
             pieces = list(part)
             for m, o in enumerate(far):
-                early = [*totals, *(pieces[f] for f in far[:2])] if m >= len(far) - 2 else last
+                early = last
+                if m >= len(far) - 3:
+                    early = [*results[:1], *(totals if m == len(far) - 1 else ())]
                 pieces[o] = swap(after([pieces[o]], early)[0], "row", o)
             places = [(o, None) for o in range(rows)]
-        totals = symmetrize(where, col_mirror, pieces, places, batch, owned, half)
-        for k, total in zip(batch, totals):
-            sums[k] = total if k == 0 else swap(total, "col", k)
-        totals = totals[:1]
-    return finish(where, col_mirror, slot, sums[0], [sums[k] for k in range(1, cols)], owned, half)
+        results, totals = [], []
+        for m, (first, count) in enumerate(cuts[n]):
+            (turn,) = after([where], [*results[:1], *(behind if m else ())])
+            results = symmetrize(turn, col_mirror, pieces, places, batch, owned, half, first, count)
+            for k, total in zip(batch, results):
+                sums[k, m] = total if k == 0 else swap(total, "col", k)
+                if k and not m:
+                    totals.append(sums[k, m])
+        behind = [sums[k, len(cuts[n]) - 1] for k in batch if k]
+    spans = {k: [(a * block, b * block) for a, b in cuts[n]] for n, batch in enumerate(batches) for k in batch}
+    keys = sorted(sums)
+    spans = [(k, *spans[k][m]) for k, m in keys]
+    return finish(where, col_mirror, slot, [sums[key] for key in keys], spans, cols, owned, half)
 
 
 def solution(mesh):

time: 206 us -> 203 us (0.985)
  waiting for transfers between devices: 84 us -> 77.6 us
  Pallas kernels: 71.2 us -> 76.6 us
    ppermute x34 -> x37, waiting for transfers between devices: 84 us -> 77.6 us  [swap(): lax.ppermute(array, axis, [(i, i ^ offset) for i in range(lax.axis_size(a...]
    pallas_call x2 -> x4, Pallas kernels: 25.3 us -> 30 us  [symmetrize(): pl.pallas_call(functools.partial(symmetrize_kernel, places, len(parts), c...]
    ppermute x34 -> x37, starting transfers between devices: 44.3 us -> 42.4 us  [swap(): lax.ppermute(array, axis, [(i, i ^ offset) for i in range(lax.axis_size(a...]
  transfers between devices with their start and end apart: 34 -> 37, of which waited for: 14 -> 15; matrix products, arithmetic and copies ran while one was open for 0% -> 0% of each run, Pallas kernels for 27% -> 30%
where the time goes in v4:
time: 203 us
  waiting for transfers between devices  77.6 us (38%)
  Pallas kernels  76.6 us (38%)
  starting transfers between devices  42.4 us (21%)
  local copies, waits for them, and re-layouts  5.16 us (3%)
    ppermute x37, waiting for transfers between devices, swap(): lax.ppermute(array, axis, [(i, i ^ offset) for i in range(lax.axis_size(a...  77.6 us
    ppermute x37, starting transfers between devices, swap(): lax.ppermute(array, axis, [(i, i ^ offset) for i in range(lax.axis_size(a...  42.4 us
    pallas_call x2, Pallas kernels, product(): pl.pallas_call(functools.partial(product_kernel, holders, chunk_count, ow...  31 us
    pallas_call x4, Pallas kernels, symmetrize(): pl.pallas_call(functools.partial(symmetrize_kernel, places, len(parts), c...  30 us
    pallas_call x1, Pallas kernels, finish(): pl.pallas_call(functools.partial(finish_kernel, cols, owned, half, run, t...  14.4 us
    unnamed x51, local copies, waits for them, and re-layouts  4.89 us
  transfers between devices with their start and end apart: 37, of which 15 were waited for; matrix products, arithmetic and copies ran while one was open for 0% of the time, Pallas kernels for 30%

profile of v4, /device:TPU:0, one launch (start us, length us, event | category | flops | bytes accessed | tf_op | source)
XLA Modules:
  0.0 202.6 jit_solution(17441279376371501311)
XLA Ops:
  0.0 0.1 pad_add_fusion.where_ref
  0.1 1.1 copy-done.3
  1.2 0.7 copy-done.4
  1.9 0.7 copy-done.5
  2.5 1.2 pack.1
  3.7 4.0 %collective-permute-start.2 = (bf16[64,3072]{1,0:T(8,128)(2,1)S(1)}, bf16[64,3072]{1,0:T(8,128)(2,1)S(1)}, u32[]{:S(2)}, u32[]{:S(2)}) collective-permute-start(bf16[64,3072]{1,0:T(8,128)(2,1)S(1)} %get-tuple-element.52), channel_id=1, source_target_pairs={{0,24},{4,28},{8,16},{12,20},{16,8},{20,12},{24,0},{28,4},{1,25},{... | collective-permute-start | bytes 1179656 | tf_op jit(solution)/shard_map/ppermute | solution.py:326
  7.7 1.6 collective-permute-start.5
  9.3 2.6 %collective-permute-start.4 = (bf16[64,3072]{1,0:T(8,128)(2,1)S(1)}, bf16[64,3072]{1,0:T(8,128)(2,1)S(1)}, u32[]{:S(2)}, u32[]{:S(2)}) collective-permute-start(bf16[64,3072]{1,0:T(8,128)(2,1)S(1)} %get-tuple-element.53), channel_id=1, source_target_pairs={{0,2},{1,3},{2,0},{3,1},{4,6},{5,7},{6,4},{7,5},{8,10},{9,11},{10,... | collective-permute-start | bytes 1179656 | tf_op jit(solution)/shard_map/ppermute | solution.py:326
  11.9 0.5 collective-permute-start
  12.4 0.5 collective-permute-start.1
  12.9 4.7 %collective-permute-done.2 = bf16[64,3072]{1,0:T(8,128)(2,1)S(1)} collective-permute-done((bf16[64,3072]{1,0:T(8,128)(2,1)S(1)}, bf16[64,3072]{1,0:T(8,128)(2,1)S(1)}, u32[]{:S(2)}, u32[]{:S(2)}) %collective-permute-start.2) | collective-permute-done | bytes 393248 | tf_op jit(solution)/shard_map/ppermute | solution.py:326
  17.7 8.9 %collective-permute-done.5 = bf16[64,3072]{1,0:T(8,128)(2,1)S(1)} collective-permute-done((bf16[64,3072]{1,0:T(8,128)(2,1)S(1)}, bf16[64,3072]{1,0:T(8,128)(2,1)S(1)}, u32[]{:S(2)}, u32[]{:S(2)}) %collective-permute-start.5) | collective-permute-done | bytes 393248 | tf_op jit(solution)/shard_map/ppermute | solution.py:326
  26.6 2.4 %collective-permute-done.4 = bf16[64,3072]{1,0:T(8,128)(2,1)S(1)} collective-permute-done((bf16[64,3072]{1,0:T(8,128)(2,1)S(1)}, bf16[64,3072]{1,0:T(8,128)(2,1)S(1)}, u32[]{:S(2)}, u32[]{:S(2)}) %collective-permute-start.4) | collective-permute-done | bytes 393248 | tf_op jit(solution)/shard_map/ppermute | solution.py:326
  28.9 0.5 collective-permute-start.9
  29.4 1.5 collective-permute-start.6
  30.9 1.5 collective-permute-start.7
  32.4 2.5 %collective-permute-start.10 = (bf16[64,3072]{1,0:T(8,128)(2,1)S(1)}, bf16[64,3072]{1,0:T(8,128)(2,1)S(1)}, u32[]{:S(2)}, u32[]{:S(2)}) collective-permute-start(bf16[64,3072]{1,0:T(8,128)(2,1)S(1)} %get-tuple-element.57), channel_id=1, source_target_pairs={{0,3},{1,2},{2,1},{3,0},{4,7},{5,6},{6,5},{7,4},{8,11},{9,10},{10,... | collective-permute-start | bytes 1179656 | tf_op jit(solution)/shard_map/ppermute | solution.py:326
  35.0 0.1 collective-permute-start.3
  35.1 6.3 %collective-permute-done.9 = bf16[64,3072]{1,0:T(8,128)(2,1)S(1)} collective-permute-done((bf16[64,3072]{1,0:T(8,128)(2,1)S(1)}, bf16[64,3072]{1,0:T(8,128)(2,1)S(1)}, u32[]{:S(2)}, u32[]{:S(2)}) %collective-permute-start.9) | collective-permute-done | bytes 393248 | tf_op jit(solution)/shard_map/ppermute | solution.py:326
  41.5 0.7 collective-permute-done.10
  42.2 0.1 collective-permute-start.11
  42.3 2.4 %collective-permute-done.6 = bf16[64,3072]{1,0:T(8,128)(2,1)S(1)} collective-permute-done((bf16[64,3072]{1,0:T(8,128)(2,1)S(1)}, bf16[64,3072]{1,0:T(8,128)(2,1)S(1)}, u32[]{:S(2)}, u32[]{:S(2)}) %collective-permute-start.6) | collective-permute-done | bytes 393248 | tf_op jit(solution)/shard_map/ppermute | solution.py:326
  44.7 0.9 collective-permute-done.7
  45.6 0.1 collective-permute-start.8
  45.7 0.6 collective-permute-start.16
  46.3 0.7 collective-permute-start.17
  47.0 1.4 collective-permute-start.18
  48.4 1.4 collective-permute-start.19
  49.8 1.2 copy-done.11
  51.0 15.6 %ladder.2 = (bf16[4,1200,128]{2,1,0:T(8,128)(2,1)}, bf16[4,1200,128]{2,1,0:T(8,128)(2,1)}) custom-call(bf16[256,3072]{1,0:T(8,128)(2,1)} %copy-done.9, bf16[256,3072]{1,0:T(8,128)(2,1)} %copy-done.11, bf16[128,3072]{1,0:T(8,128)(2,1)} %copy-done.6, bf16[128,3072]{1,0:T(8,128)(2,1)} %copy-done.14, bf16[128,3072]{1,0:T(8,128)(2,1)} %copy-done.8, ...), custom_call_target="tpu_custom_call" | custom-call | flops 7549747200 | bytes 21037056 | tf_op jit(solution)/shard_map/ladder/pallas_call | solution.py:120
  66.7 0.7 collective-permute-start.22
  67.4 0.7 collective-permute-start.21
  68.4 0.6 collective-permute-start.20
  69.0 8.5 %collective-permute-done.21 = bf16[64,3072]{1,0:T(8,128)(2,1)S(1)} collective-permute-done((bf16[64,3072]{1,0:T(8,128)(2,1)S(1)}, bf16[64,3072]{1,0:T(8,128)(2,1)S(1)}, u32[]{:S(2)}, u32[]{:S(2)}) %collective-permute-start.21) | collective-permute-done | bytes 393248 | tf_op jit(solution)/shard_map/ppermute | solution.py:326
  77.6 0.1 collective-permute-start.23
  77.8 1.6 collective-permute-start.15
  79.4 1.4 collective-permute-start.14
  80.9 0.7 collective-permute-start.13
  81.6 0.9 copy-done.12
  82.5 15.4 %ladder.3 = (bf16[1200,128]{1,0:T(8,128)(2,1)}, bf16[1200,128]{1,0:T(8,128)(2,1)}, bf16[1200,128]{1,0:T(8,128)(2,1)}, bf16[1200,128]{1,0:T(8,128)(2,1)}, bf16[12...) custom-call(bf16[384,3072]{1,0:T(8,128)(2,1)} %copy-done.10, ...), custom_call_target="tpu_custom_call" | custom-call | flops 7549747200 | bytes 21037056 | tf_op jit(solution)/shard_map/ladder/pallas_call | solution.py:120
  98.0 10.2 %collective-permute-done.14.refs_3_ = bf16[2,1200,128]{2,1,0:T(8,128)(2,1)S(1)} collective-permute-done((bf16[2,1200,128]{2,1,0:T(8,128)(2,1)S(1)}, bf16[2,1200,128]{2,1,0:T(8,128)(2,1)S(1)}, u32[]{:S(2)}, u32[]{:S(2)}) %collective-permute-start.14) | collective-permute-done | bytes 614432 | tf_op jit(solution)/shard_map/ppermute | solution.py:326
  108.2 1.2 collective-permute-start.31
  109.3 1.4 collective-permute-start.30
  110.8 6.4 %symmetrize.4 = (bf16[64,3840]{1,0:T(8,128)(2,1)S(1)}, bf16[32,3840]{1,0:T(8,128)(2,1)S(1)}) custom-call(s32[2]{0:T(128)S(1)} %pad_add_fusion.where_ref, s32[9600]{0:T(1024)S(1)} %copy-done.2, bf16[4,1200,128]{2,1,0:T(8,128)(2,1)S(1)} %copy-done, bf16[4,1200,128]{2,1,0:T(8,128)(2,1)S(1)} %collective-permute-done.12.refs_1_, ...), custom_call_target="tpu_custom_call" | custom-call | flops 342343680 | bytes 1228800 | tf_op jit(solution)/shard_map/symmetrize/pallas_call | solution.py:212
  117.2 4.8 %collective-permute-start.24 = (bf16[32,3840]{1,0:T(8,128)(2,1)S(1)}, bf16[32,3840]{1,0:T(8,128)(2,1)S(1)}, u32[]{:S(2)}, u32[]{:S(2)}) collective-permute-start(bf16[32,3840]{1,0:T(8,128)(2,1)S(1)} %get-tuple-element.77), channel_id=1, source_target_pairs={{0,2},{1,3},{2,0},{3,1},{4,6},{5,7},{6,4},{7,5},{8,10},{9,11},{10,... | collective-permute-start | bytes 737288 | tf_op jit(solution)/shard_map/ppermute | solution.py:326
  122.0 1.0 collective-permute-start.29
  123.0 8.5 %symmetrize.5 = (bf16[64,5760]{1,0:T(8,128)(2,1)S(1)}, bf16[32,5760]{1,0:T(8,128)(2,1)S(1)}) custom-call(s32[2]{0:T(128)S(1)} %pad_add_fusion.where_ref, s32[9600]{0:T(1024)S(1)} %copy-done.2, bf16[4,1200,128]{2,1,0:T(8,128)(2,1)S(1)} %copy-done, bf16[4,1200,128]{2,1,0:T(8,128)(2,1)S(1)} %collective-permute-done.12.refs_1_, ...), custom_call_target="tpu_custom_call" | custom-call | flops 513515520 | bytes 1228800 | tf_op jit(solution)/shard_map/symmetrize/pallas_call | solution.py:212
  131.5 0.7 collective-permute-start.28
  132.2 1.5 collective-permute-done.24.refs_4_
  133.7 0.8 collective-permute-start.27
  134.4 0.7 collective-permute-start.26
  135.1 0.4 collective-permute-start.25
  135.5 1.2 collective-permute-start.33
  136.8 4.6 %collective-permute-done.28.refs_4_ = bf16[1200,128]{1,0:T(8,128)(2,1)S(1)} collective-permute-done((bf16[1200,128]{1,0:T(8,128)(2,1)S(1)}, bf16[1200,128]{1,0:T(8,128)(2,1)S(1)}, u32[]{:S(2)}, u32[]{:S(2)}) %collective-permute-start.28) | collective-permute-done | bytes 307232 | tf_op jit(solution)/shard_map/ppermute | solution.py:326
  141.4 1.9 collective-permute-done.27.refs_3_
  143.2 6.5 %collective-permute-done.26.refs_2_ = bf16[1200,128]{1,0:T(8,128)(2,1)S(1)} collective-permute-done((bf16[1200,128]{1,0:T(8,128)(2,1)S(1)}, bf16[1200,128]{1,0:T(8,128)(2,1)S(1)}, u32[]{:S(2)}, u32[]{:S(2)}) %collective-permute-start.26) | collective-permute-done | bytes 307232 | tf_op jit(solution)/shard_map/ppermute | solution.py:326
  149.7 8.7 %symmetrize.6 = (bf16[32,5760]{1,0:T(8,128)(2,1)S(1)}, bf16[32,5760]{1,0:T(8,128)(2,1)S(1)}) custom-call(s32[2]{0:T(128)S(1)} %pad_add_fusion.where_ref, s32[9600]{0:T(1024)S(1)} %copy-done.2, bf16[1200,128]{1,0:T(8,128)(2,1)S(1)} %copy-done.1, bf16[1200,128]{1,0:T(8,128)(2,1)S(1)} %collective-permute-done.25.refs_1_, ...), custom_call_target="tpu_custom_call" | custom-call | flops 419143680 | bytes 1228800 | tf_op jit(solution)/shard_map/symmetrize/pallas_call | solution.py:212
  158.5 2.1 %collective-permute-start.35 = (bf16[32,5760]{1,0:T(8,128)(2,1)S(1)}, bf16[32,5760]{1,0:T(8,128)(2,1)S(1)}, u32[]{:S(2)}, u32[]{:S(2)}) collective-permute-start(bf16[32,5760]{1,0:T(8,128)(2,1)S(1)} %get-tuple-element.95), channel_id=1, source_target_pairs={{0,3},{1,2},{2,1},{3,0},{4,7},{5,6},{6,5},{7,4},{8,11},{9,10},{10,... | collective-permute-start | bytes 1105928 | tf_op jit(solution)/shard_map/ppermute | solution.py:326
  160.6 6.4 %symmetrize.7 = (bf16[32,3840]{1,0:T(8,128)(2,1)S(1)}, bf16[32,3840]{1,0:T(8,128)(2,1)S(1)}) custom-call(s32[2]{0:T(128)S(1)} %pad_add_fusion.where_ref, s32[9600]{0:T(1024)S(1)} %copy-done.2, bf16[1200,128]{1,0:T(8,128)(2,1)S(1)} %copy-done.1, bf16[1200,128]{1,0:T(8,128)(2,1)S(1)} %collective-permute-done.25.refs_1_, ...), custom_call_target="tpu_custom_call" | custom-call | flops 279429120 | bytes 1228800 | tf_op jit(solution)/shard_map/symmetrize/pallas_call | solution.py:212
  167.1 1.1 collective-permute-start.34
  168.2 1.7 collective-permute-start.36
  169.9 12.8 %collective-permute-done.34.refs_3_ = bf16[32,3840]{1,0:T(8,128)(2,1)S(1)} collective-permute-done((bf16[32,3840]{1,0:T(8,128)(2,1)S(1)}, bf16[32,3840]{1,0:T(8,128)(2,1)S(1)}, u32[]{:S(2)}, u32[]{:S(2)}) %collective-permute-start.34) | collective-permute-done | bytes 245792 | tf_op jit(solution)/shard_map/ppermute | solution.py:326
  182.7 5.3 %collective-permute-done.36.refs_7_ = bf16[32,3840]{1,0:T(8,128)(2,1)S(1)} collective-permute-done((bf16[32,3840]{1,0:T(8,128)(2,1)S(1)}, bf16[32,3840]{1,0:T(8,128)(2,1)S(1)}, u32[]{:S(2)}, u32[]{:S(2)}) %collective-permute-start.36) | collective-permute-done | bytes 245792 | tf_op jit(solution)/shard_map/ppermute | solution.py:326
  188.1 14.4 %finish.1 = bf16[128,9600]{1,0:T(8,128)(2,1)} custom-call(s32[2]{0:T(128)S(1)} %pad_add_fusion.where_ref, s32[9600]{0:T(1024)S(1)} %copy-done.2, s32[1,128]{1,0:T(1,128)S(1)} %get-tuple-element.51.slot_ref, bf16[64,3840]{1,0:T(8,128)(2,1)S(1)} %get-tuple-element.62.refs_0_, bf16[64,5760]{1,0:T(8,128)(2,1)S(1)} %get-tuple-element.64.refs_1_, ...), custom_call_target="tpu_custom_call" | custom-call | flops 1013145600 | bytes 9830400 | tf_op jit(solution)/shard_map/finish/pallas_call | solution.py:301
  (80 shorter events, 1.0 us)
Async XLA Ops:
  0.1 1.1 copy-start.3
  1.2 0.7 copy-start.4
  1.9 0.7 copy-start.5
  3.7 13.9 %collective-permute-start.2 = (bf16[64,3072]{1,0:T(8,128)(2,1)S(1)}, bf16[64,3072]{1,0:T(8,128)(2,1)S(1)}, u32[]{:S(2)}, u32[]{:S(2)}) collective-permute-start(bf16[64,3072]{1,0:T(8,128)(2,1)S(1)} %get-tuple-element.52), channel_id=1, source_target_pairs={{0,24},{4,28},{8,16},{12,20},{16,8},{20,12},{24,0},{28,4},{1,25},{... | collective-permute-start | bytes 1179656 | tf_op jit(solution)/shard_map/ppermute | solution.py:326
  7.7 18.9 %collective-permute-start.5 = (bf16[64,3072]{1,0:T(8,128)(2,1)S(1)}, bf16[64,3072]{1,0:T(8,128)(2,1)S(1)}, u32[]{:S(2)}, u32[]{:S(2)}) collective-permute-start(bf16[64,3072]{1,0:T(8,128)(2,1)S(1)} %get-tuple-element.54), channel_id=1, source_target_pairs={{0,1},{1,0},{2,3},{3,2},{4,5},{5,4},{6,7},{7,6},{8,9},{9,8},{10,11... | collective-permute-start | bytes 1179656 | tf_op jit(solution)/shard_map/ppermute | solution.py:326
  9.3 19.7 %collective-permute-start.4 = (bf16[64,3072]{1,0:T(8,128)(2,1)S(1)}, bf16[64,3072]{1,0:T(8,128)(2,1)S(1)}, u32[]{:S(2)}, u32[]{:S(2)}) collective-permute-start(bf16[64,3072]{1,0:T(8,128)(2,1)S(1)} %get-tuple-element.53), channel_id=1, source_target_pairs={{0,2},{1,3},{2,0},{3,1},{4,6},{5,7},{6,4},{7,5},{8,10},{9,11},{10,... | collective-permute-start | bytes 1179656 | tf_op jit(solution)/shard_map/ppermute | solution.py:326
  11.9 20.6 %collective-permute-start = (bf16[64,3072]{1,0:T(8,128)(2,1)S(1)}, bf16[64,3072]{1,0:T(8,128)(2,1)S(1)}, u32[]{:S(2)}, u32[]{:S(2)}) collective-permute-start(bf16[64,3072]{1,0:T(8,128)(2,1)S(1)} %get-tuple-element.52), channel_id=1, source_target_pairs={{0,8},{4,12},{8,0},{12,4},{16,24},{20,28},{24,16},{28,20},{1,9},{5... | collective-permute-start | bytes 1179656 | tf_op jit(solution)/shard_map/ppermute | solution.py:326
  12.4 22.5 %collective-permute-start.1 = (bf16[64,3072]{1,0:T(8,128)(2,1)S(1)}, bf16[64,3072]{1,0:T(8,128)(2,1)S(1)}, u32[]{:S(2)}, u32[]{:S(2)}) collective-permute-start(bf16[64,3072]{1,0:T(8,128)(2,1)S(1)} %get-tuple-element.52), channel_id=1, source_target_pairs={{0,16},{4,20},{8,24},{12,28},{16,0},{20,4},{24,8},{28,12},{1,17},{... | collective-permute-start | bytes 1179656 | tf_op jit(solution)/shard_map/ppermute | solution.py:326
  28.9 12.5 %collective-permute-start.9 = (bf16[64,3072]{1,0:T(8,128)(2,1)S(1)}, bf16[64,3072]{1,0:T(8,128)(2,1)S(1)}, u32[]{:S(2)}, u32[]{:S(2)}) collective-permute-start(bf16[64,3072]{1,0:T(8,128)(2,1)S(1)} %collective-permute-done.4), channel_id=1, source_target_pairs={{0,24},{4,28},{8,16},{12,20},{16,8},{20,12},{24,0},{28,4},{1,25},{... | collective-permute-start | bytes 1179656 | tf_op jit(solution)/shard_map/ppermute | solution.py:326
  29.4 15.2 %collective-permute-start.6 = (bf16[64,3072]{1,0:T(8,128)(2,1)S(1)}, bf16[64,3072]{1,0:T(8,128)(2,1)S(1)}, u32[]{:S(2)}, u32[]{:S(2)}) collective-permute-start(bf16[64,3072]{1,0:T(8,128)(2,1)S(1)} %collective-permute-done.4), channel_id=1, source_target_pairs={{0,8},{4,12},{8,0},{12,4},{16,24},{20,28},{24,16},{28,20},{1,9},{5... | collective-permute-start | bytes 1179656 | tf_op jit(solution)/shard_map/ppermute | solution.py:326
  30.9 14.7 %collective-permute-start.7 = (bf16[64,3072]{1,0:T(8,128)(2,1)S(1)}, bf16[64,3072]{1,0:T(8,128)(2,1)S(1)}, u32[]{:S(2)}, u32[]{:S(2)}) collective-permute-start(bf16[64,3072]{1,0:T(8,128)(2,1)S(1)} %collective-permute-done.4), channel_id=1, source_target_pairs={{0,16},{4,20},{8,24},{12,28},{16,0},{20,4},{24,8},{28,12},{1,17},{... | collective-permute-start | bytes 1179656 | tf_op jit(solution)/shard_map/ppermute | solution.py:326
  32.4 9.7 %collective-permute-start.10 = (bf16[64,3072]{1,0:T(8,128)(2,1)S(1)}, bf16[64,3072]{1,0:T(8,128)(2,1)S(1)}, u32[]{:S(2)}, u32[]{:S(2)}) collective-permute-start(bf16[64,3072]{1,0:T(8,128)(2,1)S(1)} %get-tuple-element.57), channel_id=1, source_target_pairs={{0,3},{1,2},{2,1},{3,0},{4,7},{5,6},{6,5},{7,4},{8,11},{9,10},{10,... | collective-permute-start | bytes 1179656 | tf_op jit(solution)/shard_map/ppermute | solution.py:326
  35.0 16.0 %copy-start.9 = (bf16[256,3072]{1,0:T(8,128)(2,1)}, bf16[256,3072]{1,0:T(8,128)(2,1)S(1)}, u32[]{:S(2)}) copy-start(bf16[256,3072]{1,0:T(8,128)(2,1)S(1)} %constant_dynamic-update-slice_fusion.refs_0_) | copy-start | bytes 4718596
  35.0 14.8 %collective-permute-start.3 = (bf16[256,3072]{1,0:T(8,128)(2,1)S(1)}, bf16[256,3072]{1,0:T(8,128)(2,1)S(1)}, u32[]{:S(2)}, u32[]{:S(2)}) collective-permute-start(bf16[256,3072]{1,0:T(8,128)(2,1)S(1)} %constant_dynamic-update-slice_fusion.refs_0_), channel_id=1, source_target_pairs={{0,4},{4,0},{8,12},{12,8},{16,20},{20,16},{24,28},{28,24},{1,5},{5... | collective-permute-start | bytes 4718600 | tf_op jit(solution)/shard_map/ppermute | solution.py:326
  42.2 8.8 %copy-start.8 = (bf16[128,3072]{1,0:T(8,128)(2,1)}, bf16[128,3072]{1,0:T(8,128)(2,1)S(1)}, u32[]{:S(2)}) copy-start(bf16[128,3072]{1,0:T(8,128)(2,1)S(1)} %constant_dynamic-update-slice_fusion.6.refs_4_) | copy-start | bytes 2359300
  42.2 4.8 %collective-permute-start.11 = (bf16[128,3072]{1,0:T(8,128)(2,1)S(1)}, bf16[128,3072]{1,0:T(8,128)(2,1)S(1)}, u32[]{:S(2)}, u32[]{:S(2)}) collective-permute-start(bf16[128,3072]{1,0:T(8,128)(2,1)S(1)} %constant_dynamic-update-slice_fusion.6.refs_4_), channel_id=1, source_target_pairs={{0,4},{4,0},{8,12},{12,8},{16,20},{20,16},{24,28},{28,24},{1,5},{5... | collective-permute-start | bytes 2359304 | tf_op jit(solution)/shard_map/ppermute | solution.py:326
  45.6 5.4 %copy-start.6 = (bf16[128,3072]{1,0:T(8,128)(2,1)}, bf16[128,3072]{1,0:T(8,128)(2,1)S(1)}, u32[]{:S(2)}) copy-start(bf16[128,3072]{1,0:T(8,128)(2,1)S(1)} %constant_dynamic-update-slice_fusion.4.refs_2_) | copy-start | bytes 2359300
  45.6 2.8 %collective-permute-start.8 = (bf16[128,3072]{1,0:T(8,128)(2,1)S(1)}, bf16[128,3072]{1,0:T(8,128)(2,1)S(1)}, u32[]{:S(2)}, u32[]{:S(2)}) collective-permute-start(bf16[128,3072]{1,0:T(8,128)(2,1)S(1)} %constant_dynamic-update-slice_fusion.4.refs_2_), channel_id=1, source_target_pairs={{0,4},{4,0},{8,12},{12,8},{16,20},{20,16},{24,28},{28,24},{1,5},{5... | collective-permute-start | bytes 2359304 | tf_op jit(solution)/shard_map/ppermute | solution.py:326
  45.7 21.7 %collective-permute-start.16 = (bf16[64,3072]{1,0:T(8,128)(2,1)S(1)}, bf16[64,3072]{1,0:T(8,128)(2,1)S(1)}, u32[]{:S(2)}, u32[]{:S(2)}) collective-permute-start(bf16[64,3072]{1,0:T(8,128)(2,1)S(1)} %collective-permute-done.5), channel_id=1, source_target_pairs={{0,8},{4,12},{8,0},{12,4},{16,24},{20,28},{24,16},{28,20},{1,9},{5... | collective-permute-start | bytes 1179656 | tf_op jit(solution)/shard_map/ppermute | solution.py:326
  46.3 21.1 %collective-permute-start.17 = (bf16[64,3072]{1,0:T(8,128)(2,1)S(1)}, bf16[64,3072]{1,0:T(8,128)(2,1)S(1)}, u32[]{:S(2)}, u32[]{:S(2)}) collective-permute-start(bf16[64,3072]{1,0:T(8,128)(2,1)S(1)} %collective-permute-done.5), channel_id=1, source_target_pairs={{0,16},{4,20},{8,24},{12,28},{16,0},{20,4},{24,8},{28,12},{1,17},{... | collective-permute-start | bytes 1179656 | tf_op jit(solution)/shard_map/ppermute | solution.py:326
  47.0 4.0 %copy-start.13 = (bf16[128,3072]{1,0:T(8,128)(2,1)}, bf16[128,3072]{1,0:T(8,128)(2,1)S(1)}, u32[]{:S(2)}) copy-start(bf16[128,3072]{1,0:T(8,128)(2,1)S(1)} %collective-permute-done.11.refs_5_) | copy-start | bytes 2359300
  47.0 19.6 %collective-permute-start.18 = (bf16[64,3072]{1,0:T(8,128)(2,1)S(1)}, bf16[64,3072]{1,0:T(8,128)(2,1)S(1)}, u32[]{:S(2)}, u32[]{:S(2)}) collective-permute-start(bf16[64,3072]{1,0:T(8,128)(2,1)S(1)} %collective-permute-done.10), channel_id=1, source_target_pairs={{0,8},{4,12},{8,0},{12,4},{16,24},{20,28},{24,16},{28,20},{1,9},{5... | collective-permute-start | bytes 1179656 | tf_op jit(solution)/shard_map/ppermute | solution.py:326
  48.4 2.6 %copy-start.14 = (bf16[128,3072]{1,0:T(8,128)(2,1)}, bf16[128,3072]{1,0:T(8,128)(2,1)S(1)}, u32[]{:S(2)}) copy-start(bf16[128,3072]{1,0:T(8,128)(2,1)S(1)} %collective-permute-done.8.refs_3_) | copy-start | bytes 2359300
  48.4 18.2 %collective-permute-start.19 = (bf16[64,3072]{1,0:T(8,128)(2,1)S(1)}, bf16[64,3072]{1,0:T(8,128)(2,1)S(1)}, u32[]{:S(2)}, u32[]{:S(2)}) collective-permute-start(bf16[64,3072]{1,0:T(8,128)(2,1)S(1)} %collective-permute-done.10), channel_id=1, source_target_pairs={{0,16},{4,20},{8,24},{12,28},{16,0},{20,4},{24,8},{28,12},{1,17},{... | collective-permute-start | bytes 1179656 | tf_op jit(solution)/shard_map/ppermute | solution.py:326
  49.8 1.2 copy-start.11
  66.7 2.2 %copy-start = (bf16[4,1200,128]{2,1,0:T(8,128)(2,1)S(1)}, bf16[4,1200,128]{2,1,0:T(8,128)(2,1)}, u32[]{:S(2)}) copy-start(bf16[4,1200,128]{2,1,0:T(8,128)(2,1)} %get-tuple-element.60.refs_0_) | copy-start | bytes 3686404
  66.7 10.8 %collective-permute-start.22 = (bf16[64,3072]{1,0:T(8,128)(2,1)S(1)}, bf16[64,3072]{1,0:T(8,128)(2,1)S(1)}, u32[]{:S(2)}, u32[]{:S(2)}) collective-permute-start(bf16[64,3072]{1,0:T(8,128)(2,1)S(1)} %collective-permute-done.19), channel_id=1, source_target_pairs={{0,8},{4,12},{8,0},{12,4},{16,24},{20,28},{24,16},{28,20},{1,9},{5... | collective-permute-start | bytes 1179656 | tf_op jit(solution)/shard_map/ppermute | solution.py:326
  67.4 10.1 %collective-permute-start.21 = (bf16[64,3072]{1,0:T(8,128)(2,1)S(1)}, bf16[64,3072]{1,0:T(8,128)(2,1)S(1)}, u32[]{:S(2)}, u32[]{:S(2)}) collective-permute-start(bf16[64,3072]{1,0:T(8,128)(2,1)S(1)} %collective-permute-done.16), channel_id=1, source_target_pairs={{0,16},{4,20},{8,24},{12,28},{16,0},{20,4},{24,8},{28,12},{1,17},{... | collective-permute-start | bytes 1179656 | tf_op jit(solution)/shard_map/ppermute | solution.py:326
  68.1 9.5 %collective-permute-start.12 = (bf16[4,1200,128]{2,1,0:T(8,128)(2,1)}, bf16[4,1200,128]{2,1,0:T(8,128)(2,1)S(1)}, u32[]{:S(2)}, u32[]{:S(2)}) collective-permute-start(bf16[4,1200,128]{2,1,0:T(8,128)(2,1)} %get-tuple-element.61), channel_id=1, source_target_pairs={{0,4},{4,0},{8,12},{12,8},{16,20},{20,16},{24,28},{28,24},{1,5},{5... | collective-permute-start | bytes 3686408 | tf_op jit(solution)/shard_map/ppermute | solution.py:326
  68.3 9.4 %copy-start.10 = (bf16[384,3072]{1,0:T(8,128)(2,1)}, bf16[384,3072]{1,0:T(8,128)(2,1)S(1)}, u32[]{:S(2)}) copy-start(bf16[384,3072]{1,0:T(8,128)(2,1)S(1)} %constant_dynamic-update-slice_fusion.8.refs_0_) | copy-start | bytes 7077892
  68.4 13.3 %collective-permute-start.20 = (bf16[384,3072]{1,0:T(8,128)(2,1)S(1)}, bf16[384,3072]{1,0:T(8,128)(2,1)}, u32[]{:S(2)}, u32[]{:S(2)}) collective-permute-start(bf16[384,3072]{1,0:T(8,128)(2,1)S(1)} %constant_dynamic-update-slice_fusion.8.refs_0_), channel_id=1, source_target_pairs={{0,4},{4,0},{8,12},{12,8},{16,20},{20,16},{24,28},{28,24},{1,5},{5... | collective-permute-start | bytes 7077896 | tf_op jit(solution)/shard_map/ppermute | solution.py:326
  77.6 3.3 %copy-start.7 = (bf16[128,3072]{1,0:T(8,128)(2,1)}, bf16[128,3072]{1,0:T(8,128)(2,1)S(1)}, u32[]{:S(2)}) copy-start(bf16[128,3072]{1,0:T(8,128)(2,1)S(1)} %constant_dynamic-update-slice_fusion.14.refs_2_) | copy-start | bytes 2359300
  77.6 4.1 %collective-permute-start.23 = (bf16[128,3072]{1,0:T(8,128)(2,1)S(1)}, bf16[128,3072]{1,0:T(8,128)(2,1)S(1)}, u32[]{:S(2)}, u32[]{:S(2)}) collective-permute-start(bf16[128,3072]{1,0:T(8,128)(2,1)S(1)} %constant_dynamic-update-slice_fusion.14.refs_2_), channel_id=1, source_target_pairs={{0,4},{4,0},{8,12},{12,8},{16,20},{20,16},{24,28},{28,24},{1,5},{5... | collective-permute-start | bytes 2359304 | tf_op jit(solution)/shard_map/ppermute | solution.py:326
  77.8 20.2 %collective-permute-start.15 = (bf16[2,1200,128]{2,1,0:T(8,128)(2,1)S(1)}, bf16[2,1200,128]{2,1,0:T(8,128)(2,1)S(1)}, u32[]{:S(2)}, u32[]{:S(2)}) collective-permute-start(bf16[2,1200,128]{2,1,0:T(8,128)(2,1)S(1)} %pad_maximum_fusion.2), channel_id=1, source_target_pairs={{0,24},{4,28},{8,16},{12,20},{16,8},{20,12},{24,0},{28,4},{1,25},{... | collective-permute-start | bytes 1843208 | tf_op jit(solution)/shard_map/ppermute | solution.py:326
  79.4 28.7 %collective-permute-start.14 = (bf16[2,1200,128]{2,1,0:T(8,128)(2,1)S(1)}, bf16[2,1200,128]{2,1,0:T(8,128)(2,1)S(1)}, u32[]{:S(2)}, u32[]{:S(2)}) collective-permute-start(bf16[2,1200,128]{2,1,0:T(8,128)(2,1)S(1)} %pad_maximum_fusion.1), channel_id=1, source_target_pairs={{0,16},{4,20},{8,24},{12,28},{16,0},{20,4},{24,8},{28,12},{1,17},{... | collective-permute-start | bytes 1843208 | tf_op jit(solution)/shard_map/ppermute | solution.py:326
  80.9 29.9 %copy-start.2 = (s32[9600]{0:T(1024)S(1)}, s32[9600]{0:T(1024)}, u32[]{:S(2)}) copy-start(s32[9600]{0:T(1024)} %mirror_ref.9) | copy-start | bytes 115204
  80.9 27.3 %collective-permute-start.13 = (bf16[2,1200,128]{2,1,0:T(8,128)(2,1)S(1)}, bf16[2,1200,128]{2,1,0:T(8,128)(2,1)S(1)}, u32[]{:S(2)}, u32[]{:S(2)}) collective-permute-start(bf16[2,1200,128]{2,1,0:T(8,128)(2,1)S(1)} %pad_maximum_fusion), channel_id=1, source_target_pairs={{0,8},{4,12},{8,0},{12,4},{16,24},{20,28},{24,16},{28,20},{1,9},{5... | collective-permute-start | bytes 1843208 | tf_op jit(solution)/shard_map/ppermute | solution.py:326
  81.6 0.9 copy-start.12
  98.0 24.0 %copy-start.19 = (bf16[1200,128]{1,0:T(8,128)(2,1)S(1)}, bf16[1200,128]{1,0:T(8,128)(2,1)}, u32[]{:S(2)}) copy-start(bf16[1200,128]{1,0:T(8,128)(2,1)} %get-tuple-element.86) | copy-start | bytes 921604
  108.2 26.2 %collective-permute-start.31 = (bf16[1200,128]{1,0:T(8,128)(2,1)}, bf16[1200,128]{1,0:T(8,128)(2,1)S(1)}, u32[]{:S(2)}, u32[]{:S(2)}) collective-permute-start(bf16[1200,128]{1,0:T(8,128)(2,1)} %get-tuple-element.90), channel_id=1, source_target_pairs={{0,28},{4,24},{8,20},{12,16},{16,12},{20,8},{24,4},{28,0},{1,29},{... | collective-permute-start | bytes 921608 | tf_op jit(solution)/shard_map/ppermute | solution.py:326
  109.3 25.8 %collective-permute-start.30 = (bf16[1200,128]{1,0:T(8,128)(2,1)}, bf16[1200,128]{1,0:T(8,128)(2,1)S(1)}, u32[]{:S(2)}, u32[]{:S(2)}) collective-permute-start(bf16[1200,128]{1,0:T(8,128)(2,1)} %get-tuple-element.88), channel_id=1, source_target_pairs={{0,24},{4,28},{8,16},{12,20},{16,8},{20,12},{24,0},{28,4},{1,25},{... | collective-permute-start | bytes 921608 | tf_op jit(solution)/shard_map/ppermute | solution.py:326
  117.2 14.3 %copy-start.18 = (bf16[1200,128]{1,0:T(8,128)(2,1)S(1)}, bf16[1200,128]{1,0:T(8,128)(2,1)}, u32[]{:S(2)}) copy-start(bf16[1200,128]{1,0:T(8,128)(2,1)} %get-tuple-element.84) | copy-start | bytes 921604
  117.2 16.5 %copy-start.17 = (bf16[1200,128]{1,0:T(8,128)(2,1)S(1)}, bf16[1200,128]{1,0:T(8,128)(2,1)}, u32[]{:S(2)}) copy-start(bf16[1200,128]{1,0:T(8,128)(2,1)} %get-tuple-element.82) | copy-start | bytes 921604
  117.2 17.2 %copy-start.16 = (bf16[1200,128]{1,0:T(8,128)(2,1)S(1)}, bf16[1200,128]{1,0:T(8,128)(2,1)}, u32[]{:S(2)}) copy-start(bf16[1200,128]{1,0:T(8,128)(2,1)} %get-tuple-element.80) | copy-start | bytes 921604
  117.2 17.9 %copy-start.15 = (bf16[1200,128]{1,0:T(8,128)(2,1)S(1)}, bf16[1200,128]{1,0:T(8,128)(2,1)}, u32[]{:S(2)}) copy-start(bf16[1200,128]{1,0:T(8,128)(2,1)} %get-tuple-element.78) | copy-start | bytes 921604
  117.2 32.5 %copy-start.1 = (bf16[1200,128]{1,0:T(8,128)(2,1)S(1)}, bf16[1200,128]{1,0:T(8,128)(2,1)}, u32[]{:S(2)}) copy-start(bf16[1200,128]{1,0:T(8,128)(2,1)} %get-tuple-element.75.refs_0_) | copy-start | bytes 921604
  117.2 16.4 %collective-permute-start.24 = (bf16[32,3840]{1,0:T(8,128)(2,1)S(1)}, bf16[32,3840]{1,0:T(8,128)(2,1)S(1)}, u32[]{:S(2)}, u32[]{:S(2)}) collective-permute-start(bf16[32,3840]{1,0:T(8,128)(2,1)S(1)} %get-tuple-element.77), channel_id=1, source_target_pairs={{0,2},{1,3},{2,0},{3,1},{4,6},{5,7},{6,4},{7,5},{8,10},{9,11},{10,... | collective-permute-start | bytes 737288 | tf_op jit(solution)/shard_map/ppermute | solution.py:326
  122.0 13.5 %collective-permute-start.29 = (bf16[1200,128]{1,0:T(8,128)(2,1)S(1)}, bf16[1200,128]{1,0:T(8,128)(2,1)S(1)}, u32[]{:S(2)}, u32[]{:S(2)}) collective-permute-start(bf16[1200,128]{1,0:T(8,128)(2,1)S(1)} %copy-done.19), channel_id=1, source_target_pairs={{0,20},{4,16},{8,28},{12,24},{16,4},{20,0},{24,12},{28,8},{1,21},{... | collective-permute-start | bytes 921608 | tf_op jit(solution)/shard_map/ppermute | solution.py:326
  131.5 9.8 %collective-permute-start.28 = (bf16[1200,128]{1,0:T(8,128)(2,1)S(1)}, bf16[1200,128]{1,0:T(8,128)(2,1)S(1)}, u32[]{:S(2)}, u32[]{:S(2)}) collective-permute-start(bf16[1200,128]{1,0:T(8,128)(2,1)S(1)} %copy-done.18), channel_id=1, source_target_pairs={{0,16},{4,20},{8,24},{12,28},{16,0},{20,4},{24,8},{28,12},{1,17},{... | collective-permute-start | bytes 921608 | tf_op jit(solution)/shard_map/ppermute | solution.py:326
  133.7 9.6 %collective-permute-start.27 = (bf16[1200,128]{1,0:T(8,128)(2,1)S(1)}, bf16[1200,128]{1,0:T(8,128)(2,1)S(1)}, u32[]{:S(2)}, u32[]{:S(2)}) collective-permute-start(bf16[1200,128]{1,0:T(8,128)(2,1)S(1)} %copy-done.17), channel_id=1, source_target_pairs={{0,12},{4,8},{8,4},{12,0},{16,28},{20,24},{24,20},{28,16},{1,13},{... | collective-permute-start | bytes 921608 | tf_op jit(solution)/shard_map/ppermute | solution.py:326
  134.4 15.3 %collective-permute-start.26 = (bf16[1200,128]{1,0:T(8,128)(2,1)S(1)}, bf16[1200,128]{1,0:T(8,128)(2,1)S(1)}, u32[]{:S(2)}, u32[]{:S(2)}) collective-permute-start(bf16[1200,128]{1,0:T(8,128)(2,1)S(1)} %copy-done.16), channel_id=1, source_target_pairs={{0,8},{4,12},{8,0},{12,4},{16,24},{20,28},{24,16},{28,20},{1,9},{5... | collective-permute-start | bytes 921608 | tf_op jit(solution)/shard_map/ppermute | solution.py:326
  135.1 14.6 %collective-permute-start.25 = (bf16[1200,128]{1,0:T(8,128)(2,1)S(1)}, bf16[1200,128]{1,0:T(8,128)(2,1)S(1)}, u32[]{:S(2)}, u32[]{:S(2)}) collective-permute-start(bf16[1200,128]{1,0:T(8,128)(2,1)S(1)} %copy-done.15), channel_id=1, source_target_pairs={{0,4},{4,0},{8,12},{12,8},{16,20},{20,16},{24,28},{28,24},{1,5},{5... | collective-permute-start | bytes 921608 | tf_op jit(solution)/shard_map/ppermute | solution.py:326
  135.5 25.1 %collective-permute-start.33 = (bf16[32,5760]{1,0:T(8,128)(2,1)S(1)}, bf16[32,5760]{1,0:T(8,128)(2,1)S(1)}, u32[]{:S(2)}, u32[]{:S(2)}) collective-permute-start(bf16[32,5760]{1,0:T(8,128)(2,1)S(1)} %get-tuple-element.92), channel_id=1, source_target_pairs={{0,2},{1,3},{2,0},{3,1},{4,6},{5,7},{6,4},{7,5},{8,10},{9,11},{10,... | collective-permute-start | bytes 1105928 | tf_op jit(solution)/shard_map/ppermute | solution.py:326
  158.4 29.7 %collective-permute-start.32 = (bf16[32,5760]{1,0:T(8,128)(2,1)S(1)}, bf16[32,5760]{1,0:T(8,128)(2,1)S(1)}, u32[]{:S(2)}, u32[]{:S(2)}) collective-permute-start(bf16[32,5760]{1,0:T(8,128)(2,1)S(1)} %get-tuple-element.91), channel_id=1, source_target_pairs={{0,1},{1,0},{2,3},{3,2},{4,5},{5,4},{6,7},{7,6},{8,9},{9,8},{10,11... | collective-permute-start | bytes 1105928 | tf_op jit(solution)/shard_map/ppermute | solution.py:326
  158.5 29.6 %collective-permute-start.35 = (bf16[32,5760]{1,0:T(8,128)(2,1)S(1)}, bf16[32,5760]{1,0:T(8,128)(2,1)S(1)}, u32[]{:S(2)}, u32[]{:S(2)}) collective-permute-start(bf16[32,5760]{1,0:T(8,128)(2,1)S(1)} %get-tuple-element.95), channel_id=1, source_target_pairs={{0,3},{1,2},{2,1},{3,0},{4,7},{5,6},{6,5},{7,4},{8,11},{9,10},{10,... | collective-permute-start | bytes 1105928 | tf_op jit(solution)/shard_map/ppermute | solution.py:326
  167.1 15.7 %collective-permute-start.34 = (bf16[32,3840]{1,0:T(8,128)(2,1)S(1)}, bf16[32,3840]{1,0:T(8,128)(2,1)S(1)}, u32[]{:S(2)}, u32[]{:S(2)}) collective-permute-start(bf16[32,3840]{1,0:T(8,128)(2,1)S(1)} %get-tuple-element.94), channel_id=1, source_target_pairs={{0,1},{1,0},{2,3},{3,2},{4,5},{5,4},{6,7},{7,6},{8,9},{9,8},{10,11... | collective-permute-start | bytes 737288 | tf_op jit(solution)/shard_map/ppermute | solution.py:326
  168.2 19.9 %collective-permute-start.36 = (bf16[32,3840]{1,0:T(8,128)(2,1)S(1)}, bf16[32,3840]{1,0:T(8,128)(2,1)S(1)}, u32[]{:S(2)}, u32[]{:S(2)}) collective-permute-start(bf16[32,3840]{1,0:T(8,128)(2,1)S(1)} %get-tuple-element.96), channel_id=1, source_target_pairs={{0,3},{1,2},{2,1},{3,0},{4,7},{5,6},{6,5},{7,4},{8,11},{9,10},{10,... | collective-permute-start | bytes 737288 | tf_op jit(solution)/shard_map/ppermute | solution.py:326

commit v5 on v4

--- a/solution.py
+++ b/solution.py
@@ -432,7 +432,7 @@
             far = sorted(range(1, rows), key=lambda o: (-(o >> 1).bit_count(), -(o % 2), -o))
             pieces = list(part)
             for m, o in enumerate(far):
-                early = last
+                early = last[-1:]
                 if m >= len(far) - 3:
                     early = [*results[:1], *(totals if m == len(far) - 1 else ())]
                 pieces[o] = swap(after([pieces[o]], early)[0], "row", o)

time: 203 us -> 201 us (level)
  no operation moved by 1% of the time
where the time goes in v5:
time: 201 us; the launch traced here: 200 us
  waiting for transfers between devices  76.8 us (38%)
  Pallas kernels  76.5 us (38%)
  starting transfers between devices  40.7 us (20%)
  local copies, waits for them, and re-layouts  5.16 us (3%)
    ppermute x37, waiting for transfers between devices, swap(): lax.ppermute(array, axis, [(i, i ^ offset) for i in range(lax.axis_size(a...  76.8 us
    ppermute x37, starting transfers between devices, swap(): lax.ppermute(array, axis, [(i, i ^ offset) for i in range(lax.axis_size(a...  40.7 us
    pallas_call x2, Pallas kernels, product(): pl.pallas_call(functools.partial(product_kernel, holders, chunk_count, ow...  31 us
    pallas_call x4, Pallas kernels, symmetrize(): pl.pallas_call(functools.partial(symmetrize_kernel, places, len(parts), c...  30 us
    pallas_call x1, Pallas kernels, finish(): pl.pallas_call(functools.partial(finish_kernel, cols, owned, half, run, t...  14.3 us
    unnamed x51, local copies, waits for them, and re-layouts  4.89 us
  transfers between devices with their start and end apart: 37, of which 15 were waited for; matrix products, arithmetic and copies ran while one was open for 0% of the time, Pallas kernels for 30%

profile of v5, /device:TPU:0, one launch (start us, length us, event | category | flops | bytes accessed | tf_op | source)
XLA Modules:
  0.0 200.1 jit_solution(685531684964474480)
XLA Ops:
  0.0 0.1 pad_add_fusion.where_ref
  0.1 1.1 copy-done.3
  1.2 0.7 copy-done.4
  1.9 0.7 copy-done.5
  2.5 1.2 pack.1
  3.7 4.0 %collective-permute-start.2 = (bf16[64,3072]{1,0:T(8,128)(2,1)S(1)}, bf16[64,3072]{1,0:T(8,128)(2,1)S(1)}, u32[]{:S(2)}, u32[]{:S(2)}) collective-permute-start(bf16[64,3072]{1,0:T(8,128)(2,1)S(1)} %get-tuple-element.52), channel_id=1, source_target_pairs={{0,24},{4,28},{8,16},{12,20},{16,8},{20,12},{24,0},{28,4},{1,25},{... | collective-permute-start | bytes 1179656 | tf_op jit(solution)/shard_map/ppermute | solution.py:326
  7.7 1.6 collective-permute-start.5
  9.3 2.6 %collective-permute-start.4 = (bf16[64,3072]{1,0:T(8,128)(2,1)S(1)}, bf16[64,3072]{1,0:T(8,128)(2,1)S(1)}, u32[]{:S(2)}, u32[]{:S(2)}) collective-permute-start(bf16[64,3072]{1,0:T(8,128)(2,1)S(1)} %get-tuple-element.53), channel_id=1, source_target_pairs={{0,2},{1,3},{2,0},{3,1},{4,6},{5,7},{6,4},{7,5},{8,10},{9,11},{10,... | collective-permute-start | bytes 1179656 | tf_op jit(solution)/shard_map/ppermute | solution.py:326
  11.9 0.5 collective-permute-start
  12.4 0.5 collective-permute-start.1
  12.9 4.7 %collective-permute-done.2 = bf16[64,3072]{1,0:T(8,128)(2,1)S(1)} collective-permute-done((bf16[64,3072]{1,0:T(8,128)(2,1)S(1)}, bf16[64,3072]{1,0:T(8,128)(2,1)S(1)}, u32[]{:S(2)}, u32[]{:S(2)}) %collective-permute-start.2) | collective-permute-done | bytes 393248 | tf_op jit(solution)/shard_map/ppermute | solution.py:326
  17.7 8.9 %collective-permute-done.5 = bf16[64,3072]{1,0:T(8,128)(2,1)S(1)} collective-permute-done((bf16[64,3072]{1,0:T(8,128)(2,1)S(1)}, bf16[64,3072]{1,0:T(8,128)(2,1)S(1)}, u32[]{:S(2)}, u32[]{:S(2)}) %collective-permute-start.5) | collective-permute-done | bytes 393248 | tf_op jit(solution)/shard_map/ppermute | solution.py:326
  26.6 2.4 %collective-permute-done.4 = bf16[64,3072]{1,0:T(8,128)(2,1)S(1)} collective-permute-done((bf16[64,3072]{1,0:T(8,128)(2,1)S(1)}, bf16[64,3072]{1,0:T(8,128)(2,1)S(1)}, u32[]{:S(2)}, u32[]{:S(2)}) %collective-permute-start.4) | collective-permute-done | bytes 393248 | tf_op jit(solution)/shard_map/ppermute | solution.py:326
  28.9 0.5 collective-permute-start.9
  29.4 1.5 collective-permute-start.6
  30.9 1.5 collective-permute-start.7
  32.4 2.5 %collective-permute-start.10 = (bf16[64,3072]{1,0:T(8,128)(2,1)S(1)}, bf16[64,3072]{1,0:T(8,128)(2,1)S(1)}, u32[]{:S(2)}, u32[]{:S(2)}) collective-permute-start(bf16[64,3072]{1,0:T(8,128)(2,1)S(1)} %get-tuple-element.57), channel_id=1, source_target_pairs={{0,3},{1,2},{2,1},{3,0},{4,7},{5,6},{6,5},{7,4},{8,11},{9,10},{10,... | collective-permute-start | bytes 1179656 | tf_op jit(solution)/shard_map/ppermute | solution.py:326
  35.0 0.1 collective-permute-start.3
  35.1 6.3 %collective-permute-done.9 = bf16[64,3072]{1,0:T(8,128)(2,1)S(1)} collective-permute-done((bf16[64,3072]{1,0:T(8,128)(2,1)S(1)}, bf16[64,3072]{1,0:T(8,128)(2,1)S(1)}, u32[]{:S(2)}, u32[]{:S(2)}) %collective-permute-start.9) | collective-permute-done | bytes 393248 | tf_op jit(solution)/shard_map/ppermute | solution.py:326
  41.5 0.7 collective-permute-done.10
  42.2 0.1 collective-permute-start.11
  42.3 2.4 %collective-permute-done.6 = bf16[64,3072]{1,0:T(8,128)(2,1)S(1)} collective-permute-done((bf16[64,3072]{1,0:T(8,128)(2,1)S(1)}, bf16[64,3072]{1,0:T(8,128)(2,1)S(1)}, u32[]{:S(2)}, u32[]{:S(2)}) %collective-permute-start.6) | collective-permute-done | bytes 393248 | tf_op jit(solution)/shard_map/ppermute | solution.py:326
  44.7 0.9 collective-permute-done.7
  45.6 0.1 collective-permute-start.8
  45.7 0.6 collective-permute-start.16
  46.3 0.7 collective-permute-start.17
  47.0 1.4 collective-permute-start.18
  48.4 1.4 collective-permute-start.19
  49.8 1.2 copy-done.11
  51.0 15.6 %ladder.2 = (bf16[4,1200,128]{2,1,0:T(8,128)(2,1)}, bf16[4,1200,128]{2,1,0:T(8,128)(2,1)}) custom-call(bf16[256,3072]{1,0:T(8,128)(2,1)} %copy-done.9, bf16[256,3072]{1,0:T(8,128)(2,1)} %copy-done.11, bf16[128,3072]{1,0:T(8,128)(2,1)} %copy-done.6, bf16[128,3072]{1,0:T(8,128)(2,1)} %copy-done.14, bf16[128,3072]{1,0:T(8,128)(2,1)} %copy-done.8, ...), custom_call_target="tpu_custom_call" | custom-call | flops 7549747200 | bytes 21037056 | tf_op jit(solution)/shard_map/ladder/pallas_call | solution.py:120
  66.7 0.7 collective-permute-start.22
  67.4 0.7 collective-permute-start.21
  68.4 0.6 collective-permute-start.20
  69.0 8.5 %collective-permute-done.21 = bf16[64,3072]{1,0:T(8,128)(2,1)S(1)} collective-permute-done((bf16[64,3072]{1,0:T(8,128)(2,1)S(1)}, bf16[64,3072]{1,0:T(8,128)(2,1)S(1)}, u32[]{:S(2)}, u32[]{:S(2)}) %collective-permute-start.21) | collective-permute-done | bytes 393248 | tf_op jit(solution)/shard_map/ppermute | solution.py:326
  77.6 0.1 collective-permute-start.23
  77.8 1.6 collective-permute-start.15
  79.4 1.4 collective-permute-start.14
  80.9 0.7 collective-permute-start.13
  81.6 0.9 copy-done.12
  82.5 15.4 %ladder.3 = (bf16[1200,128]{1,0:T(8,128)(2,1)}, bf16[1200,128]{1,0:T(8,128)(2,1)}, bf16[1200,128]{1,0:T(8,128)(2,1)}, bf16[1200,128]{1,0:T(8,128)(2,1)}, bf16[12...) custom-call(bf16[384,3072]{1,0:T(8,128)(2,1)} %copy-done.10, ...), custom_call_target="tpu_custom_call" | custom-call | flops 7549747200 | bytes 21037056 | tf_op jit(solution)/shard_map/ladder/pallas_call | solution.py:120
  98.0 0.8 collective-permute-start.31
  98.8 1.4 collective-permute-start.30
  100.2 8.3 %collective-permute-done.14.refs_3_ = bf16[2,1200,128]{2,1,0:T(8,128)(2,1)S(1)} collective-permute-done((bf16[2,1200,128]{2,1,0:T(8,128)(2,1)S(1)}, bf16[2,1200,128]{2,1,0:T(8,128)(2,1)S(1)}, u32[]{:S(2)}, u32[]{:S(2)}) %collective-permute-start.14) | collective-permute-done | bytes 614432 | tf_op jit(solution)/shard_map/ppermute | solution.py:326
  108.5 6.4 %symmetrize.4 = (bf16[64,3840]{1,0:T(8,128)(2,1)S(1)}, bf16[32,3840]{1,0:T(8,128)(2,1)S(1)}) custom-call(s32[2]{0:T(128)S(1)} %pad_add_fusion.where_ref, s32[9600]{0:T(1024)S(1)} %copy-done.2, bf16[4,1200,128]{2,1,0:T(8,128)(2,1)S(1)} %copy-done, bf16[4,1200,128]{2,1,0:T(8,128)(2,1)S(1)} %collective-permute-done.12.refs_1_, ...), custom_call_target="tpu_custom_call" | custom-call | flops 342343680 | bytes 1228800 | tf_op jit(solution)/shard_map/symmetrize/pallas_call | solution.py:212
  115.0 4.9 %collective-permute-start.24 = (bf16[32,3840]{1,0:T(8,128)(2,1)S(1)}, bf16[32,3840]{1,0:T(8,128)(2,1)S(1)}, u32[]{:S(2)}, u32[]{:S(2)}) collective-permute-start(bf16[32,3840]{1,0:T(8,128)(2,1)S(1)} %get-tuple-element.77), channel_id=1, source_target_pairs={{0,2},{1,3},{2,0},{3,1},{4,6},{5,7},{6,4},{7,5},{8,10},{9,11},{10,... | collective-permute-start | bytes 737288 | tf_op jit(solution)/shard_map/ppermute | solution.py:326
  119.9 0.7 collective-permute-start.29
  120.6 8.5 %symmetrize.5 = (bf16[64,5760]{1,0:T(8,128)(2,1)S(1)}, bf16[32,5760]{1,0:T(8,128)(2,1)S(1)}) custom-call(s32[2]{0:T(128)S(1)} %pad_add_fusion.where_ref, s32[9600]{0:T(1024)S(1)} %copy-done.2, bf16[4,1200,128]{2,1,0:T(8,128)(2,1)S(1)} %copy-done, bf16[4,1200,128]{2,1,0:T(8,128)(2,1)S(1)} %collective-permute-done.12.refs_1_, ...), custom_call_target="tpu_custom_call" | custom-call | flops 513515520 | bytes 1228800 | tf_op jit(solution)/shard_map/symmetrize/pallas_call | solution.py:212
  129.1 0.8 collective-permute-start.28
  129.9 1.3 collective-permute-done.24.refs_4_
  131.1 0.3 collective-permute-start.27
  131.5 1.2 collective-permute-start.26
  132.6 0.4 collective-permute-start.25
  133.0 6.1 %collective-permute-done.28.refs_4_ = bf16[1200,128]{1,0:T(8,128)(2,1)S(1)} collective-permute-done((bf16[1200,128]{1,0:T(8,128)(2,1)S(1)}, bf16[1200,128]{1,0:T(8,128)(2,1)S(1)}, u32[]{:S(2)}, u32[]{:S(2)}) %collective-permute-start.28) | collective-permute-done | bytes 307232 | tf_op jit(solution)/shard_map/ppermute | solution.py:326
  139.1 1.6 collective-permute-done.27.refs_3_
  140.7 6.5 %collective-permute-done.26.refs_2_ = bf16[1200,128]{1,0:T(8,128)(2,1)S(1)} collective-permute-done((bf16[1200,128]{1,0:T(8,128)(2,1)S(1)}, bf16[1200,128]{1,0:T(8,128)(2,1)S(1)}, u32[]{:S(2)}, u32[]{:S(2)}) %collective-permute-start.26) | collective-permute-done | bytes 307232 | tf_op jit(solution)/shard_map/ppermute | solution.py:326
  147.2 8.7 %symmetrize.6 = (bf16[32,5760]{1,0:T(8,128)(2,1)S(1)}, bf16[32,5760]{1,0:T(8,128)(2,1)S(1)}) custom-call(s32[2]{0:T(128)S(1)} %pad_add_fusion.where_ref, s32[9600]{0:T(1024)S(1)} %copy-done.2, bf16[1200,128]{1,0:T(8,128)(2,1)S(1)} %copy-done.1, bf16[1200,128]{1,0:T(8,128)(2,1)S(1)} %collective-permute-done.25.refs_1_, ...), custom_call_target="tpu_custom_call" | custom-call | flops 419143680 | bytes 1228800 | tf_op jit(solution)/shard_map/symmetrize/pallas_call | solution.py:212
  155.9 0.1 collective-permute-start.32
  156.0 2.1 %collective-permute-start.35 = (bf16[32,5760]{1,0:T(8,128)(2,1)S(1)}, bf16[32,5760]{1,0:T(8,128)(2,1)S(1)}, u32[]{:S(2)}, u32[]{:S(2)}) collective-permute-start(bf16[32,5760]{1,0:T(8,128)(2,1)S(1)} %get-tuple-element.95), channel_id=1, source_target_pairs={{0,3},{1,2},{2,1},{3,0},{4,7},{5,6},{6,5},{7,4},{8,11},{9,10},{10,... | collective-permute-start | bytes 1105928 | tf_op jit(solution)/shard_map/ppermute | solution.py:326
  158.1 6.4 %symmetrize.7 = (bf16[32,3840]{1,0:T(8,128)(2,1)S(1)}, bf16[32,3840]{1,0:T(8,128)(2,1)S(1)}) custom-call(s32[2]{0:T(128)S(1)} %pad_add_fusion.where_ref, s32[9600]{0:T(1024)S(1)} %copy-done.2, bf16[1200,128]{1,0:T(8,128)(2,1)S(1)} %copy-done.1, bf16[1200,128]{1,0:T(8,128)(2,1)S(1)} %collective-permute-done.25.refs_1_, ...), custom_call_target="tpu_custom_call" | custom-call | flops 279429120 | bytes 1228800 | tf_op jit(solution)/shard_map/symmetrize/pallas_call | solution.py:212
  164.5 1.1 collective-permute-start.34
  165.6 1.8 collective-permute-start.36
  167.4 12.8 %collective-permute-done.34.refs_3_ = bf16[32,3840]{1,0:T(8,128)(2,1)S(1)} collective-permute-done((bf16[32,3840]{1,0:T(8,128)(2,1)S(1)}, bf16[32,3840]{1,0:T(8,128)(2,1)S(1)}, u32[]{:S(2)}, u32[]{:S(2)}) %collective-permute-start.34) | collective-permute-done | bytes 245792 | tf_op jit(solution)/shard_map/ppermute | solution.py:326
  180.2 5.3 %collective-permute-done.36.refs_7_ = bf16[32,3840]{1,0:T(8,128)(2,1)S(1)} collective-permute-done((bf16[32,3840]{1,0:T(8,128)(2,1)S(1)}, bf16[32,3840]{1,0:T(8,128)(2,1)S(1)}, u32[]{:S(2)}, u32[]{:S(2)}) %collective-permute-start.36) | collective-permute-done | bytes 245792 | tf_op jit(solution)/shard_map/ppermute | solution.py:326
  185.6 14.3 %finish.1 = bf16[128,9600]{1,0:T(8,128)(2,1)} custom-call(s32[2]{0:T(128)S(1)} %pad_add_fusion.where_ref, s32[9600]{0:T(1024)S(1)} %copy-done.2, s32[1,128]{1,0:T(1,128)S(1)} %get-tuple-element.51.slot_ref, bf16[64,3840]{1,0:T(8,128)(2,1)S(1)} %get-tuple-element.62.refs_0_, bf16[64,5760]{1,0:T(8,128)(2,1)S(1)} %get-tuple-element.64.refs_1_, ...), custom_call_target="tpu_custom_call" | custom-call | flops 1013145600 | bytes 9830400 | tf_op jit(solution)/shard_map/finish/pallas_call | solution.py:301
  (80 shorter events, 0.9 us)
Async XLA Ops:
  0.1 1.1 copy-start.3
  1.2 0.7 copy-start.4
  1.9 0.7 copy-start.5
  3.7 13.9 %collective-permute-start.2 = (bf16[64,3072]{1,0:T(8,128)(2,1)S(1)}, bf16[64,3072]{1,0:T(8,128)(2,1)S(1)}, u32[]{:S(2)}, u32[]{:S(2)}) collective-permute-start(bf16[64,3072]{1,0:T(8,128)(2,1)S(1)} %get-tuple-element.52), channel_id=1, source_target_pairs={{0,24},{4,28},{8,16},{12,20},{16,8},{20,12},{24,0},{28,4},{1,25},{... | collective-permute-start | bytes 1179656 | tf_op jit(solution)/shard_map/ppermute | solution.py:326
  7.7 18.9 %collective-permute-start.5 = (bf16[64,3072]{1,0:T(8,128)(2,1)S(1)}, bf16[64,3072]{1,0:T(8,128)(2,1)S(1)}, u32[]{:S(2)}, u32[]{:S(2)}) collective-permute-start(bf16[64,3072]{1,0:T(8,128)(2,1)S(1)} %get-tuple-element.54), channel_id=1, source_target_pairs={{0,1},{1,0},{2,3},{3,2},{4,5},{5,4},{6,7},{7,6},{8,9},{9,8},{10,11... | collective-permute-start | bytes 1179656 | tf_op jit(solution)/shard_map/ppermute | solution.py:326
  9.3 19.7 %collective-permute-start.4 = (bf16[64,3072]{1,0:T(8,128)(2,1)S(1)}, bf16[64,3072]{1,0:T(8,128)(2,1)S(1)}, u32[]{:S(2)}, u32[]{:S(2)}) collective-permute-start(bf16[64,3072]{1,0:T(8,128)(2,1)S(1)} %get-tuple-element.53), channel_id=1, source_target_pairs={{0,2},{1,3},{2,0},{3,1},{4,6},{5,7},{6,4},{7,5},{8,10},{9,11},{10,... | collective-permute-start | bytes 1179656 | tf_op jit(solution)/shard_map/ppermute | solution.py:326
  11.9 20.6 %collective-permute-start = (bf16[64,3072]{1,0:T(8,128)(2,1)S(1)}, bf16[64,3072]{1,0:T(8,128)(2,1)S(1)}, u32[]{:S(2)}, u32[]{:S(2)}) collective-permute-start(bf16[64,3072]{1,0:T(8,128)(2,1)S(1)} %get-tuple-element.52), channel_id=1, source_target_pairs={{0,8},{4,12},{8,0},{12,4},{16,24},{20,28},{24,16},{28,20},{1,9},{5... | collective-permute-start | bytes 1179656 | tf_op jit(solution)/shard_map/ppermute | solution.py:326
  12.4 22.5 %collective-permute-start.1 = (bf16[64,3072]{1,0:T(8,128)(2,1)S(1)}, bf16[64,3072]{1,0:T(8,128)(2,1)S(1)}, u32[]{:S(2)}, u32[]{:S(2)}) collective-permute-start(bf16[64,3072]{1,0:T(8,128)(2,1)S(1)} %get-tuple-element.52), channel_id=1, source_target_pairs={{0,16},{4,20},{8,24},{12,28},{16,0},{20,4},{24,8},{28,12},{1,17},{... | collective-permute-start | bytes 1179656 | tf_op jit(solution)/shard_map/ppermute | solution.py:326
  28.9 12.5 %collective-permute-start.9 = (bf16[64,3072]{1,0:T(8,128)(2,1)S(1)}, bf16[64,3072]{1,0:T(8,128)(2,1)S(1)}, u32[]{:S(2)}, u32[]{:S(2)}) collective-permute-start(bf16[64,3072]{1,0:T(8,128)(2,1)S(1)} %collective-permute-done.4), channel_id=1, source_target_pairs={{0,24},{4,28},{8,16},{12,20},{16,8},{20,12},{24,0},{28,4},{1,25},{... | collective-permute-start | bytes 1179656 | tf_op jit(solution)/shard_map/ppermute | solution.py:326
  29.4 15.2 %collective-permute-start.6 = (bf16[64,3072]{1,0:T(8,128)(2,1)S(1)}, bf16[64,3072]{1,0:T(8,128)(2,1)S(1)}, u32[]{:S(2)}, u32[]{:S(2)}) collective-permute-start(bf16[64,3072]{1,0:T(8,128)(2,1)S(1)} %collective-permute-done.4), channel_id=1, source_target_pairs={{0,8},{4,12},{8,0},{12,4},{16,24},{20,28},{24,16},{28,20},{1,9},{5... | collective-permute-start | bytes 1179656 | tf_op jit(solution)/shard_map/ppermute | solution.py:326
  30.9 14.7 %collective-permute-start.7 = (bf16[64,3072]{1,0:T(8,128)(2,1)S(1)}, bf16[64,3072]{1,0:T(8,128)(2,1)S(1)}, u32[]{:S(2)}, u32[]{:S(2)}) collective-permute-start(bf16[64,3072]{1,0:T(8,128)(2,1)S(1)} %collective-permute-done.4), channel_id=1, source_target_pairs={{0,16},{4,20},{8,24},{12,28},{16,0},{20,4},{24,8},{28,12},{1,17},{... | collective-permute-start | bytes 1179656 | tf_op jit(solution)/shard_map/ppermute | solution.py:326
  32.4 9.7 %collective-permute-start.10 = (bf16[64,3072]{1,0:T(8,128)(2,1)S(1)}, bf16[64,3072]{1,0:T(8,128)(2,1)S(1)}, u32[]{:S(2)}, u32[]{:S(2)}) collective-permute-start(bf16[64,3072]{1,0:T(8,128)(2,1)S(1)} %get-tuple-element.57), channel_id=1, source_target_pairs={{0,3},{1,2},{2,1},{3,0},{4,7},{5,6},{6,5},{7,4},{8,11},{9,10},{10,... | collective-permute-start | bytes 1179656 | tf_op jit(solution)/shard_map/ppermute | solution.py:326
  35.0 16.0 %copy-start.9 = (bf16[256,3072]{1,0:T(8,128)(2,1)}, bf16[256,3072]{1,0:T(8,128)(2,1)S(1)}, u32[]{:S(2)}) copy-start(bf16[256,3072]{1,0:T(8,128)(2,1)S(1)} %constant_dynamic-update-slice_fusion.refs_0_) | copy-start | bytes 4718596
  35.0 14.8 %collective-permute-start.3 = (bf16[256,3072]{1,0:T(8,128)(2,1)S(1)}, bf16[256,3072]{1,0:T(8,128)(2,1)S(1)}, u32[]{:S(2)}, u32[]{:S(2)}) collective-permute-start(bf16[256,3072]{1,0:T(8,128)(2,1)S(1)} %constant_dynamic-update-slice_fusion.refs_0_), channel_id=1, source_target_pairs={{0,4},{4,0},{8,12},{12,8},{16,20},{20,16},{24,28},{28,24},{1,5},{5... | collective-permute-start | bytes 4718600 | tf_op jit(solution)/shard_map/ppermute | solution.py:326
  42.2 8.8 %copy-start.8 = (bf16[128,3072]{1,0:T(8,128)(2,1)}, bf16[128,3072]{1,0:T(8,128)(2,1)S(1)}, u32[]{:S(2)}) copy-start(bf16[128,3072]{1,0:T(8,128)(2,1)S(1)} %constant_dynamic-update-slice_fusion.6.refs_4_) | copy-start | bytes 2359300
  42.2 4.8 %collective-permute-start.11 = (bf16[128,3072]{1,0:T(8,128)(2,1)S(1)}, bf16[128,3072]{1,0:T(8,128)(2,1)S(1)}, u32[]{:S(2)}, u32[]{:S(2)}) collective-permute-start(bf16[128,3072]{1,0:T(8,128)(2,1)S(1)} %constant_dynamic-update-slice_fusion.6.refs_4_), channel_id=1, source_target_pairs={{0,4},{4,0},{8,12},{12,8},{16,20},{20,16},{24,28},{28,24},{1,5},{5... | collective-permute-start | bytes 2359304 | tf_op jit(solution)/shard_map/ppermute | solution.py:326
  45.6 5.4 %copy-start.6 = (bf16[128,3072]{1,0:T(8,128)(2,1)}, bf16[128,3072]{1,0:T(8,128)(2,1)S(1)}, u32[]{:S(2)}) copy-start(bf16[128,3072]{1,0:T(8,128)(2,1)S(1)} %constant_dynamic-update-slice_fusion.4.refs_2_) | copy-start | bytes 2359300
  45.6 2.8 %collective-permute-start.8 = (bf16[128,3072]{1,0:T(8,128)(2,1)S(1)}, bf16[128,3072]{1,0:T(8,128)(2,1)S(1)}, u32[]{:S(2)}, u32[]{:S(2)}) collective-permute-start(bf16[128,3072]{1,0:T(8,128)(2,1)S(1)} %constant_dynamic-update-slice_fusion.4.refs_2_), channel_id=1, source_target_pairs={{0,4},{4,0},{8,12},{12,8},{16,20},{20,16},{24,28},{28,24},{1,5},{5... | collective-permute-start | bytes 2359304 | tf_op jit(solution)/shard_map/ppermute | solution.py:326
  45.7 21.7 %collective-permute-start.16 = (bf16[64,3072]{1,0:T(8,128)(2,1)S(1)}, bf16[64,3072]{1,0:T(8,128)(2,1)S(1)}, u32[]{:S(2)}, u32[]{:S(2)}) collective-permute-start(bf16[64,3072]{1,0:T(8,128)(2,1)S(1)} %collective-permute-done.5), channel_id=1, source_target_pairs={{0,8},{4,12},{8,0},{12,4},{16,24},{20,28},{24,16},{28,20},{1,9},{5... | collective-permute-start | bytes 1179656 | tf_op jit(solution)/shard_map/ppermute | solution.py:326
  46.3 21.1 %collective-permute-start.17 = (bf16[64,3072]{1,0:T(8,128)(2,1)S(1)}, bf16[64,3072]{1,0:T(8,128)(2,1)S(1)}, u32[]{:S(2)}, u32[]{:S(2)}) collective-permute-start(bf16[64,3072]{1,0:T(8,128)(2,1)S(1)} %collective-permute-done.5), channel_id=1, source_target_pairs={{0,16},{4,20},{8,24},{12,28},{16,0},{20,4},{24,8},{28,12},{1,17},{... | collective-permute-start | bytes 1179656 | tf_op jit(solution)/shard_map/ppermute | solution.py:326
  47.0 4.0 %copy-start.13 = (bf16[128,3072]{1,0:T(8,128)(2,1)}, bf16[128,3072]{1,0:T(8,128)(2,1)S(1)}, u32[]{:S(2)}) copy-start(bf16[128,3072]{1,0:T(8,128)(2,1)S(1)} %collective-permute-done.11.refs_5_) | copy-start | bytes 2359300
  47.0 19.6 %collective-permute-start.18 = (bf16[64,3072]{1,0:T(8,128)(2,1)S(1)}, bf16[64,3072]{1,0:T(8,128)(2,1)S(1)}, u32[]{:S(2)}, u32[]{:S(2)}) collective-permute-start(bf16[64,3072]{1,0:T(8,128)(2,1)S(1)} %collective-permute-done.10), channel_id=1, source_target_pairs={{0,8},{4,12},{8,0},{12,4},{16,24},{20,28},{24,16},{28,20},{1,9},{5... | collective-permute-start | bytes 1179656 | tf_op jit(solution)/shard_map/ppermute | solution.py:326
  48.4 2.6 %copy-start.14 = (bf16[128,3072]{1,0:T(8,128)(2,1)}, bf16[128,3072]{1,0:T(8,128)(2,1)S(1)}, u32[]{:S(2)}) copy-start(bf16[128,3072]{1,0:T(8,128)(2,1)S(1)} %collective-permute-done.8.refs_3_) | copy-start | bytes 2359300
  48.4 18.2 %collective-permute-start.19 = (bf16[64,3072]{1,0:T(8,128)(2,1)S(1)}, bf16[64,3072]{1,0:T(8,128)(2,1)S(1)}, u32[]{:S(2)}, u32[]{:S(2)}) collective-permute-start(bf16[64,3072]{1,0:T(8,128)(2,1)S(1)} %collective-permute-done.10), channel_id=1, source_target_pairs={{0,16},{4,20},{8,24},{12,28},{16,0},{20,4},{24,8},{28,12},{1,17},{... | collective-permute-start | bytes 1179656 | tf_op jit(solution)/shard_map/ppermute | solution.py:326
  49.8 1.2 copy-start.11
  66.7 2.2 %copy-start = (bf16[4,1200,128]{2,1,0:T(8,128)(2,1)S(1)}, bf16[4,1200,128]{2,1,0:T(8,128)(2,1)}, u32[]{:S(2)}) copy-start(bf16[4,1200,128]{2,1,0:T(8,128)(2,1)} %get-tuple-element.60.refs_0_) | copy-start | bytes 3686404
  66.7 10.8 %collective-permute-start.22 = (bf16[64,3072]{1,0:T(8,128)(2,1)S(1)}, bf16[64,3072]{1,0:T(8,128)(2,1)S(1)}, u32[]{:S(2)}, u32[]{:S(2)}) collective-permute-start(bf16[64,3072]{1,0:T(8,128)(2,1)S(1)} %collective-permute-done.19), channel_id=1, source_target_pairs={{0,8},{4,12},{8,0},{12,4},{16,24},{20,28},{24,16},{28,20},{1,9},{5... | collective-permute-start | bytes 1179656 | tf_op jit(solution)/shard_map/ppermute | solution.py:326
  67.4 10.1 %collective-permute-start.21 = (bf16[64,3072]{1,0:T(8,128)(2,1)S(1)}, bf16[64,3072]{1,0:T(8,128)(2,1)S(1)}, u32[]{:S(2)}, u32[]{:S(2)}) collective-permute-start(bf16[64,3072]{1,0:T(8,128)(2,1)S(1)} %collective-permute-done.16), channel_id=1, source_target_pairs={{0,16},{4,20},{8,24},{12,28},{16,0},{20,4},{24,8},{28,12},{1,17},{... | collective-permute-start | bytes 1179656 | tf_op jit(solution)/shard_map/ppermute | solution.py:326
  68.1 9.5 %collective-permute-start.12 = (bf16[4,1200,128]{2,1,0:T(8,128)(2,1)}, bf16[4,1200,128]{2,1,0:T(8,128)(2,1)S(1)}, u32[]{:S(2)}, u32[]{:S(2)}) collective-permute-start(bf16[4,1200,128]{2,1,0:T(8,128)(2,1)} %get-tuple-element.61), channel_id=1, source_target_pairs={{0,4},{4,0},{8,12},{12,8},{16,20},{20,16},{24,28},{28,24},{1,5},{5... | collective-permute-start | bytes 3686408 | tf_op jit(solution)/shard_map/ppermute | solution.py:326
  68.3 9.4 %copy-start.10 = (bf16[384,3072]{1,0:T(8,128)(2,1)}, bf16[384,3072]{1,0:T(8,128)(2,1)S(1)}, u32[]{:S(2)}) copy-start(bf16[384,3072]{1,0:T(8,128)(2,1)S(1)} %constant_dynamic-update-slice_fusion.8.refs_0_) | copy-start | bytes 7077892
  68.4 13.3 %collective-permute-start.20 = (bf16[384,3072]{1,0:T(8,128)(2,1)S(1)}, bf16[384,3072]{1,0:T(8,128)(2,1)}, u32[]{:S(2)}, u32[]{:S(2)}) collective-permute-start(bf16[384,3072]{1,0:T(8,128)(2,1)S(1)} %constant_dynamic-update-slice_fusion.8.refs_0_), channel_id=1, source_target_pairs={{0,4},{4,0},{8,12},{12,8},{16,20},{20,16},{24,28},{28,24},{1,5},{5... | collective-permute-start | bytes 7077896 | tf_op jit(solution)/shard_map/ppermute | solution.py:326
  77.6 3.3 %copy-start.7 = (bf16[128,3072]{1,0:T(8,128)(2,1)}, bf16[128,3072]{1,0:T(8,128)(2,1)S(1)}, u32[]{:S(2)}) copy-start(bf16[128,3072]{1,0:T(8,128)(2,1)S(1)} %constant_dynamic-update-slice_fusion.14.refs_2_) | copy-start | bytes 2359300
  77.6 4.1 %collective-permute-start.23 = (bf16[128,3072]{1,0:T(8,128)(2,1)S(1)}, bf16[128,3072]{1,0:T(8,128)(2,1)S(1)}, u32[]{:S(2)}, u32[]{:S(2)}) collective-permute-start(bf16[128,3072]{1,0:T(8,128)(2,1)S(1)} %constant_dynamic-update-slice_fusion.14.refs_2_), channel_id=1, source_target_pairs={{0,4},{4,0},{8,12},{12,8},{16,20},{20,16},{24,28},{28,24},{1,5},{5... | collective-permute-start | bytes 2359304 | tf_op jit(solution)/shard_map/ppermute | solution.py:326
  77.8 20.2 %collective-permute-start.15 = (bf16[2,1200,128]{2,1,0:T(8,128)(2,1)S(1)}, bf16[2,1200,128]{2,1,0:T(8,128)(2,1)S(1)}, u32[]{:S(2)}, u32[]{:S(2)}) collective-permute-start(bf16[2,1200,128]{2,1,0:T(8,128)(2,1)S(1)} %pad_maximum_fusion.2), channel_id=1, source_target_pairs={{0,24},{4,28},{8,16},{12,20},{16,8},{20,12},{24,0},{28,4},{1,25},{... | collective-permute-start | bytes 1843208 | tf_op jit(solution)/shard_map/ppermute | solution.py:326
  79.4 29.1 %collective-permute-start.14 = (bf16[2,1200,128]{2,1,0:T(8,128)(2,1)S(1)}, bf16[2,1200,128]{2,1,0:T(8,128)(2,1)S(1)}, u32[]{:S(2)}, u32[]{:S(2)}) collective-permute-start(bf16[2,1200,128]{2,1,0:T(8,128)(2,1)S(1)} %pad_maximum_fusion.1), channel_id=1, source_target_pairs={{0,16},{4,20},{8,24},{12,28},{16,0},{20,4},{24,8},{28,12},{1,17},{... | collective-permute-start | bytes 1843208 | tf_op jit(solution)/shard_map/ppermute | solution.py:326
  80.9 27.6 %copy-start.2 = (s32[9600]{0:T(1024)S(1)}, s32[9600]{0:T(1024)}, u32[]{:S(2)}) copy-start(s32[9600]{0:T(1024)} %mirror_ref.9) | copy-start | bytes 115204
  80.9 27.6 %collective-permute-start.13 = (bf16[2,1200,128]{2,1,0:T(8,128)(2,1)S(1)}, bf16[2,1200,128]{2,1,0:T(8,128)(2,1)S(1)}, u32[]{:S(2)}, u32[]{:S(2)}) collective-permute-start(bf16[2,1200,128]{2,1,0:T(8,128)(2,1)S(1)} %pad_maximum_fusion), channel_id=1, source_target_pairs={{0,8},{4,12},{8,0},{12,4},{16,24},{20,28},{24,16},{28,20},{1,9},{5... | collective-permute-start | bytes 1843208 | tf_op jit(solution)/shard_map/ppermute | solution.py:326
  81.6 0.9 copy-start.12
  98.0 21.9 %copy-start.19 = (bf16[1200,128]{1,0:T(8,128)(2,1)S(1)}, bf16[1200,128]{1,0:T(8,128)(2,1)}, u32[]{:S(2)}) copy-start(bf16[1200,128]{1,0:T(8,128)(2,1)} %get-tuple-element.86) | copy-start | bytes 921604
  98.0 33.5 %collective-permute-start.31 = (bf16[1200,128]{1,0:T(8,128)(2,1)}, bf16[1200,128]{1,0:T(8,128)(2,1)S(1)}, u32[]{:S(2)}, u32[]{:S(2)}) collective-permute-start(bf16[1200,128]{1,0:T(8,128)(2,1)} %get-tuple-element.90), channel_id=1, source_target_pairs={{0,28},{4,24},{8,20},{12,16},{16,12},{20,8},{24,4},{28,0},{1,29},{... | collective-permute-start | bytes 921608 | tf_op jit(solution)/shard_map/ppermute | solution.py:326
  98.8 33.8 %collective-permute-start.30 = (bf16[1200,128]{1,0:T(8,128)(2,1)}, bf16[1200,128]{1,0:T(8,128)(2,1)S(1)}, u32[]{:S(2)}, u32[]{:S(2)}) collective-permute-start(bf16[1200,128]{1,0:T(8,128)(2,1)} %get-tuple-element.88), channel_id=1, source_target_pairs={{0,24},{4,28},{8,16},{12,20},{16,8},{20,12},{24,0},{28,4},{1,25},{... | collective-permute-start | bytes 921608 | tf_op jit(solution)/shard_map/ppermute | solution.py:326
  115.0 14.1 %copy-start.18 = (bf16[1200,128]{1,0:T(8,128)(2,1)S(1)}, bf16[1200,128]{1,0:T(8,128)(2,1)}, u32[]{:S(2)}) copy-start(bf16[1200,128]{1,0:T(8,128)(2,1)} %get-tuple-element.84) | copy-start | bytes 921604
  115.0 16.2 %copy-start.17 = (bf16[1200,128]{1,0:T(8,128)(2,1)S(1)}, bf16[1200,128]{1,0:T(8,128)(2,1)}, u32[]{:S(2)}) copy-start(bf16[1200,128]{1,0:T(8,128)(2,1)} %get-tuple-element.82) | copy-start | bytes 921604
  115.0 16.5 %copy-start.16 = (bf16[1200,128]{1,0:T(8,128)(2,1)S(1)}, bf16[1200,128]{1,0:T(8,128)(2,1)}, u32[]{:S(2)}) copy-start(bf16[1200,128]{1,0:T(8,128)(2,1)} %get-tuple-element.80) | copy-start | bytes 921604
  115.0 17.7 %copy-start.15 = (bf16[1200,128]{1,0:T(8,128)(2,1)S(1)}, bf16[1200,128]{1,0:T(8,128)(2,1)}, u32[]{:S(2)}) copy-start(bf16[1200,128]{1,0:T(8,128)(2,1)} %get-tuple-element.78) | copy-start | bytes 921604
  115.0 32.2 %copy-start.1 = (bf16[1200,128]{1,0:T(8,128)(2,1)S(1)}, bf16[1200,128]{1,0:T(8,128)(2,1)}, u32[]{:S(2)}) copy-start(bf16[1200,128]{1,0:T(8,128)(2,1)} %get-tuple-element.75.refs_0_) | copy-start | bytes 921604
  115.0 16.1 %collective-permute-start.24 = (bf16[32,3840]{1,0:T(8,128)(2,1)S(1)}, bf16[32,3840]{1,0:T(8,128)(2,1)S(1)}, u32[]{:S(2)}, u32[]{:S(2)}) collective-permute-start(bf16[32,3840]{1,0:T(8,128)(2,1)S(1)} %get-tuple-element.77), channel_id=1, source_target_pairs={{0,2},{1,3},{2,0},{3,1},{4,6},{5,7},{6,4},{7,5},{8,10},{9,11},{10,... | collective-permute-start | bytes 737288 | tf_op jit(solution)/shard_map/ppermute | solution.py:326
  119.9 13.1 %collective-permute-start.29 = (bf16[1200,128]{1,0:T(8,128)(2,1)S(1)}, bf16[1200,128]{1,0:T(8,128)(2,1)S(1)}, u32[]{:S(2)}, u32[]{:S(2)}) collective-permute-start(bf16[1200,128]{1,0:T(8,128)(2,1)S(1)} %copy-done.19), channel_id=1, source_target_pairs={{0,20},{4,16},{8,28},{12,24},{16,4},{20,0},{24,12},{28,8},{1,21},{... | collective-permute-start | bytes 921608 | tf_op jit(solution)/shard_map/ppermute | solution.py:326
  129.1 10.1 %collective-permute-start.28 = (bf16[1200,128]{1,0:T(8,128)(2,1)S(1)}, bf16[1200,128]{1,0:T(8,128)(2,1)S(1)}, u32[]{:S(2)}, u32[]{:S(2)}) collective-permute-start(bf16[1200,128]{1,0:T(8,128)(2,1)S(1)} %copy-done.18), channel_id=1, source_target_pairs={{0,16},{4,20},{8,24},{12,28},{16,0},{20,4},{24,8},{28,12},{1,17},{... | collective-permute-start | bytes 921608 | tf_op jit(solution)/shard_map/ppermute | solution.py:326
  131.1 9.6 %collective-permute-start.27 = (bf16[1200,128]{1,0:T(8,128)(2,1)S(1)}, bf16[1200,128]{1,0:T(8,128)(2,1)S(1)}, u32[]{:S(2)}, u32[]{:S(2)}) collective-permute-start(bf16[1200,128]{1,0:T(8,128)(2,1)S(1)} %copy-done.17), channel_id=1, source_target_pairs={{0,12},{4,8},{8,4},{12,0},{16,28},{20,24},{24,20},{28,16},{1,13},{... | collective-permute-start | bytes 921608 | tf_op jit(solution)/shard_map/ppermute | solution.py:326
  131.5 15.7 %collective-permute-start.26 = (bf16[1200,128]{1,0:T(8,128)(2,1)S(1)}, bf16[1200,128]{1,0:T(8,128)(2,1)S(1)}, u32[]{:S(2)}, u32[]{:S(2)}) collective-permute-start(bf16[1200,128]{1,0:T(8,128)(2,1)S(1)} %copy-done.16), channel_id=1, source_target_pairs={{0,8},{4,12},{8,0},{12,4},{16,24},{20,28},{24,16},{28,20},{1,9},{5... | collective-permute-start | bytes 921608 | tf_op jit(solution)/shard_map/ppermute | solution.py:326
  132.6 14.6 %collective-permute-start.25 = (bf16[1200,128]{1,0:T(8,128)(2,1)S(1)}, bf16[1200,128]{1,0:T(8,128)(2,1)S(1)}, u32[]{:S(2)}, u32[]{:S(2)}) collective-permute-start(bf16[1200,128]{1,0:T(8,128)(2,1)S(1)} %copy-done.15), channel_id=1, source_target_pairs={{0,4},{4,0},{8,12},{12,8},{16,20},{20,16},{24,28},{28,24},{1,5},{5... | collective-permute-start | bytes 921608 | tf_op jit(solution)/shard_map/ppermute | solution.py:326
  133.0 25.0 %collective-permute-start.33 = (bf16[32,5760]{1,0:T(8,128)(2,1)S(1)}, bf16[32,5760]{1,0:T(8,128)(2,1)S(1)}, u32[]{:S(2)}, u32[]{:S(2)}) collective-permute-start(bf16[32,5760]{1,0:T(8,128)(2,1)S(1)} %get-tuple-element.92), channel_id=1, source_target_pairs={{0,2},{1,3},{2,0},{3,1},{4,6},{5,7},{6,4},{7,5},{8,10},{9,11},{10,... | collective-permute-start | bytes 1105928 | tf_op jit(solution)/shard_map/ppermute | solution.py:326
  155.9 29.7 %collective-permute-start.32 = (bf16[32,5760]{1,0:T(8,128)(2,1)S(1)}, bf16[32,5760]{1,0:T(8,128)(2,1)S(1)}, u32[]{:S(2)}, u32[]{:S(2)}) collective-permute-start(bf16[32,5760]{1,0:T(8,128)(2,1)S(1)} %get-tuple-element.91), channel_id=1, source_target_pairs={{0,1},{1,0},{2,3},{3,2},{4,5},{5,4},{6,7},{7,6},{8,9},{9,8},{10,11... | collective-permute-start | bytes 1105928 | tf_op jit(solution)/shard_map/ppermute | solution.py:326
  156.0 29.6 %collective-permute-start.35 = (bf16[32,5760]{1,0:T(8,128)(2,1)S(1)}, bf16[32,5760]{1,0:T(8,128)(2,1)S(1)}, u32[]{:S(2)}, u32[]{:S(2)}) collective-permute-start(bf16[32,5760]{1,0:T(8,128)(2,1)S(1)} %get-tuple-element.95), channel_id=1, source_target_pairs={{0,3},{1,2},{2,1},{3,0},{4,7},{5,6},{6,5},{7,4},{8,11},{9,10},{10,... | collective-permute-start | bytes 1105928 | tf_op jit(solution)/shard_map/ppermute | solution.py:326
  164.5 15.7 %collective-permute-start.34 = (bf16[32,3840]{1,0:T(8,128)(2,1)S(1)}, bf16[32,3840]{1,0:T(8,128)(2,1)S(1)}, u32[]{:S(2)}, u32[]{:S(2)}) collective-permute-start(bf16[32,3840]{1,0:T(8,128)(2,1)S(1)} %get-tuple-element.94), channel_id=1, source_target_pairs={{0,1},{1,0},{2,3},{3,2},{4,5},{5,4},{6,7},{7,6},{8,9},{9,8},{10,11... | collective-permute-start | bytes 737288 | tf_op jit(solution)/shard_map/ppermute | solution.py:326
  165.6 20.0 %collective-permute-start.36 = (bf16[32,3840]{1,0:T(8,128)(2,1)S(1)}, bf16[32,3840]{1,0:T(8,128)(2,1)S(1)}, u32[]{:S(2)}, u32[]{:S(2)}) collective-permute-start(bf16[32,3840]{1,0:T(8,128)(2,1)S(1)} %get-tuple-element.96), channel_id=1, source_target_pairs={{0,3},{1,2},{2,1},{3,0},{4,7},{5,6},{6,5},{7,4},{8,11},{9,10},{10,... | collective-permute-start | bytes 737288 | tf_op jit(solution)/shard_map/ppermute | solution.py:326
